TPU v7x, 1024 devices: a whole 8x8x8 slice. The times are simulated.
1024 devices in a mesh: lon: 32 (over x_lo, y, core), lat: 32 (over x_hi, z).
Axes of the slice: x: 8 (x_hi: 4, x_lo: 2; x = x_hi * 2 + x_lo), y: 8, z: 8, core: 2. Of those that a mesh axis runs over, the one named last changes fastest.
Arguments:
- adjoint_in: float32 [384, 384, 216], P('lat', 'lon'), may hold values from -6 to 6
- stored_winds: bfloat16 [4, 384, 384, 144], P(None, 'lat', 'lon'), may hold values from -0.34 to 0.34
- innovations: bfloat16 [32, 32, 256, 216], P('lat', 'lon'), may hold values from -6 to 6
- columns: int32 [32, 32, 256], P('lat', 'lon'), may hold values from 0 to 143
- kernel_ids: int32 [32, 32, 256], P('lat', 'lon'), may hold values from 0 to 63
- counts: int32 [32, 32, 32], P('lat', 'lon'), may hold values from 0 to 8, as said below
- offsets: int32 [32, 32, 32], P('lat', 'lon'), may hold values from 0 to 248, as said below
- kernel_table: float32 [64, 216], replicated, may hold values from 0.1 to 1.5
- correlation: bfloat16 [384, 384], P(None, 'lon'), may hold values from -0.3125 to 0.3125
Outputs:
- adjoint_field: float32 [384, 384, 216], P('lat', 'lon')
- flux_gradient: float32 [384, 3, 384], P('lat', None, 'lon')
Inputs may be any that keep to these rules, and one draw needn't show every extreme that they name: For each device and owner, the rows offsets to offsets + counts - 1 form that owner's run; the runs are disjoint, in owner order, and lie within the 256 rows. In every band some owner receives exactly 8 rows from every device of the band. `offsets`: start of each owner's run, as described for counts.
All inputs are finite; a program needn't handle non-finite values.
Results may differ from a plain program's by a relative error of at most 0.0029.
Values may be sent and summed in bfloat16 or wider, within the bound.
No kernel may reach another device: no remote copies, remote signals or barrier semaphores. Data moves between devices by JAX's collectives and lax.ppermute only.
A program may use at most 32 MiB of HBM per device.

v0:
```python
import jax
import jax.numpy as jnp
from jax import lax
from jax.sharding import PartitionSpec as P

CAP = 8


HORIZ_MIX = 0.18
VERT_MIX = 0.1


def padded(block, sides, width, periodic):
    for axis, dim in sides:
        count = lax.axis_size(axis)
        forward = [(i, i + 1) for i in range(count - 1)]
        if periodic:
            forward.append((count - 1, 0))
        backward = [(target, source) for source, target in forward]
        low = lax.ppermute(
            lax.slice_in_dim(block, block.shape[dim] - width, None, axis=dim), axis, forward
        )
        high = lax.ppermute(lax.slice_in_dim(block, 0, width, axis=dim), axis, backward)
        block = jnp.concatenate([low, block, high], axis=dim)
    return block


def advance(center, east, west, north, south, east_wind, north_wind):
    levels = east_wind.shape[-1]
    shaped = center.shape[:-1] + (center.shape[-1] // levels, levels)
    middle = center.reshape(shaped)
    east_v = east.reshape(shaped)
    west_v = west.reshape(shaped)
    north_v = north.reshape(shaped)
    south_v = south.reshape(shaped)
    upper = jnp.concatenate([middle[..., 1:], middle[..., -1:]], axis=-1)
    lower = jnp.concatenate([middle[..., :1], middle[..., :-1]], axis=-1)
    east_c = east_wind[..., None, :]
    north_c = north_wind[..., None, :]
    result = (
        middle
        + east_c * (east_v - west_v) * 0.5
        + north_c * (north_v - south_v) * 0.5
        + HORIZ_MIX * (east_v + west_v + north_v + south_v - 4.0 * middle)
        + VERT_MIX * (upper + lower - 2.0 * middle)
    )
    return result.reshape(center.shape)


def single_step(field, winds_now):
    levels = winds_now.shape[-1] // 2
    cycle = padded(field, (("lon", 1),), 1, True)
    band = padded(field, (("lat", 0),), 1, False)
    return advance(
        field,
        cycle[:, 2:],
        cycle[:, :-2],
        band[2:],
        band[:-2],
        winds_now[..., :levels],
        winds_now[..., levels:],
    )


def per_device(
    adjoint_in,
    stored_winds,
    innovations,
    columns,
    kernel_ids,
    counts,
    offsets,
    kernel_table,
    correlation,
):
    lat_rows, lon_cols, width = adjoint_in.shape
    levels = stored_winds.shape[-1] // 2
    species = width // levels
    cells = lat_rows * lon_cols
    nkernel = kernel_table.shape[0]
    held_rows = innovations.shape[2]
    count_row = counts[0, 0]
    offset_row = offsets[0, 0]
    slot_ids = jnp.arange(CAP, dtype=jnp.int32)
    row_index = jnp.minimum(offset_row[:, None] + slot_ids[None, :], held_rows - 1)
    valid = slot_ids[None, :] < count_row[:, None]
    sent_rows = innovations[0, 0][row_index]
    codes = jnp.where(valid, kernel_ids[0, 0][row_index] * cells + columns[0, 0][row_index], -1)
    row_values = lax.all_to_all(sent_rows, "lon", split_axis=0, concat_axis=0, tiled=True)
    row_codes = lax.all_to_all(codes, "lon", split_axis=0, concat_axis=0, tiled=True)
    kernel_row = row_codes // cells
    onehot = (kernel_row[..., None] == jnp.arange(nkernel, dtype=jnp.int32)).astype(jnp.float32)
    table_rows = jnp.einsum("nkc,cf->nkf", onehot, kernel_table, precision=lax.Precision.HIGHEST)
    target = jnp.where(row_codes >= 0, row_codes % cells, cells).astype(jnp.int32)
    weighted, target = (row_values.astype(jnp.float32) * table_rows, target)
    forcing = (
        jnp.zeros((cells, width), jnp.float32)
        .at[target.reshape(-1)]
        .add(weighted.reshape(-1, width), mode="drop")
        .reshape(lat_rows, lon_cols, width)
    )
    field = adjoint_in + forcing
    surface = jnp.zeros((lat_rows, lon_cols, species), jnp.float32)
    steps_total = stored_winds.shape[0]
    for step_index in range(steps_total):
        winds_now = stored_winds[steps_total - 1 - step_index].astype(jnp.float32)
        field = single_step(field, winds_now)
        surface = surface + field[..., ::levels]
    surface_bf = jnp.transpose(surface.astype(jnp.bfloat16), (0, 2, 1)).reshape(
        lat_rows * species, lon_cols
    )
    gradient = jnp.dot(
        lax.all_gather(surface_bf, "lon", axis=1, tiled=True),
        correlation,
        preferred_element_type=jnp.float32,
    )
    return (field, gradient.reshape(lat_rows, species, lon_cols))


def solution(mesh):
    return jax.shard_map(
        per_device,
        mesh=mesh,
        in_specs=(
            P("lat", "lon", None),
            P(None, "lat", "lon", None),
            P("lat", "lon", None, None),
            P("lat", "lon", None),
            P("lat", "lon", None),
            P("lat", "lon", None),
            P("lat", "lon", None),
            P(),
            P(None, "lon"),
        ),
        out_specs=(P("lat", "lon", None), P("lat", None, "lon")),
        check_vma=False,
    )
```

profile of v0, /device:TPU:9, one launch (start us, length us, event | category | flops | bytes accessed | tf_op | source)
XLA Modules:
  0.0 182.7 jit_solution(17700103971196972840)
XLA Ops:
  0.7 0.7 copy-done.31
  1.5 0.7 copy-done.1
  2.2 1.9 %gather_fusion = s32[256]{0:T(256)S(1)} fusion(s32[256]{0:T(256)S(1)} %bitcast.64, s32[1024]{0:T(1024)S(1)} %pad_clamp_fusion), kind=kCustom, calls=%fused_computation | custom fusion | bytes 3072 | tf_op jit(solution)/shard_map/gather | solution.py:88
  4.2 0.7 copy-done.2
  4.8 1.9 %gather_fusion.1 = s32[256]{0:T(256)S(1)} fusion(s32[256]{0:T(256)S(1)} %bitcast.65, s32[1024]{0:T(1024)S(1)} %pad_clamp_fusion), kind=kCustom, calls=%fused_computation.1 | custom fusion | bytes 3072 | tf_op jit(solution)/shard_map/gather | solution.py:88
  6.9 0.7 copy-done.30
  7.5 0.7 fusion.40
  8.2 8.4 %all-to-all-start = ((s32[32,1,8]{2,1,0:T(1,128)}), s32[32,1,8]{2,1,0:T(1,128)S(1)}, u32[]{:S(2)}, u32[]{:S(2)}) async-start(s32[32,1,8]{2,1,0:T(1,128)} %bitcast.4), calls=%async_computation | async-start | bytes 32768 | tf_op jit(solution)/shard_map/all_to_all | solution.py:90
  16.6 0.4 fusion.45
  17.6 0.8 copy-done.22
  18.5 1.8 gather_fusion.2
  20.4 0.8 mul.301
  21.3 0.8 mul.305
  22.2 0.8 mul.313
  23.1 0.9 mul.317
  24.0 0.8 mul.333
  24.9 0.8 mul.337
  25.8 0.9 mul.353
  26.7 0.8 mul.357
  27.5 8.3 %all-to-all-start.1 = ((bf16[32,8,216]{2,1,0:T(8,128)(2,1)}), bf16[32,8,216]{2,1,0:T(8,128)(2,1)S(1)}, u32[]{:S(2)}, u32[]{:S(2)}) async-start(bf16[32,8,216]{2,1,0:T(8,128)(2,1)} %bitcast.7), calls=%async_computation.1 | async-start | bytes 262144 | tf_op jit(solution)/shard_map/all_to_all | solution.py:89
  36.4 8.3 %all-to-all-done.1 = bf16[32,8,216]{2,1,0:T(8,128)(2,1)S(1)} async-done(((bf16[32,8,216]{2,1,0:T(8,128)(2,1)}), bf16[32,8,216]{2,1,0:T(8,128)(2,1)S(1)}, u32[]{:S(2)}, u32[]{:S(2)}) %all-to-all-start.1) | async-done | bytes 110624 | tf_op jit(solution)/shard_map/all_to_all | solution.py:89
  44.8 0.3 fusion
  45.1 2.0 %scatter_custom_fusion = f32[144,216]{1,0:T(8,128)S(1)} fusion(s32[256]{0:T(256)S(1)} %bitcast.68, f32[256,216]{1,0:T(8,128)S(1)} %fusion, f32[]{:T(128)} %constant.12.clone.1), kind=kCustom, calls=%fused_computation.76 | custom fusion | flops 55296 | bytes 124420 | tf_op jit(solution)/shard_map/scatter-add | solution.py:99
  47.1 0.9 copy-done.21
  48.2 17.9 %collective-permute-start.2 = (f32[1,12,216]{2,1,0:T(8,128)S(1)}, f32[1,12,216]{2,1,0:T(8,128)S(1)}, u32[]{:S(2)}, u32[]{:S(2)}) collective-permute-start(f32[1,12,216]{2,1,0:T(8,128)S(1)} %get-tuple-element.61), channel_id=1, source_target_pairs={{1,0},{2,1},{3,2},{4,3},{5,4},{6,5},{7,6},{8,7},{9,8},{10,9},{11,1... | collective-permute-start | bytes 31112 | tf_op jit(solution)/shard_map/ppermute | solution.py:23
  66.1 1.9 %collective-permute-start.3 = (f32[1,12,216]{2,1,0:T(8,128)S(1)}, f32[1,12,216]{2,1,0:T(8,128)S(1)}, u32[]{:S(2)}, u32[]{:S(2)}) collective-permute-start(f32[1,12,216]{2,1,0:T(8,128)S(1)} %get-tuple-element.62), channel_id=1, source_target_pairs={{0,1},{1,2},{2,3},{3,4},{4,5},{5,6},{6,7},{7,8},{8,9},{9,10},{10,1... | collective-permute-start | bytes 31112 | tf_op jit(solution)/shard_map/ppermute | solution.py:20
  68.0 2.7 %collective-permute-start = (f32[12,1,216]{2,1,0:T(1,128)S(1)}, f32[12,1,216]{2,1,0:T(1,128)S(1)}, u32[]{:S(2)}, u32[]{:S(2)}) collective-permute-start(f32[12,1,216]{2,1,0:T(1,128)S(1)} %get-tuple-element.65), channel_id=1, source_target_pairs={{32,0},{64,32},{96,64},{128,96},{160,128},{192,160},{224,192},{256... | collective-permute-start | bytes 31112 | tf_op jit(solution)/shard_map/ppermute | solution.py:23
  70.7 2.9 %collective-permute-start.1 = (f32[12,1,216]{2,1,0:T(1,128)S(1)}, f32[12,1,216]{2,1,0:T(1,128)S(1)}, u32[]{:S(2)}, u32[]{:S(2)}) collective-permute-start(f32[12,1,216]{2,1,0:T(1,128)S(1)} %get-tuple-element.64), channel_id=1, source_target_pairs={{0,32},{32,64},{64,96},{96,128},{128,160},{160,192},{192,224},{224... | collective-permute-start | bytes 31112 | tf_op jit(solution)/shard_map/ppermute | solution.py:20
  73.6 0.2 fusion.55
  73.8 0.2 fusion.54
  74.2 0.7 collective-permute-done.3
  75.1 0.5 copy-done.27
  76.2 0.3 fusion.21
  77.1 0.7 copy-done.16
  77.9 0.2 multiply_add_fusion.3
  78.1 5.9 %collective-permute-start.4 = (f32[12,1,216]{2,1,0:T(1,128)S(1)}, f32[12,1,216]{2,1,0:T(1,128)S(1)}, u32[]{:S(2)}, u32[]{:S(2)}) collective-permute-start(f32[12,1,216]{2,1,0:T(1,128)S(1)} %get-tuple-element.57), channel_id=1, source_target_pairs={{32,0},{64,32},{96,64},{128,96},{160,128},{192,160},{224,192},{256... | collective-permute-start | bytes 31112 | tf_op jit(solution)/shard_map/ppermute | solution.py:23
  84.0 1.9 %collective-permute-start.5 = (f32[12,1,216]{2,1,0:T(1,128)S(1)}, f32[12,1,216]{2,1,0:T(1,128)S(1)}, u32[]{:S(2)}, u32[]{:S(2)}) collective-permute-start(f32[12,1,216]{2,1,0:T(1,128)S(1)} %get-tuple-element.56), channel_id=1, source_target_pairs={{0,32},{32,64},{64,96},{96,128},{128,160},{160,192},{192,224},{224... | collective-permute-start | bytes 31112 | tf_op jit(solution)/shard_map/ppermute | solution.py:20
  86.0 7.6 %collective-permute-start.6 = (f32[1,12,216]{2,1,0:T(8,128)S(1)}, f32[1,12,216]{2,1,0:T(8,128)S(1)}, u32[]{:S(2)}, u32[]{:S(2)}) collective-permute-start(f32[1,12,216]{2,1,0:T(8,128)S(1)} %slice.296), channel_id=1, source_target_pairs={{1,0},{2,1},{3,2},{4,3},{5,4},{6,5},{7,6},{8,7},{9,8},{10,9},{11,1... | collective-permute-start | bytes 31112 | tf_op jit(solution)/shard_map/ppermute | solution.py:23
  93.7 1.9 %collective-permute-start.7 = (f32[1,12,216]{2,1,0:T(8,128)S(1)}, f32[1,12,216]{2,1,0:T(8,128)S(1)}, u32[]{:S(2)}, u32[]{:S(2)}) collective-permute-start(f32[1,12,216]{2,1,0:T(8,128)S(1)} %slice.297), channel_id=1, source_target_pairs={{0,1},{1,2},{2,3},{3,4},{4,5},{5,6},{6,7},{7,8},{8,9},{9,10},{10,1... | collective-permute-start | bytes 31112 | tf_op jit(solution)/shard_map/ppermute | solution.py:20
  95.8 0.8 slice.292
  96.6 5.8 %collective-permute-done.7 = f32[1,12,216]{2,1,0:T(8,128)S(1)} collective-permute-done((f32[1,12,216]{2,1,0:T(8,128)S(1)}, f32[1,12,216]{2,1,0:T(8,128)S(1)}, u32[]{:S(2)}, u32[]{:S(2)}) %collective-permute-start.7) | collective-permute-done | bytes 10400 | tf_op jit(solution)/shard_map/ppermute | solution.py:20
  103.2 0.7 copy-done.7
  104.0 0.3 fusion.13
  104.8 0.7 copy-done.14
  105.8 3.8 %collective-permute-start.8 = (f32[12,1,216]{2,1,0:T(1,128)S(1)}, f32[12,1,216]{2,1,0:T(1,128)S(1)}, u32[]{:S(2)}, u32[]{:S(2)}) collective-permute-start(f32[12,1,216]{2,1,0:T(1,128)S(1)} %get-tuple-element.51), channel_id=1, source_target_pairs={{32,0},{64,32},{96,64},{128,96},{160,128},{192,160},{224,192},{256... | collective-permute-start | bytes 31112 | tf_op jit(solution)/shard_map/ppermute | solution.py:23
  109.7 1.9 %collective-permute-start.9 = (f32[12,1,216]{2,1,0:T(1,128)S(1)}, f32[12,1,216]{2,1,0:T(1,128)S(1)}, u32[]{:S(2)}, u32[]{:S(2)}) collective-permute-start(f32[12,1,216]{2,1,0:T(1,128)S(1)} %get-tuple-element.50), channel_id=1, source_target_pairs={{0,32},{32,64},{64,96},{96,128},{128,160},{160,192},{192,224},{224... | collective-permute-start | bytes 31112 | tf_op jit(solution)/shard_map/ppermute | solution.py:20
  111.7 2.0 %collective-permute-start.10 = (f32[1,12,216]{2,1,0:T(8,128)S(1)}, f32[1,12,216]{2,1,0:T(8,128)S(1)}, u32[]{:S(2)}, u32[]{:S(2)}) collective-permute-start(f32[1,12,216]{2,1,0:T(8,128)S(1)} %slice.298), channel_id=1, source_target_pairs={{1,0},{2,1},{3,2},{4,3},{5,4},{6,5},{7,6},{8,7},{9,8},{10,9},{11,1... | collective-permute-start | bytes 31112 | tf_op jit(solution)/shard_map/ppermute | solution.py:23
  113.8 3.4 %collective-permute-start.11 = (f32[1,12,216]{2,1,0:T(8,128)S(1)}, f32[1,12,216]{2,1,0:T(8,128)S(1)}, u32[]{:S(2)}, u32[]{:S(2)}) collective-permute-start(f32[1,12,216]{2,1,0:T(8,128)S(1)} %slice.299), channel_id=1, source_target_pairs={{0,1},{1,2},{2,3},{3,4},{4,5},{5,6},{6,7},{7,8},{8,9},{9,10},{10,1... | collective-permute-start | bytes 31112 | tf_op jit(solution)/shard_map/ppermute | solution.py:20
  117.4 0.8 slice.293
  118.2 4.3 %collective-permute-done.11 = f32[1,12,216]{2,1,0:T(8,128)S(1)} collective-permute-done((f32[1,12,216]{2,1,0:T(8,128)S(1)}, f32[1,12,216]{2,1,0:T(8,128)S(1)}, u32[]{:S(2)}, u32[]{:S(2)}) %collective-permute-start.11) | collective-permute-done | bytes 10400 | tf_op jit(solution)/shard_map/ppermute | solution.py:20
  123.3 0.7 copy-done.5
  124.0 0.3 fusion.5
  125.0 0.7 copy-done.12
  126.0 5.5 %collective-permute-start.12 = (f32[12,1,216]{2,1,0:T(1,128)S(1)}, f32[12,1,216]{2,1,0:T(1,128)S(1)}, u32[]{:S(2)}, u32[]{:S(2)}) collective-permute-start(f32[12,1,216]{2,1,0:T(1,128)S(1)} %get-tuple-element.43), channel_id=1, source_target_pairs={{32,0},{64,32},{96,64},{128,96},{160,128},{192,160},{224,192},{256... | collective-permute-start | bytes 31112 | tf_op jit(solution)/shard_map/ppermute | solution.py:23
  131.5 1.9 %collective-permute-start.13 = (f32[12,1,216]{2,1,0:T(1,128)S(1)}, f32[12,1,216]{2,1,0:T(1,128)S(1)}, u32[]{:S(2)}, u32[]{:S(2)}) collective-permute-start(f32[12,1,216]{2,1,0:T(1,128)S(1)} %get-tuple-element.42), channel_id=1, source_target_pairs={{0,32},{32,64},{64,96},{96,128},{128,160},{160,192},{192,224},{224... | collective-permute-start | bytes 31112 | tf_op jit(solution)/shard_map/ppermute | solution.py:20
  133.5 1.9 %collective-permute-start.14 = (f32[1,12,216]{2,1,0:T(8,128)S(1)}, f32[1,12,216]{2,1,0:T(8,128)S(1)}, u32[]{:S(2)}, u32[]{:S(2)}) collective-permute-start(f32[1,12,216]{2,1,0:T(8,128)S(1)} %slice.300), channel_id=1, source_target_pairs={{1,0},{2,1},{3,2},{4,3},{5,4},{6,5},{7,6},{8,7},{9,8},{10,9},{11,1... | collective-permute-start | bytes 31112 | tf_op jit(solution)/shard_map/ppermute | solution.py:23
  135.5 3.4 %collective-permute-start.15 = (f32[1,12,216]{2,1,0:T(8,128)S(1)}, f32[1,12,216]{2,1,0:T(8,128)S(1)}, u32[]{:S(2)}, u32[]{:S(2)}) collective-permute-start(f32[1,12,216]{2,1,0:T(8,128)S(1)} %slice.301), channel_id=1, source_target_pairs={{0,1},{1,2},{2,3},{3,4},{4,5},{5,6},{6,7},{7,8},{8,9},{9,10},{10,1... | collective-permute-start | bytes 31112 | tf_op jit(solution)/shard_map/ppermute | solution.py:20
  138.9 0.2 maximum_add_fusion.3
  139.6 4.6 %collective-permute-done.15 = f32[1,12,216]{2,1,0:T(8,128)S(1)} collective-permute-done((f32[1,12,216]{2,1,0:T(8,128)S(1)}, f32[1,12,216]{2,1,0:T(8,128)S(1)}, u32[]{:S(2)}, u32[]{:S(2)}) %collective-permute-start.15) | collective-permute-done | bytes 10400 | tf_op jit(solution)/shard_map/ppermute | solution.py:20
  144.2 0.2 multiply_add_fusion
  144.6 0.8 copy-done.19
  145.8 35.4 %all-gather = bf16[32,12,36]{2,1,0:T(8,128)(2,1)S(1)} all-gather(bf16[1,12,36]{2,1,0:T(8,128)(2,1)S(1)} %copy.217), channel_id=1, replica_groups=mesh['lon'=32,'lat'=32] {'lon'}, dimensions={0}, use_global_device_ids=true | all-gather | bytes 28512 | tf_op jit(solution)/shard_map/all_gather | solution.py:113
  181.2 0.7 copy-done.29
  182.1 0.6 reshape.319
  (159 shorter events, 8.6 us)
Async XLA Ops:
  0.6 44.1 %copy-start = (f32[64,216]{1,0:T(8,128)S(1)}, f32[64,216]{1,0:T(8,128)}, u32[]{:S(2)}) copy-start(f32[64,216]{1,0:T(8,128)} %param.16) | copy-start | bytes 165892
  0.6 0.7 copy-start.31
  1.5 0.7 copy-start.1
  4.1 0.7 copy-start.2
  4.8 11.8 %copy-start.3 = (bf16[4,12,12,144]{3,0,2,1:T(4,128)(2,1)S(1)}, bf16[4,12,12,144]{3,0,2,1:T(4,128)(2,1)}, u32[]{:S(2)}) copy-start(bf16[4,12,12,144]{3,0,2,1:T(4,128)(2,1)} %param.10) | copy-start | bytes 497668
  6.9 0.7 copy-start.30
  8.2 19.3 %all-to-all-start = ((s32[32,1,8]{2,1,0:T(1,128)}), s32[32,1,8]{2,1,0:T(1,128)S(1)}, u32[]{:S(2)}, u32[]{:S(2)}) async-start(s32[32,1,8]{2,1,0:T(1,128)} %bitcast.4), calls=%async_computation | async-start | bytes 32768 | tf_op jit(solution)/shard_map/all_to_all | solution.py:90
  17.3 4.8 %copy-start.6 = (f32[12,12,72]{2,1,0:T(8,128)}, f32[12,12,72]{2,1,0:T(8,128)S(1)}, u32[]{:S(2)}) copy-start(f32[12,12,72]{2,1,0:T(8,128)S(1)} %get-tuple-element.52) | copy-start | bytes 124420
  17.3 5.7 %copy-start.8 = (f32[12,12,72]{2,1,0:T(8,128)}, f32[12,12,72]{2,1,0:T(8,128)S(1)}, u32[]{:S(2)}) copy-start(f32[12,12,72]{2,1,0:T(8,128)S(1)} %get-tuple-element.53) | copy-start | bytes 124420
  17.5 7.4 %copy-start.4 = (f32[12,12,72]{2,1,0:T(8,128)}, f32[12,12,72]{2,1,0:T(8,128)S(1)}, u32[]{:S(2)}) copy-start(f32[12,12,72]{2,1,0:T(8,128)S(1)} %get-tuple-element.47) | copy-start | bytes 124420
  17.5 0.9 copy-start.22
  27.5 17.2 %all-to-all-start.1 = ((bf16[32,8,216]{2,1,0:T(8,128)(2,1)}), bf16[32,8,216]{2,1,0:T(8,128)(2,1)S(1)}, u32[]{:S(2)}, u32[]{:S(2)}) async-start(bf16[32,8,216]{2,1,0:T(8,128)(2,1)} %bitcast.7), calls=%async_computation.1 | async-start | bytes 262144 | tf_op jit(solution)/shard_map/all_to_all | solution.py:89
  47.0 0.9 copy-start.21
  48.2 26.0 %collective-permute-start.2 = (f32[1,12,216]{2,1,0:T(8,128)S(1)}, f32[1,12,216]{2,1,0:T(8,128)S(1)}, u32[]{:S(2)}, u32[]{:S(2)}) collective-permute-start(f32[1,12,216]{2,1,0:T(8,128)S(1)} %get-tuple-element.61), channel_id=1, source_target_pairs={{1,0},{2,1},{3,2},{4,3},{5,4},{6,5},{7,6},{8,7},{9,8},{10,9},{11,1... | collective-permute-start | bytes 31112 | tf_op jit(solution)/shard_map/ppermute | solution.py:23
  66.1 8.8 %collective-permute-start.3 = (f32[1,12,216]{2,1,0:T(8,128)S(1)}, f32[1,12,216]{2,1,0:T(8,128)S(1)}, u32[]{:S(2)}, u32[]{:S(2)}) collective-permute-start(f32[1,12,216]{2,1,0:T(8,128)S(1)} %get-tuple-element.62), channel_id=1, source_target_pairs={{0,1},{1,2},{2,3},{3,4},{4,5},{5,6},{6,7},{7,8},{8,9},{9,10},{10,1... | collective-permute-start | bytes 31112 | tf_op jit(solution)/shard_map/ppermute | solution.py:20
  68.0 6.9 %collective-permute-start = (f32[12,1,216]{2,1,0:T(1,128)S(1)}, f32[12,1,216]{2,1,0:T(1,128)S(1)}, u32[]{:S(2)}, u32[]{:S(2)}) collective-permute-start(f32[12,1,216]{2,1,0:T(1,128)S(1)} %get-tuple-element.65), channel_id=1, source_target_pairs={{32,0},{64,32},{96,64},{128,96},{160,128},{192,160},{224,192},{256... | collective-permute-start | bytes 31112 | tf_op jit(solution)/shard_map/ppermute | solution.py:23
  70.7 4.2 %collective-permute-start.1 = (f32[12,1,216]{2,1,0:T(1,128)S(1)}, f32[12,1,216]{2,1,0:T(1,128)S(1)}, u32[]{:S(2)}, u32[]{:S(2)}) collective-permute-start(f32[12,1,216]{2,1,0:T(1,128)S(1)} %get-tuple-element.64), channel_id=1, source_target_pairs={{0,32},{32,64},{64,96},{96,128},{128,160},{160,192},{192,224},{224... | collective-permute-start | bytes 31112 | tf_op jit(solution)/shard_map/ppermute | solution.py:20
  74.9 0.6 copy-start.27
  76.9 0.9 copy-start.16
  76.9 1.0 copy-start.17
  76.9 1.0 copy-start.28
  78.1 18.4 %collective-permute-start.4 = (f32[12,1,216]{2,1,0:T(1,128)S(1)}, f32[12,1,216]{2,1,0:T(1,128)S(1)}, u32[]{:S(2)}, u32[]{:S(2)}) collective-permute-start(f32[12,1,216]{2,1,0:T(1,128)S(1)} %get-tuple-element.57), channel_id=1, source_target_pairs={{32,0},{64,32},{96,64},{128,96},{160,128},{192,160},{224,192},{256... | collective-permute-start | bytes 31112 | tf_op jit(solution)/shard_map/ppermute | solution.py:23
  84.0 12.5 %collective-permute-start.5 = (f32[12,1,216]{2,1,0:T(1,128)S(1)}, f32[12,1,216]{2,1,0:T(1,128)S(1)}, u32[]{:S(2)}, u32[]{:S(2)}) collective-permute-start(f32[12,1,216]{2,1,0:T(1,128)S(1)} %get-tuple-element.56), channel_id=1, source_target_pairs={{0,32},{32,64},{64,96},{96,128},{128,160},{160,192},{192,224},{224... | collective-permute-start | bytes 31112 | tf_op jit(solution)/shard_map/ppermute | solution.py:20
  86.0 10.5 %collective-permute-start.6 = (f32[1,12,216]{2,1,0:T(8,128)S(1)}, f32[1,12,216]{2,1,0:T(8,128)S(1)}, u32[]{:S(2)}, u32[]{:S(2)}) collective-permute-start(f32[1,12,216]{2,1,0:T(8,128)S(1)} %slice.296), channel_id=1, source_target_pairs={{1,0},{2,1},{3,2},{4,3},{5,4},{6,5},{7,6},{8,7},{9,8},{10,9},{11,1... | collective-permute-start | bytes 31112 | tf_op jit(solution)/shard_map/ppermute | solution.py:23
  93.7 8.7 %collective-permute-start.7 = (f32[1,12,216]{2,1,0:T(8,128)S(1)}, f32[1,12,216]{2,1,0:T(8,128)S(1)}, u32[]{:S(2)}, u32[]{:S(2)}) collective-permute-start(f32[1,12,216]{2,1,0:T(8,128)S(1)} %slice.297), channel_id=1, source_target_pairs={{0,1},{1,2},{2,3},{3,4},{4,5},{5,6},{6,7},{7,8},{8,9},{9,10},{10,1... | collective-permute-start | bytes 31112 | tf_op jit(solution)/shard_map/ppermute | solution.py:20
  96.5 6.0 %copy-start.25 = (f32[12,1,216]{2,1,0:T(1,128)}, f32[12,1,216]{2,1,0:T(1,128)S(1)}, u32[]{:S(2)}) copy-start(f32[12,1,216]{2,1,0:T(1,128)S(1)} %collective-permute-done.5) | copy-start | bytes 31108
  103.0 0.9 copy-start.7
  103.0 0.9 copy-start.9
  104.6 0.9 copy-start.14
  104.6 1.0 copy-start.15
  104.6 1.0 copy-start.26
  105.8 12.3 %collective-permute-start.8 = (f32[12,1,216]{2,1,0:T(1,128)S(1)}, f32[12,1,216]{2,1,0:T(1,128)S(1)}, u32[]{:S(2)}, u32[]{:S(2)}) collective-permute-start(f32[12,1,216]{2,1,0:T(1,128)S(1)} %get-tuple-element.51), channel_id=1, source_target_pairs={{32,0},{64,32},{96,64},{128,96},{160,128},{192,160},{224,192},{256... | collective-permute-start | bytes 31112 | tf_op jit(solution)/shard_map/ppermute | solution.py:23
  109.7 8.5 %collective-permute-start.9 = (f32[12,1,216]{2,1,0:T(1,128)S(1)}, f32[12,1,216]{2,1,0:T(1,128)S(1)}, u32[]{:S(2)}, u32[]{:S(2)}) collective-permute-start(f32[12,1,216]{2,1,0:T(1,128)S(1)} %get-tuple-element.50), channel_id=1, source_target_pairs={{0,32},{32,64},{64,96},{96,128},{128,160},{160,192},{192,224},{224... | collective-permute-start | bytes 31112 | tf_op jit(solution)/shard_map/ppermute | solution.py:20
  111.7 6.5 %collective-permute-start.10 = (f32[1,12,216]{2,1,0:T(8,128)S(1)}, f32[1,12,216]{2,1,0:T(8,128)S(1)}, u32[]{:S(2)}, u32[]{:S(2)}) collective-permute-start(f32[1,12,216]{2,1,0:T(8,128)S(1)} %slice.298), channel_id=1, source_target_pairs={{1,0},{2,1},{3,2},{4,3},{5,4},{6,5},{7,6},{8,7},{9,8},{10,9},{11,1... | collective-permute-start | bytes 31112 | tf_op jit(solution)/shard_map/ppermute | solution.py:23
  113.8 8.7 %collective-permute-start.11 = (f32[1,12,216]{2,1,0:T(8,128)S(1)}, f32[1,12,216]{2,1,0:T(8,128)S(1)}, u32[]{:S(2)}, u32[]{:S(2)}) collective-permute-start(f32[1,12,216]{2,1,0:T(8,128)S(1)} %slice.299), channel_id=1, source_target_pairs={{0,1},{1,2},{2,3},{3,4},{4,5},{5,6},{6,7},{7,8},{8,9},{9,10},{10,1... | collective-permute-start | bytes 31112 | tf_op jit(solution)/shard_map/ppermute | solution.py:20
  118.2 4.4 %copy-start.23 = (f32[12,1,216]{2,1,0:T(1,128)}, f32[12,1,216]{2,1,0:T(1,128)S(1)}, u32[]{:S(2)}) copy-start(f32[12,1,216]{2,1,0:T(1,128)S(1)} %collective-permute-done.9) | copy-start | bytes 31108
  123.1 0.9 copy-start.5
  124.8 0.9 copy-start.12
  124.8 1.0 copy-start.13
  124.8 1.0 copy-start.24
  126.0 13.5 %collective-permute-start.12 = (f32[12,1,216]{2,1,0:T(1,128)S(1)}, f32[12,1,216]{2,1,0:T(1,128)S(1)}, u32[]{:S(2)}, u32[]{:S(2)}) collective-permute-start(f32[12,1,216]{2,1,0:T(1,128)S(1)} %get-tuple-element.43), channel_id=1, source_target_pairs={{32,0},{64,32},{96,64},{128,96},{160,128},{192,160},{224,192},{256... | collective-permute-start | bytes 31112 | tf_op jit(solution)/shard_map/ppermute | solution.py:23
  131.5 8.1 %collective-permute-start.13 = (f32[12,1,216]{2,1,0:T(1,128)S(1)}, f32[12,1,216]{2,1,0:T(1,128)S(1)}, u32[]{:S(2)}, u32[]{:S(2)}) collective-permute-start(f32[12,1,216]{2,1,0:T(1,128)S(1)} %get-tuple-element.42), channel_id=1, source_target_pairs={{0,32},{32,64},{64,96},{96,128},{128,160},{160,192},{192,224},{224... | collective-permute-start | bytes 31112 | tf_op jit(solution)/shard_map/ppermute | solution.py:20
  133.5 6.1 %collective-permute-start.14 = (f32[1,12,216]{2,1,0:T(8,128)S(1)}, f32[1,12,216]{2,1,0:T(8,128)S(1)}, u32[]{:S(2)}, u32[]{:S(2)}) collective-permute-start(f32[1,12,216]{2,1,0:T(8,128)S(1)} %slice.300), channel_id=1, source_target_pairs={{1,0},{2,1},{3,2},{4,3},{5,4},{6,5},{7,6},{8,7},{9,8},{10,9},{11,1... | collective-permute-start | bytes 31112 | tf_op jit(solution)/shard_map/ppermute | solution.py:23
  135.5 8.7 %collective-permute-start.15 = (f32[1,12,216]{2,1,0:T(8,128)S(1)}, f32[1,12,216]{2,1,0:T(8,128)S(1)}, u32[]{:S(2)}, u32[]{:S(2)}) collective-permute-start(f32[1,12,216]{2,1,0:T(8,128)S(1)} %slice.301), channel_id=1, source_target_pairs={{0,1},{1,2},{2,3},{3,4},{4,5},{5,6},{6,7},{7,8},{8,9},{9,10},{10,1... | collective-permute-start | bytes 31112 | tf_op jit(solution)/shard_map/ppermute | solution.py:20
  139.4 4.9 %copy-start.10 = (f32[12,12,216]{2,1,0:T(8,128)S(1)}, f32[12,12,216]{2,1,0:T(8,128)}, u32[]{:S(2)}) copy-start(f32[12,12,216]{2,1,0:T(8,128)} %mul.353) | copy-start | bytes 373252
  139.4 4.8 %copy-start.11 = (f32[12,12,216]{2,1,0:T(8,128)S(1)}, f32[12,12,216]{2,1,0:T(8,128)}, u32[]{:S(2)}) copy-start(f32[12,12,216]{2,1,0:T(8,128)} %mul.357) | copy-start | bytes 373252
  144.4 1.1 copy-start.18
  144.5 1.0 copy-start.19
  144.5 1.0 copy-start.20
  181.2 0.7 copy-start.29
where the time goes:
time: 184 us; the launch traced here: 183 us
  starting transfers between devices  83.2 us (45%)
  blocking collectives  35.4 us (19%)
  local copies, waits for them, and re-layouts  32.9 us (18%)
  waiting for transfers between devices  23.9 us (13%)
  other arithmetic  5.13 us (3%)
    ppermute x8, starting transfers between devices, padded(): lax.ppermute(lax.slice_in_dim(block, 0, width, axis=dim), axis, backward)  47.2 us
    all_gather x1, blocking collectives, per_device(): lax.all_gather(surface_bf, 'lon', axis=1, tiled=True)  35.4 us
    ppermute x8, starting transfers between devices, padded(): lax.ppermute(lax.slice_in_dim(block, block.shape[dim] - width, None, axis...  19.3 us
    ppermute x8, waiting for transfers between devices, padded(): lax.ppermute(lax.slice_in_dim(block, block.shape[dim] - width, None, axis...  15.6 us
    unnamed x71, local copies, waits for them, and re-layouts  10.8 us
    all_to_all x1, starting transfers between devices, per_device(): lax.all_to_all(codes, 'lon', split_axis=0, concat_axis=0, tiled=True)  8.41 us
    all_to_all x1, waiting for transfers between devices, per_device(): lax.all_to_all(sent_rows, 'lon', split_axis=0, concat_axis=0, tiled=True)  8.34 us
    all_to_all x1, starting transfers between devices, per_device(): lax.all_to_all(sent_rows, 'lon', split_axis=0, concat_axis=0, tiled=True)  8.31 us
  transfers between devices with their start and end apart: 18, of which 5 were waited for; matrix products, arithmetic and copies ran while one was open for 8% of the time, Pallas kernels for 0%

commit v1 on v0

v1 whole, which is shorter than its diff:
```python
import functools

import jax
import jax.numpy as jnp
from jax import lax
from jax.experimental import pallas as pl
from jax.experimental.pallas import tpu as pltpu
from jax.sharding import PartitionSpec as P

CAP = 8
HORIZ_MIX = 0.18
VERT_MIX = 0.1
CENTER = 1.0 - 4.0 * HORIZ_MIX - 2.0 * VERT_MIX

ROWS = 12
HALO = 4
SUB = 16
WIDE = 256
LEVELS = 72
SPECIES = 3
WIDTH = SPECIES * LEVELS
CODE_LANE = 216
KERNEL_LANE = 217
F32 = jnp.float32
BF16 = jnp.bfloat16


def iota(shape, dim):
    return lax.broadcasted_iota(jnp.int32, shape, dim)


def vmem_call(body, outs, scratch=(), name=None):
    return pl.pallas_call(
        body,
        out_shape=outs,
        scratch_shapes=list(scratch),
        name=name,
        compiler_params=pltpu.CompilerParams(vmem_limit_bytes=48 * 1024 * 1024),
    )


def split2(value):
    high = value.astype(BF16).astype(F32)
    return high, (value - high).astype(BF16).astype(F32)


def route_body(innov_ref, columns_ref, kernels_ref, counts_ref, offsets_ref, out_ref, padded_ref):
    held = innov_ref.shape[2]
    owners = counts_ref.shape[2]
    eye = iota((owners, owners), 0) == iota((owners, owners), 1)
    offset_col = jnp.sum(jnp.where(eye, offsets_ref[0].astype(F32), 0.0), axis=1, keepdims=True)
    count_col = jnp.sum(jnp.where(eye, counts_ref[0].astype(F32), 0.0), axis=1, keepdims=True)
    place = iota((owners, held), 1).astype(F32) - offset_col
    place = jnp.where(place < count_col, place, -1.0)
    slot = iota((owners, CAP, held), 1).astype(F32)
    pick = jnp.where(place[:, None, :] == slot, 1.0, 0.0).reshape(owners * CAP, held).astype(BF16)
    padded_ref[...] = jnp.zeros_like(padded_ref)
    padded_ref[:, :WIDTH] = innov_ref[0, 0]
    cell = columns_ref[0]
    code = (cell + 4 * ((cell * 171) >> 11) + 1).astype(F32)
    half = WIDE // 2
    line = iota((half, held), 0)
    codes = jnp.where(
        line == CODE_LANE - half,
        code,
        jnp.where(line == KERNEL_LANE - half, kernels_ref[0].astype(F32), 0.0),
    ).astype(BF16)
    sent = jnp.dot(pick, padded_ref[...], preferred_element_type=F32)
    tail = lax.dot_general(pick, codes, (((1,), (1,)), ((), ())), preferred_element_type=F32)
    out_ref[:, :half] = sent[:, :half].astype(BF16)
    out_ref[:, half:] = (sent[:, half:] + tail).astype(BF16)


def pad_winds_body(winds_ref, out_ref):
    out_ref[...] = jnp.zeros_like(out_ref)
    out_ref[:, :, :ROWS, : 2 * LEVELS] = winds_ref[...]


def force_body(recv_ref, table_ref, adjoint_ref, winds_ref, lam_ref, north_ref, south_ref, table_s):
    total = recv_ref.shape[0]
    nkernel = table_ref.shape[0]
    recv = recv_ref[...]
    wide = recv.astype(F32)
    pick = jnp.where((iota((8, WIDE), 1) == CODE_LANE), 1.0, 0.0).astype(BF16)
    code_line = lax.dot_general(pick, recv, (((1,), (1,)), ((), ())), preferred_element_type=F32)
    kernel_col = wide[:, KERNEL_LANE : KERNEL_LANE + 1]
    lane = iota((total, 3 * nkernel), 1)
    lane = (lane - jnp.where(lane >= nkernel, nkernel, 0) - jnp.where(lane >= 2 * nkernel, nkernel, 0)).astype(F32)
    onehot = jnp.where(kernel_col == lane, 1.0, 0.0).astype(BF16)
    table = table_ref[...]
    table_s[...] = jnp.zeros_like(table_s)
    high = table.astype(BF16)
    rest = table - high.astype(F32)
    middle = rest.astype(BF16)
    table_s[0:nkernel, :WIDTH] = high
    table_s[nkernel : 2 * nkernel, :WIDTH] = middle
    table_s[2 * nkernel :, :WIDTH] = (rest - middle.astype(F32)).astype(BF16)
    weights = jnp.dot(onehot, table_s[...], preferred_element_type=F32)
    weighted = wide * weights
    whigh = weighted.astype(BF16)
    wlow = (weighted - whigh.astype(F32)).astype(BF16)
    cell = (iota((ROWS * SUB, total), 0) + 1).astype(F32)
    scatter = jnp.where(cell == code_line[0:1, :], 1.0, 0.0).astype(BF16)
    force = jnp.dot(scatter, whigh, preferred_element_type=F32) + jnp.dot(
        scatter, wlow, preferred_element_type=F32
    )
    lam_ref[...] = force.reshape(ROWS, SUB, WIDE)
    lam_ref[:, :ROWS, :WIDTH] = lam_ref[:, :ROWS, :WIDTH] + adjoint_ref[...]
    for strip, first in ((north_ref, ROWS - HALO), (south_ref, 0)):
        edge = lam_ref[first : first + HALO]
        ehigh = edge.astype(BF16)
        strip[0:4] = ehigh
        strip[4:8] = (edge - ehigh.astype(F32)).astype(BF16)
        base = 8
        for step in (1, 2, 3):
            depth = HALO - step
            start = ROWS - depth if first else 0
            strip[base : base + depth] = winds_ref[4 - step, start : start + depth]
            base += depth


WIND_BASE = {1: 8, 2: 11, 3: 13}


def ext_lam(lam_ref, from_north, from_south, row):
    if 0 <= row < ROWS:
        return lam_ref[row]
    strip, index = (from_north, row - ROWS) if row >= ROWS else (from_south, row + HALO)
    return strip[index].astype(F32) + strip[index + 4].astype(F32)


def ext_wind(winds_ref, from_north, from_south, step, row):
    if 0 <= row < ROWS:
        return winds_ref[4 - step, row].astype(F32)
    depth = HALO - step
    if row >= ROWS:
        strip, index = from_north, row - ROWS
    else:
        strip, index = from_south, row + depth
    if not 0 <= index < depth:
        return jnp.zeros((SUB, WIDE), F32)
    return strip[WIND_BASE[step] + index].astype(F32)


def ext_index(row):
    return row if row >= 0 else row + ROWS + 2 * HALO


def edge_body(lam_ref, from_north, from_south, winds_ref, east_ref, west_ref):
    sub = iota((8, WIDE), 0)
    for row in range(-HALO, ROWS + HALO):
        lam = ext_lam(lam_ref, from_north, from_south, row)
        w1 = ext_wind(winds_ref, from_north, from_south, 1, row)
        w2 = ext_wind(winds_ref, from_north, from_south, 2, row)
        w3 = ext_wind(winds_ref, from_north, from_south, 3, row)
        for out, tile in ((east_ref, 1), (west_ref, 0)):
            cut = slice(8 * tile, 8 * tile + 8)
            high, low = split2(lam[cut])
            values = jnp.where(sub < 4, high, pltpu.roll(low, 4, 0))
            first = pltpu.roll(w1[cut], 4, 0)
            if tile == 1:
                rest = jnp.where(sub >= 2, w2[cut], pltpu.roll(w3[cut], 6, 0))
            else:
                rest = jnp.where(sub < 2, w2[cut], pltpu.roll(w3[cut], 2, 0))
            winds = jnp.where(sub >= 4, first, rest)
            out[ext_index(row)] = jnp.concatenate([values, winds], axis=0).astype(BF16)


def steps_body(
    lam_ref, from_north, from_south, winds_ref, from_east, from_west, field_ref, surface_ref,
    lam_a, lam_b, wide_s, coef_s, acc_s,
):
    lat = lax.axis_index("lat")
    has_south = jnp.where(lat > 0, 1.0, 0.0).astype(F32)
    has_north = jnp.where(lat < lax.axis_size("lat") - 1, 1.0, 0.0).astype(F32)
    cols = SUB + 8
    sub = iota((8, WIDE), 0)
    for row in range(-HALO, ROWS + HALO):
        at = ext_index(row)
        lam = ext_lam(lam_ref, from_north, from_south, row)
        east = from_east[at].astype(F32)
        west = from_west[at].astype(F32)
        east_lam = east[0:8] + pltpu.roll(east[0:8], 4, 0)
        west_lam = west[0:8] + pltpu.roll(west[0:8], 4, 0)
        lam_a[at, 0:8] = lam[0:8]
        lam_a[at, 8:16] = jnp.where(sub < 4, lam[8:16], east_lam)
        lam_a[at, 16:24] = west_lam
        for step in range(1, 5):
            reach = HALO - step
            if not -reach <= row < ROWS + reach:
                continue
            wind = ext_wind(winds_ref, from_north, from_south, step, row)
            ew, ww = east[8:16], west[8:16]
            if step == 2:
                ew, ww = pltpu.roll(ew, 4, 0), pltpu.roll(ww, 4, 0)
            if step == 3:
                ew, ww = pltpu.roll(ew, 2, 0), pltpu.roll(ww, 6, 0)
            place = (step - 1) * (ROWS + 2 * HALO) + at
            wide_s[place, 0:16] = jnp.concatenate(
                [wind[0:8], jnp.where(sub < 4, wind[8:16], ew)], axis=0
            ).astype(BF16)
            wide_s[place, 16:24] = ww.astype(BF16)
    spread_k = iota((WIDE, 2 * WIDE), 0)
    spread_n = iota((WIDE, 2 * WIDE), 1)
    north_half = spread_n >= WIDE
    lane_n = jnp.where(north_half, spread_n - WIDE, spread_n)
    level_n = lane_n - jnp.where(lane_n >= LEVELS, LEVELS, 0) - jnp.where(lane_n >= 2 * LEVELS, LEVELS, 0)
    match = (spread_k == level_n + jnp.where(north_half, LEVELS, 0)) & (lane_n < WIDTH)
    spread = jnp.where(match, 0.5, 0.0).astype(BF16)
    lane = iota((cols, WIDE), 1)
    top = (lane == LEVELS - 1) | (lane == 2 * LEVELS - 1) | (lane == 3 * LEVELS - 1)
    bottom = (lane == 0) | (lane == LEVELS) | (lane == 2 * LEVELS)
    now, later = lam_a, lam_b
    for step in range(1, 5):
        reach = HALO - step
        rows = list(range(-reach, ROWS + reach))
        order = sorted(ext_index(r) for r in rows)
        groups = [(0, ROWS + reach)]
        if reach:
            groups.append((ROWS + 2 * HALO - reach, ROWS + 2 * HALO))
        base = (step - 1) * (ROWS + 2 * HALO)
        for lo, hi in groups:
            lhs = wide_s[base + lo : base + hi].reshape((hi - lo) * cols, WIDE)
            coef_s[lo:hi] = jnp.dot(lhs, spread, preferred_element_type=F32).reshape(hi - lo, cols, 2 * WIDE)
        del order
        for row in rows:
            at = ext_index(row)
            mid = now[at]
            north = now[ext_index(row + 1)]
            south = now[ext_index(row - 1)]
            east = pltpu.roll(mid, cols - 1, 0)
            west = pltpu.roll(mid, 1, 0)
            upper = jnp.where(top, mid, pltpu.roll(mid, WIDE - 1, 1))
            lower = jnp.where(bottom, mid, pltpu.roll(mid, 1, 1))
            u = coef_s[at, :, :WIDE]
            v = coef_s[at, :, WIDE:]
            new = (
                CENTER * mid
                + u * (east - west)
                + v * (north - south)
                + HORIZ_MIX * ((east + west) + (north + south))
                + VERT_MIX * (upper + lower)
            )
            if row < 0:
                new = new * has_south
            if row >= ROWS:
                new = new * has_north
            if step < 4:
                later[at] = new
            else:
                field_ref[row] = new[:ROWS, :WIDTH]
            if 0 <= row < ROWS:
                if step == 1:
                    acc_s[row] = new[:SUB]
                else:
                    acc_s[row] = acc_s[row] + new[:SUB]
        now, later = later, now
    lane = iota((SUB, 128), 1)
    surface = jnp.zeros((SUB, 128), F32)
    for row in range(ROWS):
        for species in range(SPECIES):
            at = row * SPECIES + species
            source = species * LEVELS
            half = acc_s[row][:, 128 * (source // 128) : 128 * (source // 128) + 128]
            moved = pltpu.roll(half, (at - source % 128) % 128, 1)
            surface = jnp.where(lane == at, moved, surface)
    surface = jnp.where(iota((SUB, 128), 0) < ROWS, surface, 0.0).astype(BF16)
    for target in range(surface_ref.shape[0]):
        surface_ref[target] = surface


def pad_correlation_body(correlation_ref, out_ref):
    total, mine = correlation_ref.shape
    out_ref[...] = jnp.zeros_like(out_ref)
    for block in range(total // ROWS):
        out_ref[block, :ROWS, :mine] = correlation_ref[block * ROWS : block * ROWS + ROWS]


def gradient_body(surface_ref, correlation_ref, out_ref):
    blocks = surface_ref.shape[0]
    surface = surface_ref[...].reshape(blocks * SUB, 128)
    correlation = correlation_ref[...].reshape(blocks * SUB, 128)
    result = lax.dot_general(surface, correlation, (((0,), (0,)), ((), ())), preferred_element_type=F32)
    for row in range(ROWS):
        out_ref[row] = result[SPECIES * row : SPECIES * row + SPECIES, :ROWS]


def per_device(
    adjoint_in, stored_winds, innovations, columns, kernel_ids, counts, offsets, kernel_table, correlation
):
    lon_count = lax.axis_size("lon")
    lat_count = lax.axis_size("lat")
    shape = jax.ShapeDtypeStruct
    sent = vmem_call(
        route_body,
        shape((lon_count * CAP, WIDE), BF16),
        [pltpu.VMEM((innovations.shape[2], WIDE), BF16)],
        name="route",
    )(innovations, columns, kernel_ids, counts, offsets)
    recv = lax.all_to_all(sent, "lon", split_axis=0, concat_axis=0, tiled=True)
    winds = vmem_call(pad_winds_body, shape((4, ROWS, SUB, WIDE), BF16), name="pad_winds")(stored_winds)
    spread = vmem_call(pad_correlation_body, shape((lon_count, SUB, 128), BF16), name="pad_correlation")(correlation)
    strip = shape((14, SUB, WIDE), BF16)
    lam, north, south = vmem_call(
        force_body,
        (shape((ROWS, SUB, WIDE), F32), strip, strip),
        [pltpu.VMEM((3 * kernel_table.shape[0], WIDE), BF16)],
        name="force",
    )(recv, kernel_table, adjoint_in, winds)
    up = [(i, i + 1) for i in range(lat_count - 1)]
    down = [(i + 1, i) for i in range(lat_count - 1)]
    from_south = lax.ppermute(north, "lat", up)
    from_north = lax.ppermute(south, "lat", down)
    edge = shape((ROWS + 2 * HALO, SUB, WIDE), BF16)
    east, west = vmem_call(edge_body, (edge, edge), name="edge")(lam, from_north, from_south, winds)
    forward = [(i, (i + 1) % lon_count) for i in range(lon_count)]
    backward = [((i + 1) % lon_count, i) for i in range(lon_count)]
    from_west = lax.ppermute(east, "lon", forward)
    from_east = lax.ppermute(west, "lon", backward)
    ext = ROWS + 2 * HALO
    cols = SUB + 8
    field, surface = vmem_call(
        steps_body,
        (shape((ROWS, ROWS, WIDTH), F32), shape((lon_count, SUB, 128), BF16)),
        [
            pltpu.VMEM((ext, cols, WIDE), F32),
            pltpu.VMEM((ext, cols, WIDE), F32),
            pltpu.VMEM((4 * ext, cols, WIDE), BF16),
            pltpu.VMEM((ext, cols, 2 * WIDE), F32),
            pltpu.VMEM((ROWS, SUB, WIDE), F32),
        ],
        name="steps",
    )(lam, from_north, from_south, winds, from_east, from_west)
    gathered = lax.all_to_all(surface, "lon", split_axis=0, concat_axis=0, tiled=True)
    gradient = vmem_call(gradient_body, shape((ROWS, SPECIES, ROWS), F32), name="gradient")(gathered, spread)
    return field, gradient


def solution(mesh):
    return jax.shard_map(
        per_device,
        mesh=mesh,
        in_specs=(
            P("lat", "lon", None),
            P(None, "lat", "lon", None),
            P("lat", "lon", None, None),
            P("lat", "lon", None),
            P("lat", "lon", None),
            P("lat", "lon", None),
            P("lat", "lon", None),
            P(),
            P(None, "lon"),
        ),
        out_specs=(P("lat", "lon", None), P("lat", None, "lon")),
        check_vma=False,
    )
```

time: 184 us -> 80.8 us (0.44)
  the two profiles are of different devices: /device:TPU:9 before, /device:TPU:14 now
where the time goes in v1:
time: 80.8 us; the launch traced here: 80.4 us
  starting transfers between devices  39.9 us (49%)
  waiting for transfers between devices  33.7 us (42%)
  Pallas kernels  4.7 us (6%)
  local copies, waits for them, and re-layouts  1.25 us (2%)
  between operations  0.83 us (1%)
    ppermute x1, starting transfers between devices, per_device(): from_north = lax.ppermute(south, 'lat', down)  19.1 us
    ppermute x1, waiting for transfers between devices, per_device(): from_south = lax.ppermute(north, 'lat', up)  9.54 us
    all_to_all x1, starting transfers between devices, per_device(): recv = lax.all_to_all(sent, 'lon', split_axis=0, concat_axis=0, tiled=True)  9.18 us
    all_to_all x1, waiting for transfers between devices, per_device(): recv = lax.all_to_all(sent, 'lon', split_axis=0, concat_axis=0, tiled=True)  8.54 us
    all_to_all x1, waiting for transfers between devices, per_device(): lax.all_to_all(surface, 'lon', split_axis=0, concat_axis=0, tiled=True)  8.49 us
    ppermute x1, waiting for transfers between devices, per_device(): from_west = lax.ppermute(east, 'lon', forward)  5.93 us
    all_to_all x1, starting transfers between devices, per_device(): lax.all_to_all(surface, 'lon', split_axis=0, concat_axis=0, tiled=True)  5.43 us
    ppermute x1, starting transfers between devices, per_device(): from_west = lax.ppermute(east, 'lon', forward)  2.41 us
  transfers between devices with their start and end apart: 6, of which 6 were waited for; matrix products, arithmetic and copies ran while one was open for 0% of the time, Pallas kernels for 0%

profile of v1, /device:TPU:14, one launch (start us, length us, event | category | flops | bytes accessed | tf_op | source)
XLA Modules:
  0.0 80.4 jit_solution(12884886457389449634)
XLA Ops:
  0.6 0.0 copy-start.2
  0.6 0.0 copy-start.3
  0.7 0.0 copy-start.4
  0.7 0.0 copy-start.5
  0.7 1.0 %copy.11.innov_ref = bf16[1,1,256,216]{3,2,1,0:T(8,128)(2,1)S(1)} copy(bf16[1,1,256,216]{2,3,1,0:T(8,128)(2,1)} %param.11) | data formatting | bytes 221184 | tf_op args[2]
  1.7 0.0 copy-done.2
  1.7 0.0 copy-done.3
  1.7 0.0 copy-done.4
  1.7 0.0 copy-done.5
  1.7 0.0 copy-start.6
  1.7 1.0 %route.1 = bf16[256,256]{1,0:T(8,128)(2,1)} custom-call(bf16[1,1,256,216]{3,2,1,0:T(8,128)(2,1)S(1)} %copy.11.innov_ref, s32[1,1,256]{2,1,0:T(1,128)S(1)} %copy-done.2, s32[1,1,256]{2,1,0:T(1,128)S(1)} %copy-done.3, s32[1,1,32]{2,1,0:T(1,128)S(1)} %copy-done.4, s32[1,1,32]{2,1,0:T(1,128)S(1)} %copy-done.5), custom_call_target="tpu_custom_call" | custom-call | tf_op jit(solution)/shard_map/route/pallas_call | solution.py:294
  2.7 9.2 %all-to-all-start = ((bf16[32,8,256]{2,1,0:T(8,128)(2,1)}), bf16[32,8,256]{2,1,0:T(8,128)(2,1)S(1)}, u32[]{:S(2)}, u32[]{:S(2)}) async-start(bf16[32,8,256]{2,1,0:T(8,128)(2,1)} %bitcast), calls=%async_computation | async-start | bytes 262144 | tf_op jit(solution)/shard_map/all_to_all | solution.py:300
  11.9 0.0 copy-done.6
  12.0 0.0 copy-start
  12.0 0.0 copy-start.1
  12.0 0.1 pad_winds.1.winds_ref
  12.0 8.5 %all-to-all-done = bf16[32,8,256]{2,1,0:T(8,128)(2,1)S(1)} async-done(((bf16[32,8,256]{2,1,0:T(8,128)(2,1)}), bf16[32,8,256]{2,1,0:T(8,128)(2,1)S(1)}, u32[]{:S(2)}, u32[]{:S(2)}) %all-to-all-start) | async-done | bytes 131104 | tf_op jit(solution)/shard_map/all_to_all | solution.py:300
  20.6 0.0 copy-done
  20.6 0.0 copy-done.1
  20.6 0.5 force.1
  21.1 19.1 %collective-permute-start = (bf16[14,16,256]{2,1,0:T(8,128)(2,1)S(1)}, bf16[14,16,256]{2,1,0:T(8,128)(2,1)S(1)}, u32[]{:S(2)}, u32[]{:S(2)}) collective-permute-start(bf16[14,16,256]{2,1,0:T(8,128)(2,1)S(1)} %get-tuple-element.10), channel_id=1, source_target_pairs={{1,0},{2,1},{3,2},{4,3},{5,4},{6,5},{7,6},{8,7},{9,8},{10,9},{11,1... | collective-permute-start | bytes 344072 | tf_op jit(solution)/shard_map/ppermute | solution.py:313
  40.1 1.9 %collective-permute-start.1 = (bf16[14,16,256]{2,1,0:T(8,128)(2,1)S(1)}, bf16[14,16,256]{2,1,0:T(8,128)(2,1)S(1)}, u32[]{:S(2)}, u32[]{:S(2)}) collective-permute-start(bf16[14,16,256]{2,1,0:T(8,128)(2,1)S(1)} %get-tuple-element.11), channel_id=1, source_target_pairs={{0,1},{1,2},{2,3},{3,4},{4,5},{5,6},{6,7},{7,8},{8,9},{9,10},{10,1... | collective-permute-start | bytes 344072 | tf_op jit(solution)/shard_map/ppermute | solution.py:312
  42.1 0.8 collective-permute-done.from_north
  42.9 9.5 %collective-permute-done.1.from_south = bf16[14,16,256]{2,1,0:T(8,128)(2,1)S(1)} collective-permute-done((bf16[14,16,256]{2,1,0:T(8,128)(2,1)S(1)}, bf16[14,16,256]{2,1,0:T(8,128)(2,1)S(1)}, u32[]{:S(2)}, u32[]{:S(2)}) %collective-permute-start.1) | collective-permute-done | bytes 114720 | tf_op jit(solution)/shard_map/ppermute | solution.py:312
  52.4 0.1 edge.1
  52.5 1.9 %collective-permute-start.2 = (bf16[20,16,256]{2,1,0:T(8,128)(2,1)S(1)}, bf16[20,16,256]{2,1,0:T(8,128)(2,1)S(1)}, u32[]{:S(2)}, u32[]{:S(2)}) collective-permute-start(bf16[20,16,256]{2,1,0:T(8,128)(2,1)S(1)} %get-tuple-element.12), channel_id=1, source_target_pairs={{32,0},{64,32},{96,64},{128,96},{160,128},{192,160},{224,192},{256... | collective-permute-start | bytes 491528 | tf_op jit(solution)/shard_map/ppermute | solution.py:319
  54.5 2.4 %collective-permute-start.3 = (bf16[20,16,256]{2,1,0:T(8,128)(2,1)S(1)}, bf16[20,16,256]{2,1,0:T(8,128)(2,1)S(1)}, u32[]{:S(2)}, u32[]{:S(2)}) collective-permute-start(bf16[20,16,256]{2,1,0:T(8,128)(2,1)S(1)} %get-tuple-element.13), channel_id=1, source_target_pairs={{0,32},{32,64},{64,96},{96,128},{128,160},{160,192},{192,224},{224... | collective-permute-start | bytes 491528 | tf_op jit(solution)/shard_map/ppermute | solution.py:318
  56.9 0.4 collective-permute-done.2.from_east
  57.3 5.9 %collective-permute-done.3.from_west = bf16[20,16,256]{2,1,0:T(8,128)(2,1)S(1)} collective-permute-done((bf16[20,16,256]{2,1,0:T(8,128)(2,1)S(1)}, bf16[20,16,256]{2,1,0:T(8,128)(2,1)S(1)}, u32[]{:S(2)}, u32[]{:S(2)}) %collective-permute-start.3) | collective-permute-done | bytes 163872 | tf_op jit(solution)/shard_map/ppermute | solution.py:318
  63.2 2.2 %steps.1 = (f32[12,12,216]{2,1,0:T(8,128)}, bf16[32,16,128]{2,1,0:T(8,128)(2,1)}) custom-call(f32[12,16,256]{2,1,0:T(8,128)S(1)} %get-tuple-element.9.lam_ref, bf16[14,16,256]{2,1,0:T(8,128)(2,1)S(1)} %collective-permute-done.from_north, bf16[14,16,256]{2,1,0:T(8,128)(2,1)S(1)} %collective-permute-done.1.from_south, ...), custom_call_target="tpu_custom_call" | custom-call | tf_op jit(solution)/shard_map/steps/pallas_call | solution.py:322
  65.4 0.0 copy-start.7
  65.4 5.4 %all-to-all-start.1 = ((bf16[32,16,128]{2,1,0:T(8,128)(2,1)}), bf16[32,16,128]{2,1,0:T(8,128)(2,1)S(1)}, u32[]{:S(2)}, u32[]{:S(2)}) async-start(bf16[32,16,128]{2,1,0:T(8,128)(2,1)} %get-tuple-element.15), calls=%async_computation.1 | async-start | bytes 262144 | tf_op jit(solution)/shard_map/all_to_all | solution.py:334
  70.9 0.0 copy-done.7
  70.9 0.1 copy.13.correlation_ref
  71.1 8.5 %all-to-all-done.1.surface_ref = bf16[32,16,128]{2,1,0:T(8,128)(2,1)S(1)} async-done(((bf16[32,16,128]{2,1,0:T(8,128)(2,1)}), bf16[32,16,128]{2,1,0:T(8,128)(2,1)S(1)}, u32[]{:S(2)}, u32[]{:S(2)}) %all-to-all-start.1) | async-done | bytes 131104 | tf_op jit(solution)/shard_map/all_to_all | solution.py:334
  79.6 0.8 %gradient.1 = f32[12,3,12]{2,1,0:T(4,128)} custom-call(bf16[32,16,128]{2,1,0:T(8,128)(2,1)S(1)} %all-to-all-done.1.surface_ref, bf16[32,16,128]{2,1,0:T(8,128)(2,1)S(1)} %pad_correlation.1.correlation_ref), custom_call_target="tpu_custom_call" | custom-call | tf_op jit(solution)/shard_map/gradient/pallas_call | solution.py:335
  (2 shorter events, 0.1 us)
Async XLA Ops:
  0.6 1.1 %copy-start.2 = (s32[1,1,256]{2,1,0:T(1,128)S(1)}, s32[1,1,256]{2,1,0:T(1,128)}, u32[]{:S(2)}) copy-start(s32[1,1,256]{2,1,0:T(1,128)} %columns_ref.1) | copy-start | bytes 3076
  0.6 1.1 %copy-start.3 = (s32[1,1,256]{2,1,0:T(1,128)S(1)}, s32[1,1,256]{2,1,0:T(1,128)}, u32[]{:S(2)}) copy-start(s32[1,1,256]{2,1,0:T(1,128)} %kernels_ref.1) | copy-start | bytes 3076
  0.7 1.1 %copy-start.4 = (s32[1,1,32]{2,1,0:T(1,128)S(1)}, s32[1,1,32]{2,1,0:T(1,128)}, u32[]{:S(2)}) copy-start(s32[1,1,32]{2,1,0:T(1,128)} %counts_ref.1) | copy-start | bytes 388
  0.7 1.1 %copy-start.5 = (s32[1,1,32]{2,1,0:T(1,128)S(1)}, s32[1,1,32]{2,1,0:T(1,128)}, u32[]{:S(2)}) copy-start(s32[1,1,32]{2,1,0:T(1,128)} %offsets_ref.1) | copy-start | bytes 388
  1.7 10.2 %copy-start.6 = (bf16[4,12,12,144]{3,0,2,1:T(4,128)(2,1)S(1)}, bf16[4,12,12,144]{3,0,2,1:T(4,128)(2,1)}, u32[]{:S(2)}) copy-start(bf16[4,12,12,144]{3,0,2,1:T(4,128)(2,1)} %param.10) | copy-start | bytes 497668
  2.7 17.9 %all-to-all-start = ((bf16[32,8,256]{2,1,0:T(8,128)(2,1)}), bf16[32,8,256]{2,1,0:T(8,128)(2,1)S(1)}, u32[]{:S(2)}, u32[]{:S(2)}) async-start(bf16[32,8,256]{2,1,0:T(8,128)(2,1)} %bitcast), calls=%async_computation | async-start | bytes 262144 | tf_op jit(solution)/shard_map/all_to_all | solution.py:300
  12.0 8.6 %copy-start = (f32[12,12,216]{2,1,0:T(8,128)S(1)}, f32[12,12,216]{2,1,0:T(8,128)}, u32[]{:S(2)}) copy-start(f32[12,12,216]{2,1,0:T(8,128)} %adjoint_ref.1) | copy-start | bytes 373252
  12.0 8.6 %copy-start.1 = (f32[64,216]{1,0:T(8,128)S(1)}, f32[64,216]{1,0:T(8,128)}, u32[]{:S(2)}) copy-start(f32[64,216]{1,0:T(8,128)} %table_ref.1) | copy-start | bytes 165892
  21.1 21.8 %collective-permute-start = (bf16[14,16,256]{2,1,0:T(8,128)(2,1)S(1)}, bf16[14,16,256]{2,1,0:T(8,128)(2,1)S(1)}, u32[]{:S(2)}, u32[]{:S(2)}) collective-permute-start(bf16[14,16,256]{2,1,0:T(8,128)(2,1)S(1)} %get-tuple-element.10), channel_id=1, source_target_pairs={{1,0},{2,1},{3,2},{4,3},{5,4},{6,5},{7,6},{8,7},{9,8},{10,9},{11,1... | collective-permute-start | bytes 344072 | tf_op jit(solution)/shard_map/ppermute | solution.py:313
  40.1 12.2 %collective-permute-start.1 = (bf16[14,16,256]{2,1,0:T(8,128)(2,1)S(1)}, bf16[14,16,256]{2,1,0:T(8,128)(2,1)S(1)}, u32[]{:S(2)}, u32[]{:S(2)}) collective-permute-start(bf16[14,16,256]{2,1,0:T(8,128)(2,1)S(1)} %get-tuple-element.11), channel_id=1, source_target_pairs={{0,1},{1,2},{2,3},{3,4},{4,5},{5,6},{6,7},{7,8},{8,9},{9,10},{10,1... | collective-permute-start | bytes 344072 | tf_op jit(solution)/shard_map/ppermute | solution.py:312
  52.5 4.7 %collective-permute-start.2 = (bf16[20,16,256]{2,1,0:T(8,128)(2,1)S(1)}, bf16[20,16,256]{2,1,0:T(8,128)(2,1)S(1)}, u32[]{:S(2)}, u32[]{:S(2)}) collective-permute-start(bf16[20,16,256]{2,1,0:T(8,128)(2,1)S(1)} %get-tuple-element.12), channel_id=1, source_target_pairs={{32,0},{64,32},{96,64},{128,96},{160,128},{192,160},{224,192},{256... | collective-permute-start | bytes 491528 | tf_op jit(solution)/shard_map/ppermute | solution.py:319
  54.5 8.7 %collective-permute-start.3 = (bf16[20,16,256]{2,1,0:T(8,128)(2,1)S(1)}, bf16[20,16,256]{2,1,0:T(8,128)(2,1)S(1)}, u32[]{:S(2)}, u32[]{:S(2)}) collective-permute-start(bf16[20,16,256]{2,1,0:T(8,128)(2,1)S(1)} %get-tuple-element.13), channel_id=1, source_target_pairs={{0,32},{32,64},{64,96},{96,128},{128,160},{160,192},{192,224},{224... | collective-permute-start | bytes 491528 | tf_op jit(solution)/shard_map/ppermute | solution.py:318
  65.4 5.4 %copy-start.7 = (bf16[384,12]{0,1:T(8,128)(2,1)S(1)}, bf16[384,12]{0,1:T(8,128)(2,1)}, u32[]{:S(2)}) copy-start(bf16[384,12]{0,1:T(8,128)(2,1)} %param.17) | copy-start | bytes 27652
  65.4 14.1 %all-to-all-start.1 = ((bf16[32,16,128]{2,1,0:T(8,128)(2,1)}), bf16[32,16,128]{2,1,0:T(8,128)(2,1)S(1)}, u32[]{:S(2)}, u32[]{:S(2)}) async-start(bf16[32,16,128]{2,1,0:T(8,128)(2,1)} %get-tuple-element.15), calls=%async_computation.1 | async-start | bytes 262144 | tf_op jit(solution)/shard_map/all_to_all | solution.py:334

commit v2 on v1

v2 whole, which is shorter than its diff:
```python
import functools

import jax
import jax.numpy as jnp
from jax import lax
from jax.experimental import pallas as pl
from jax.experimental.pallas import tpu as pltpu
from jax.sharding import PartitionSpec as P

CAP = 8
HORIZ_MIX = 0.18
VERT_MIX = 0.1
CENTER = 1.0 - 4.0 * HORIZ_MIX - 2.0 * VERT_MIX

ROWS = 12
HALO = 4
SUB = 16
WIDE = 256
LEVELS = 72
SPECIES = 3
WIDTH = SPECIES * LEVELS
CODE_LANE = 216
KERNEL_LANE = 217
F32 = jnp.float32
BF16 = jnp.bfloat16


def iota(shape, dim):
    return lax.broadcasted_iota(jnp.int32, shape, dim)


def vmem_call(body, outs, scratch=(), name=None, limit=48 * 1024 * 1024, **specs):
    return pl.pallas_call(
        body,
        out_shape=outs,
        scratch_shapes=list(scratch),
        name=name,
        compiler_params=pltpu.CompilerParams(vmem_limit_bytes=limit),
        **specs,
    )


def split2(value):
    high = value.astype(BF16).astype(F32)
    return high, (value - high).astype(BF16).astype(F32)


def route_body(
    counts_hbm, offsets_hbm, columns_hbm, kernels_hbm, innov_hbm, out_ref,
    counts_s, offsets_s, columns_s, kernels_s, innov_s, sems,
):
    moves = (
        (counts_hbm.at[0], counts_s),
        (offsets_hbm.at[0], offsets_s),
        (columns_hbm.at[0], columns_s),
        (kernels_hbm.at[0], kernels_s),
        (innov_hbm.at[0, 0], innov_s),
    )
    copies = [pltpu.make_async_copy(source, target, sems.at[i]) for i, (source, target) in enumerate(moves)]
    for copy in copies:
        copy.start()
    for copy in copies[:4]:
        copy.wait()
    held = innov_s.shape[1]
    owners = counts_s.shape[1]
    eye = iota((owners, owners), 0) == iota((owners, owners), 1)
    offset_col = jnp.sum(jnp.where(eye, offsets_s[...].astype(F32), 0.0), axis=1, keepdims=True)
    count_col = jnp.sum(jnp.where(eye, counts_s[...].astype(F32), 0.0), axis=1, keepdims=True)
    place = iota((owners, held), 1).astype(F32) - offset_col
    place = jnp.where(place < count_col, place, -1.0)
    slot = iota((owners, CAP, held), 1).astype(F32)
    pick = jnp.where(place[:, None, :] == slot, 1.0, 0.0).reshape(owners * CAP, held).astype(BF16)
    cell = columns_s[...]
    code = (cell + 4 * ((cell * 171) >> 11) + 1).astype(F32)
    half = WIDE // 2
    line = iota((half, held), 0)
    codes = jnp.where(
        line == CODE_LANE - half,
        code,
        jnp.where(line == KERNEL_LANE - half, kernels_s[...].astype(F32), 0.0),
    ).astype(BF16)
    tail = lax.dot_general(pick, codes, (((1,), (1,)), ((), ())), preferred_element_type=F32)
    out_ref[:, half:] = tail.astype(BF16)
    copies[4].wait()
    sent = lax.dot_general(
        pick, innov_s[...], (((1,), (1,)), ((), ())), preferred_element_type=F32
    ).astype(BF16)
    out_ref[:, :half] = sent[:, :half]
    out_ref[:, half:WIDTH] = sent[:, half:]


def pad_winds_body(winds_ref, out_ref):
    out_ref[...] = jnp.zeros_like(out_ref)
    out_ref[:, :, :ROWS, : 2 * LEVELS] = winds_ref[...]


STRIP = 17


def pieces(row):
    return pltpu.roll(row[0:8], 4, 0), row[0:8], pltpu.roll(row[8:16], 4, 0)


def with_piece(row, piece):
    sub = iota((8, row.shape[1]), 0)
    return jnp.concatenate([row[0:8], jnp.where(sub < 4, row[8:16], piece)], axis=0)


def pack_strip(lam_rows, wind_rows):
    parts = [split2(row) for row in lam_rows]
    rows = [high for high, _ in parts] + [low for _, low in parts]
    extra = pieces(rows[6]) + pieces(rows[7])
    lane = iota((SUB, 128), 1)
    halves = []
    for index in range(6):
        packed = with_piece(rows[index], extra[index])
        spare = pltpu.roll(wind_rows[index][:, 128:], WIDTH - 128, 1)
        halves += [packed[:, :128], jnp.where(lane < WIDTH - 128, packed[:, 128:], spare)]
    main = [row[:, :128] for row in wind_rows]
    extra = pieces(main[4])
    halves += [with_piece(main[index], extra[index]) for index in range(3)] + [main[3], main[5]]
    return halves


def unpack_strip(halves):
    lane = iota((SUB, 128), 1)
    sub = iota((8, WIDE), 0)
    tiles = [
        jnp.concatenate([halves[2 * i], jnp.where(lane < WIDTH - 128, halves[2 * i + 1], 0.0)], axis=1)
        for i in range(6)
    ]
    rows = list(tiles)
    for index in (0, 3):
        first, second, third = (tile[8:16] for tile in tiles[index : index + 3])
        rows.append(
            jnp.concatenate([jnp.where(sub < 4, pltpu.roll(first, 4, 0), second), pltpu.roll(third, 4, 0)], axis=0)
        )
    lam_rows = [rows[i] + rows[i + 4] for i in range(4)]
    main = [halves[12], halves[13], halves[14], halves[15], None, halves[16]]
    first, second, third = (half[8:16] for half in main[:3])
    main[4] = jnp.concatenate(
        [jnp.where(sub[:, :128] < 4, pltpu.roll(first, 4, 0), second), pltpu.roll(third, 4, 0)], axis=0
    )
    wind_rows = []
    for index in range(6):
        spare = pltpu.roll(halves[2 * index + 1], 256 - WIDTH, 1)
        wind_rows.append(jnp.concatenate([main[index], jnp.where(lane < 2 * LEVELS - 128, spare, 0.0)], axis=1))
    return lam_rows, wind_rows


def force_body(recv_ref, table_ref, adjoint_ref, winds_ref, lam_ref, first_ref, second_ref, table_s):
    total = recv_ref.shape[0]
    nkernel = table_ref.shape[0]
    recv = recv_ref[...]
    wide = recv.astype(F32)
    pick = jnp.where((iota((8, WIDE), 1) == CODE_LANE), 1.0, 0.0).astype(BF16)
    code_line = lax.dot_general(pick, recv, (((1,), (1,)), ((), ())), preferred_element_type=F32)
    kernel_col = wide[:, KERNEL_LANE : KERNEL_LANE + 1]
    lane = iota((total, 3 * nkernel), 1)
    lane = (lane - jnp.where(lane >= nkernel, nkernel, 0) - jnp.where(lane >= 2 * nkernel, nkernel, 0)).astype(F32)
    onehot = jnp.where(kernel_col == lane, 1.0, 0.0).astype(BF16)
    table = table_ref[...]
    table_s[...] = jnp.zeros_like(table_s)
    high = table.astype(BF16)
    rest = table - high.astype(F32)
    middle = rest.astype(BF16)
    table_s[0:nkernel, :WIDTH] = high
    table_s[nkernel : 2 * nkernel, :WIDTH] = middle
    table_s[2 * nkernel :, :WIDTH] = (rest - middle.astype(F32)).astype(BF16)
    weights = jnp.dot(onehot, table_s[...], preferred_element_type=F32)
    weighted = wide * weights
    whigh = weighted.astype(BF16)
    wlow = (weighted - whigh.astype(F32)).astype(BF16)
    cell = (iota((ROWS * SUB, total), 0) + 1).astype(F32)
    scatter = jnp.where(cell == code_line[0:1, :], 1.0, 0.0).astype(BF16)
    force = jnp.dot(scatter, whigh, preferred_element_type=F32) + jnp.dot(
        scatter, wlow, preferred_element_type=F32
    )
    lam_ref[...] = force.reshape(ROWS, SUB, WIDE)
    lam_ref[:, :ROWS, :WIDTH] = lam_ref[:, :ROWS, :WIDTH] + adjoint_ref[...]
    made = []
    for lower in (False, True):
        start = 0 if lower else ROWS - HALO
        wind_rows = []
        for step in (1, 2, 3):
            depth = HALO - step
            begin = 0 if lower else ROWS - depth
            wind_rows += [winds_ref[4 - step, begin + i].astype(F32) for i in range(depth)]
        made.append(pack_strip([lam_ref[start + i] for i in range(HALO)], wind_rows))
    even = lax.rem(lax.axis_index("lat"), 2) == 0
    for index, (north, south) in enumerate(zip(*made, strict=True)):
        first_ref[index] = jnp.where(even, north, south).astype(BF16)
        second_ref[index] = jnp.where(even, south, north).astype(BF16)


WIND_FIRST = {1: 0, 2: 3, 3: 5}
EXT = ROWS + 2 * HALO


def ext_index(row):
    return row if row >= 0 else row + EXT


def wind_index(step, row):
    base = (0, 18, 34, 48)[step - 1]
    reach = HALO - step
    return base + (row if row >= 0 else row + ROWS + 2 * reach)


def edge_body(lam_ref, from_first, from_second, winds_ref, sibling_ref, cross_ref, lam_out, winds_out):
    even_lat = lax.rem(lax.axis_index("lat"), 2) == 0
    first = [from_first[i].astype(F32) for i in range(STRIP)]
    second = [from_second[i].astype(F32) for i in range(STRIP)]
    north_lam, north_winds = unpack_strip([jnp.where(even_lat, a, b) for a, b in zip(first, second, strict=True)])
    south_lam, south_winds = unpack_strip([jnp.where(even_lat, b, a) for a, b in zip(first, second, strict=True)])
    even = lax.rem(lax.axis_index("lon"), 2) == 0
    sub = iota((8, WIDE), 0)
    none = jnp.zeros((SUB, WIDE), F32)
    for row in range(-HALO, ROWS + HALO):
        own = 0 <= row < ROWS
        lam = lam_ref[row] if own else (south_lam[row + HALO] if row < 0 else north_lam[row - ROWS])
        lam_out[ext_index(row)] = lam
        wind = {}
        for step in (1, 2, 3, 4):
            reach = HALO - step
            if own:
                raw = winds_ref[4 - step, row]
                winds_out[wind_index(step, row)] = raw
                wind[step] = raw.astype(F32)
            elif -reach <= row < ROWS + reach:
                rows, at = (south_winds, row + reach) if row < 0 else (north_winds, row - ROWS)
                wind[step] = rows[WIND_FIRST[step] + at]
                winds_out[wind_index(step, row)] = wind[step].astype(BF16)
            else:
                wind[step] = none
        made = []
        for tile in (1, 0):
            cut = slice(8 * tile, 8 * tile + 8)
            high, low = split2(lam[cut])
            values = jnp.where(sub < 4, high, pltpu.roll(low, 4, 0))
            upper = pltpu.roll(wind[1][cut], 4, 0)
            if tile == 1:
                rest = jnp.where(sub >= 2, wind[2][cut], pltpu.roll(wind[3][cut], 6, 0))
            else:
                rest = jnp.where(sub < 2, wind[2][cut], pltpu.roll(wind[3][cut], 2, 0))
            made.append(jnp.concatenate([values, jnp.where(sub >= 4, upper, rest)], axis=0))
        to_east, to_west = made
        sibling_ref[ext_index(row)] = jnp.where(even, to_east, to_west).astype(BF16)
        cross_ref[ext_index(row)] = jnp.where(even, to_west, to_east).astype(BF16)


def pack_low(tile):
    lane = iota(tile.shape[:-1] + (128,), len(tile.shape) - 1)
    return jnp.where((lane >= 16) & (lane < 24), tile[..., 128:], tile[..., :128])


def assemble(refs, lam_s, wide_s, narrow):
    lam_ref, winds_ref, from_sibling, from_cross = refs
    even = lax.rem(lax.axis_index("lon"), 2) == 0
    sub = iota((8, 128 if narrow else WIDE), 0)
    lanes = 128 if narrow else WIDE
    keep = pack_low if narrow else (lambda tile: tile)
    for row in range(-HALO, ROWS + HALO):
        at = ext_index(row)
        lam = keep(lam_ref[at])
        sibling = from_sibling[at].astype(F32)
        cross = from_cross[at].astype(F32)
        east = jnp.where(even, sibling, cross)
        west = jnp.where(even, cross, sibling)
        east_lam, west_lam = keep(east[0:8]), keep(west[0:8])
        lam_s[at, 0:8] = lam[0:8]
        lam_s[at, 8:16] = jnp.where(sub < 4, lam[8:16], east_lam + pltpu.roll(east_lam, 4, 0))
        lam_s[at, 16:24] = west_lam + pltpu.roll(west_lam, 4, 0)
        for step in range(1, 5):
            reach = HALO - step
            if not -reach <= row < ROWS + reach:
                continue
            place = wind_index(step, row)
            wind = winds_ref[place, :, :lanes].astype(F32)
            ew, ww = east[8:16, :lanes], west[8:16, :lanes]
            if step == 2:
                ew, ww = pltpu.roll(ew, 4, 0), pltpu.roll(ww, 4, 0)
            if step == 3:
                ew, ww = pltpu.roll(ew, 2, 0), pltpu.roll(ww, 6, 0)
            wide_s[place, 0:16] = jnp.concatenate(
                [wind[0:8], jnp.where(sub < 4, wind[8:16], ew)], axis=0
            ).astype(BF16)
            wide_s[place, 16:24] = ww.astype(BF16)


def wind_spread(narrow):
    lanes = 128 if narrow else WIDE
    source = iota((lanes, 2 * lanes), 0)
    lane = iota((lanes, 2 * lanes), 1)
    second = lane >= lanes
    lane = jnp.where(second, lane - lanes, lane)
    if narrow:
        level = jnp.where(lane >= LEVELS, lane - LEVELS, jnp.where(lane >= 16, lane - 16, lane))
        used = level < 8
    else:
        level = lane - jnp.where(lane >= LEVELS, LEVELS, 0) - jnp.where(lane >= 2 * LEVELS, LEVELS, 0)
        used = lane < WIDTH
    match = (source == level + jnp.where(second, LEVELS, 0)) & used
    return jnp.where(match, 0.5, 0.0).astype(BF16)


def advance(lam_a, lam_b, wide_s, coef_s, narrow, emit):
    lat = lax.axis_index("lat")
    has_south = jnp.where(lat > 0, 1.0, 0.0).astype(F32)
    has_north = jnp.where(lat < lax.axis_size("lat") - 1, 1.0, 0.0).astype(F32)
    cols = SUB + 8
    lanes = 128 if narrow else WIDE
    spread = wind_spread(narrow)
    lane = iota((cols, lanes), 1)
    if narrow:
        top = None
        bottom = (lane == 0) | (lane == 16) | (lane == LEVELS)
    else:
        top = (lane == LEVELS - 1) | (lane == 2 * LEVELS - 1) | (lane == 3 * LEVELS - 1)
        bottom = (lane == 0) | (lane == LEVELS) | (lane == 2 * LEVELS)
    now, later = lam_a, lam_b
    for step in range(1, 5):
        reach = HALO - step
        count = ROWS + 2 * reach
        base = wind_index(step, 0)
        lhs = wide_s[base : base + count].reshape(count * cols, lanes)
        coef_s[:count] = jnp.dot(lhs, spread, preferred_element_type=F32).reshape(count, cols, 2 * lanes)
        for row in range(-reach, ROWS + reach):
            at = ext_index(row)
            mid = now[at]
            north = now[ext_index(row + 1)]
            south = now[ext_index(row - 1)]
            east = pltpu.roll(mid, cols - 1, 0)
            west = pltpu.roll(mid, 1, 0)
            upper = pltpu.roll(mid, lanes - 1, 1)
            if top is not None:
                upper = jnp.where(top, mid, upper)
            lower = jnp.where(bottom, mid, pltpu.roll(mid, 1, 1))
            place = wind_index(step, row) - base
            u = coef_s[place, :, :lanes]
            v = coef_s[place, :, lanes:]
            new = (
                CENTER * mid
                + u * (east - west)
                + v * (north - south)
                + HORIZ_MIX * ((east + west) + (north + south))
                + VERT_MIX * (upper + lower)
            )
            if row < 0:
                new = new * has_south
            if row >= ROWS:
                new = new * has_north
            if step < 4:
                later[at] = new
            if 0 <= row < ROWS:
                emit(step, row, new)
        now, later = later, now


def surface_body(
    lam_ref, winds_ref, from_sibling, from_cross, out_ref, lam_a, lam_b, wide_s, coef_s, acc_s
):
    refs = (lam_ref, winds_ref, from_sibling, from_cross)
    assemble(refs, lam_a, wide_s, True)

    def emit(step, row, value):
        acc_s[row] = value[:SUB] if step == 1 else acc_s[row] + value[:SUB]

    advance(lam_a, lam_b, wide_s, coef_s, True, emit)
    lane = iota((SUB, 128), 1)
    surface = jnp.zeros((SUB, 128), F32)
    for row in range(ROWS):
        held = acc_s[row]
        for species, source in enumerate((0, LEVELS, 16)):
            at = row * SPECIES + species
            surface = jnp.where(lane == at, pltpu.roll(held, (at - source) % 128, 1), surface)
    surface = jnp.where(iota((SUB, 128), 0) < ROWS, surface, 0.0)
    block = jnp.where(lane[:8] < 64, surface[0:8], pltpu.roll(surface[8:16], 64, 1))
    both = jnp.concatenate([block, block], axis=0).astype(BF16)
    for pair in range(out_ref.shape[0] // SUB):
        out_ref[SUB * pair : SUB * pair + SUB] = both


def steps_body(lam_ref, winds_ref, from_sibling, from_cross, field_ref, lam_a, lam_b, wide_s, coef_s):
    refs = (lam_ref, winds_ref, from_sibling, from_cross)
    assemble(refs, lam_a, wide_s, False)

    def emit(step, row, value):
        if step == 4:
            field_ref[row] = value[:ROWS, :WIDTH]

    advance(lam_a, lam_b, wide_s, coef_s, False, emit)


def correlation_body(correlation_ref, out_ref):
    total = correlation_ref.shape[1]
    length = total // ROWS * 8
    source = iota((total, length), 0)
    block = iota((total, length), 1) >> 3
    place = iota((total, length), 1) & 7
    first = source == block * ROWS + place
    second = (source == block * ROWS + 8 + place) & (place < 4)
    for index, match in enumerate((first, second)):
        pick = jnp.where(match, 1.0, 0.0).astype(BF16)
        part = jnp.dot(correlation_ref[...], pick, preferred_element_type=F32)
        part = jnp.concatenate([part, jnp.zeros((SUB - ROWS, length), F32)], axis=0)
        out_ref[SUB * index : SUB * index + SUB] = part.astype(BF16)


def gradient_body(surface_ref, correlation_ref, out_ref):
    both = jnp.dot(correlation_ref[...], surface_ref[...], preferred_element_type=F32)
    sums = both[:SUB] + pltpu.roll(both[SUB:], 64, 1)
    result = jnp.transpose(sums)
    for row in range(ROWS):
        out_ref[row] = result[SPECIES * row : SPECIES * row + SPECIES, :ROWS]


def per_device(
    adjoint_in, stored_winds, innovations, columns, kernel_ids, counts, offsets, kernel_table, correlation
):
    lon_count = lax.axis_size("lon")
    lat_count = lax.axis_size("lat")
    shape = jax.ShapeDtypeStruct
    held = innovations.shape[2]
    sent = vmem_call(
        route_body,
        shape((lon_count * CAP, WIDE), BF16),
        [
            pltpu.VMEM((1, lon_count), jnp.int32),
            pltpu.VMEM((1, lon_count), jnp.int32),
            pltpu.VMEM((1, held), jnp.int32),
            pltpu.VMEM((1, held), jnp.int32),
            pltpu.VMEM((WIDTH, held), BF16),
            pltpu.SemaphoreType.DMA((5,)),
        ],
        name="route",
        limit=63 * 1000 * 1000,
        in_specs=[pl.BlockSpec(memory_space=pltpu.HBM)] * 5,
    )(counts, offsets, columns, kernel_ids, jnp.swapaxes(innovations, 2, 3))
    recv = lax.all_to_all(sent, "lon", split_axis=0, concat_axis=0, tiled=True)
    winds = vmem_call(pad_winds_body, shape((4, ROWS, SUB, WIDE), BF16), name="pad_winds")(stored_winds)
    turned = vmem_call(correlation_body, shape((2 * SUB, lon_count * 8), BF16), name="correlation")(correlation.T)
    strip = shape((STRIP, SUB, 128), BF16)
    lam, first, second = vmem_call(
        force_body,
        (shape((ROWS, SUB, WIDE), F32), strip, strip),
        [pltpu.VMEM((3 * kernel_table.shape[0], WIDE), BF16)],
        name="force",
    )(recv, kernel_table, adjoint_in, winds)
    partner = [(i, i ^ 1) for i in range(lat_count) if i ^ 1 < lat_count]
    other = [(i, i + 1 if i % 2 else i - 1) for i in range(1, lat_count - 1 + lat_count % 2)]
    from_first = lax.ppermute(first, "lat", partner)
    from_second = lax.ppermute(second, "lat", other)
    edge = shape((EXT, SUB, WIDE), BF16)
    to_sibling, to_cross, lam_ext, winds_ext = vmem_call(
        edge_body, (edge, edge, shape((EXT, SUB, WIDE), F32), shape((60, SUB, WIDE), BF16)), name="edge"
    )(lam, from_first, from_second, winds)
    from_cross = lax.ppermute(
        to_cross, "lon", [(i, (i + (1 if i % 2 else -1)) % lon_count) for i in range(lon_count)]
    )
    from_sibling = lax.ppermute(to_sibling, "lon", [(i, i ^ 1) for i in range(lon_count)])
    cols = SUB + 8

    def scratch(lanes):
        return [
            pltpu.VMEM((EXT, cols, lanes), F32),
            pltpu.VMEM((EXT, cols, lanes), F32),
            pltpu.VMEM((60, cols, lanes), BF16),
            pltpu.VMEM((EXT, cols, 2 * lanes), F32),
        ]

    state = (lam_ext, winds_ext, from_sibling, from_cross)
    surface = vmem_call(
        surface_body,
        shape((lon_count * 8, 128), BF16),
        scratch(128) + [pltpu.VMEM((ROWS, SUB, 128), F32)],
        name="surface",
    )(*state)
    gathered = lax.all_to_all(surface, "lon", split_axis=0, concat_axis=0, tiled=True)
    field = vmem_call(steps_body, shape((ROWS, ROWS, WIDTH), F32), scratch(WIDE), name="steps")(*state)
    gradient = vmem_call(gradient_body, shape((ROWS, SPECIES, ROWS), F32), name="gradient")(gathered, turned)
    return field, gradient


def solution(mesh):
    return jax.shard_map(
        per_device,
        mesh=mesh,
        in_specs=(
            P("lat", "lon", None),
            P(None, "lat", "lon", None),
            P("lat", "lon", None, None),
            P("lat", "lon", None),
            P("lat", "lon", None),
            P("lat", "lon", None),
            P("lat", "lon", None),
            P(),
            P(None, "lon"),
        ),
        out_specs=(P("lat", "lon", None), P("lat", None, "lon")),
        check_vma=False,
    )
```

time: 80.8 us -> 71.1 us (0.88)
  waiting for transfers between devices: 33.7 us -> 24.4 us
  Pallas kernels: 4.7 us -> 7.34 us
  starting transfers between devices: 39.9 us -> 37.8 us
  local copies, waits for them, and re-layouts: 1.25 us -> 0.07 us
    ppermute x4, waiting for transfers between devices: 16.7 us -> 10.7 us  [the longest x1 6.81 us: per_device(): lax.ppermute(to_cross, 'lon', [(i, (i + (1 if i % 2 else -1)) % lon_count...]
    all_to_all x1, waiting for transfers between devices: 8.49 us -> 5.16 us  [per_device(): lax.all_to_all(surface, 'lon', split_axis=0, concat_axis=0, tiled=True)]
    all_to_all x1, starting transfers between devices: 5.43 us -> 3.75 us  [per_device(): lax.all_to_all(surface, 'lon', split_axis=0, concat_axis=0, tiled=True)]
    pallas_call x3 -> x4, Pallas kernels: 2.39 us -> 3.92 us  [the longest x1 2.06 us: per_device(): vmem_call(steps_body, shape((ROWS, ROWS, WIDTH), F32), scratch(WIDE), nam...]
    unnamed x19 -> x9, local copies, waits for them, and re-layouts: 1.25 us -> 0.07 us
    pallas_call x1, Pallas kernels: 0.95 us -> 1.98 us  [per_device(): vmem_call(route_body, shape((lon_count * CAP, WIDE), BF16), [pltpu.VMEM((...]
  transfers between devices with their start and end apart: 6 -> 6, of which waited for: 6 -> 4; matrix products, arithmetic and copies ran while one was open for 0% -> 0% of each run, Pallas kernels for 0% -> 3%
where the time goes in v2:
time: 71.1 us; the launch traced here: 70.4 us
  starting transfers between devices  37.8 us (53%)
  waiting for transfers between devices  24.4 us (34%)
  Pallas kernels  7.34 us (10%)
  between operations  0.77 us (1%)
    ppermute x1, starting transfers between devices, per_device(): from_second = lax.ppermute(second, 'lat', other)  15.8 us
    all_to_all x1, starting transfers between devices, per_device(): recv = lax.all_to_all(sent, 'lon', split_axis=0, concat_axis=0, tiled=True)  9.19 us
    all_to_all x1, waiting for transfers between devices, per_device(): recv = lax.all_to_all(sent, 'lon', split_axis=0, concat_axis=0, tiled=True)  8.54 us
    ppermute x1, waiting for transfers between devices, per_device(): lax.ppermute(to_cross, 'lon', [(i, (i + (1 if i % 2 else -1)) % lon_count...  6.81 us
    ppermute x1, starting transfers between devices, per_device(): from_first = lax.ppermute(first, 'lat', partner)  5.19 us
    all_to_all x1, waiting for transfers between devices, per_device(): lax.all_to_all(surface, 'lon', split_axis=0, concat_axis=0, tiled=True)  5.16 us
    ppermute x1, waiting for transfers between devices, per_device(): from_second = lax.ppermute(second, 'lat', other)  3.93 us
    all_to_all x1, starting transfers between devices, per_device(): lax.all_to_all(surface, 'lon', split_axis=0, concat_axis=0, tiled=True)  3.75 us
  transfers between devices with their start and end apart: 6, of which 4 were waited for; matrix products, arithmetic and copies ran while one was open for 0% of the time, Pallas kernels for 3%

profile of v2, /device:TPU:14, one launch (start us, length us, event | category | flops | bytes accessed | tf_op | source)
XLA Modules:
  0.0 70.4 jit_solution(11825413808608223281)
XLA Ops:
  0.6 0.0 copy-start.3
  0.6 2.0 %route.1 = bf16[256,256]{1,0:T(8,128)(2,1)} custom-call(s32[1,1,32]{2,1,0:T(1,128)} %counts_hbm.1, s32[1,1,32]{2,1,0:T(1,128)} %offsets_hbm.1, s32[1,1,256]{2,1,0:T(1,128)} %columns_hbm.1, s32[1,1,256]{2,1,0:T(1,128)} %kernels_hbm.1, bf16[1,1,216,256]{3,2,1,0:T(8,128)(2,1)} %bitcast.10), custom_call_target="tpu_custom_call" | custom-call | tf_op jit(solution)/shard_map/route/pallas_call | solution.py:425
  2.6 9.2 %all-to-all-start = ((bf16[32,8,256]{2,1,0:T(8,128)(2,1)}), bf16[32,8,256]{2,1,0:T(8,128)(2,1)S(1)}, u32[]{:S(2)}, u32[]{:S(2)}) async-start(bf16[32,8,256]{2,1,0:T(8,128)(2,1)} %bitcast.9), calls=%async_computation | async-start | bytes 262144 | tf_op jit(solution)/shard_map/all_to_all | solution.py:440
  11.8 0.0 copy-done.3
  11.9 0.0 copy-start
  11.9 0.0 copy-start.1
  11.9 0.1 pad_winds.1.winds_ref
  12.0 8.5 %all-to-all-done = bf16[32,8,256]{2,1,0:T(8,128)(2,1)S(1)} async-done(((bf16[32,8,256]{2,1,0:T(8,128)(2,1)}), bf16[32,8,256]{2,1,0:T(8,128)(2,1)S(1)}, u32[]{:S(2)}, u32[]{:S(2)}) %all-to-all-start) | async-done | bytes 131104 | tf_op jit(solution)/shard_map/all_to_all | solution.py:440
  20.5 0.0 copy-done
  20.5 0.0 copy-done.1
  20.5 0.5 force.1
  21.0 5.2 %collective-permute-start = (bf16[17,16,128]{2,1,0:T(8,128)(2,1)S(1)}, bf16[17,16,128]{2,1,0:T(8,128)(2,1)S(1)}, u32[]{:S(2)}, u32[]{:S(2)}) collective-permute-start(bf16[17,16,128]{2,1,0:T(8,128)(2,1)S(1)} %get-tuple-element.10), channel_id=1, source_target_pairs={{0,1},{1,0},{2,3},{3,2},{4,5},{5,4},{6,7},{7,6},{8,9},{9,8},{10,11... | collective-permute-start | bytes 208904 | tf_op jit(solution)/shard_map/ppermute | solution.py:452
  26.2 15.8 %collective-permute-start.1 = (bf16[17,16,128]{2,1,0:T(8,128)(2,1)S(1)}, bf16[17,16,128]{2,1,0:T(8,128)(2,1)S(1)}, u32[]{:S(2)}, u32[]{:S(2)}) collective-permute-start(bf16[17,16,128]{2,1,0:T(8,128)(2,1)S(1)} %get-tuple-element.11), channel_id=1, source_target_pairs={{1,2},{2,1},{3,4},{4,3},{5,6},{6,5},{7,8},{8,7},{9,10},{10,9},{11,... | collective-permute-start | bytes 208904 | tf_op jit(solution)/shard_map/ppermute | solution.py:453
  42.0 0.0 collective-permute-done.from_first
  42.0 3.9 %collective-permute-done.1.from_second = bf16[17,16,128]{2,1,0:T(8,128)(2,1)S(1)} collective-permute-done((bf16[17,16,128]{2,1,0:T(8,128)(2,1)S(1)}, bf16[17,16,128]{2,1,0:T(8,128)(2,1)S(1)}, u32[]{:S(2)}, u32[]{:S(2)}) %collective-permute-start.1) | collective-permute-done | bytes 69664 | tf_op jit(solution)/shard_map/ppermute | solution.py:453
  46.0 0.2 edge.1
  46.2 1.9 %collective-permute-start.2 = (bf16[20,16,256]{2,1,0:T(8,128)(2,1)S(1)}, bf16[20,16,256]{2,1,0:T(8,128)(2,1)S(1)}, u32[]{:S(2)}, u32[]{:S(2)}) collective-permute-start(bf16[20,16,256]{2,1,0:T(8,128)(2,1)S(1)} %get-tuple-element.14), channel_id=1, source_target_pairs={{0,32},{32,0},{64,96},{96,64},{128,160},{160,128},{192,224},{224,1... | collective-permute-start | bytes 491528 | tf_op jit(solution)/shard_map/ppermute | solution.py:461
  48.1 1.9 %collective-permute-start.3 = (bf16[20,16,256]{2,1,0:T(8,128)(2,1)S(1)}, bf16[20,16,256]{2,1,0:T(8,128)(2,1)S(1)}, u32[]{:S(2)}, u32[]{:S(2)}) collective-permute-start(bf16[20,16,256]{2,1,0:T(8,128)(2,1)S(1)} %get-tuple-element.15), channel_id=1, source_target_pairs={{0,992},{32,64},{64,32},{96,128},{128,96},{160,192},{192,160},{224... | collective-permute-start | bytes 491528 | tf_op jit(solution)/shard_map/ppermute | solution.py:458
  50.0 0.0 collective-permute-done.2.from_sibling
  50.0 6.8 %collective-permute-done.3.from_cross = bf16[20,16,256]{2,1,0:T(8,128)(2,1)S(1)} collective-permute-done((bf16[20,16,256]{2,1,0:T(8,128)(2,1)S(1)}, bf16[20,16,256]{2,1,0:T(8,128)(2,1)S(1)}, u32[]{:S(2)}, u32[]{:S(2)}) %collective-permute-start.3) | collective-permute-done | bytes 163872 | tf_op jit(solution)/shard_map/ppermute | solution.py:458
  56.9 1.4 %surface.1 = bf16[256,128]{1,0:T(8,128)(2,1)} custom-call(f32[20,16,256]{2,1,0:T(8,128)S(1)} %get-tuple-element.12.lam_ref, bf16[60,16,256]{2,1,0:T(8,128)(2,1)S(1)} %get-tuple-element.13.winds_ref, bf16[20,16,256]{2,1,0:T(8,128)(2,1)S(1)} %collective-permute-done.2.from_sibling, bf16[20,16,256]{2,1,0:T(8,128)(2,1)S(1)} %collective-permute-done.3.from_cross), custom_call_target="tpu_custom_call" | custom-call | tf_op jit(solution)/shard_map/surface/pallas_call | solution.py:473
  58.3 0.0 copy-start.2
  58.3 3.8 %all-to-all-start.1 = ((bf16[32,8,128]{2,1,0:T(8,128)(2,1)}), bf16[32,8,128]{2,1,0:T(8,128)(2,1)S(1)}, u32[]{:S(2)}, u32[]{:S(2)}) async-start(bf16[32,8,128]{2,1,0:T(8,128)(2,1)} %bitcast.3), calls=%async_computation.1 | async-start | bytes 131072 | tf_op jit(solution)/shard_map/all_to_all | solution.py:479
  62.1 0.0 copy-done.2
  62.1 0.2 correlation.1.correlation_ref
  62.3 2.1 %steps.1 = f32[12,12,216]{2,1,0:T(8,128)} custom-call(f32[20,16,256]{2,1,0:T(8,128)S(1)} %get-tuple-element.12.lam_ref, bf16[60,16,256]{2,1,0:T(8,128)(2,1)S(1)} %get-tuple-element.13.winds_ref, bf16[20,16,256]{2,1,0:T(8,128)(2,1)S(1)} %collective-permute-done.2.from_sibling, bf16[20,16,256]{2,1,0:T(8,128)(2,1)S(1)} %collective-permute-done.3.from_cross), custom_call_target="tpu_custom_call" | custom-call | tf_op jit(solution)/shard_map/steps/pallas_call | solution.py:480
  64.3 5.2 %all-to-all-done.1 = bf16[32,8,128]{2,1,0:T(8,128)(2,1)S(1)} async-done(((bf16[32,8,128]{2,1,0:T(8,128)(2,1)}), bf16[32,8,128]{2,1,0:T(8,128)(2,1)S(1)}, u32[]{:S(2)}, u32[]{:S(2)}) %all-to-all-start.1) | async-done | bytes 65568 | tf_op jit(solution)/shard_map/all_to_all | solution.py:479
  69.5 0.9 %gradient.1 = f32[12,3,12]{2,1,0:T(4,128)} custom-call(bf16[256,128]{1,0:T(8,128)(2,1)S(1)} %bitcast.7, bf16[32,256]{1,0:T(8,128)(2,1)S(1)} %correlation.1.correlation_ref), custom_call_target="tpu_custom_call" | custom-call | tf_op jit(solution)/shard_map/gradient/pallas_call | solution.py:481
  (1 shorter events, 0.0 us)
Async XLA Ops:
  0.6 11.2 %copy-start.3 = (bf16[4,12,12,144]{3,0,2,1:T(4,128)(2,1)S(1)}, bf16[4,12,12,144]{3,0,2,1:T(4,128)(2,1)}, u32[]{:S(2)}) copy-start(bf16[4,12,12,144]{3,0,2,1:T(4,128)(2,1)} %param.10) | copy-start | bytes 497668
  2.6 17.9 %all-to-all-start = ((bf16[32,8,256]{2,1,0:T(8,128)(2,1)}), bf16[32,8,256]{2,1,0:T(8,128)(2,1)S(1)}, u32[]{:S(2)}, u32[]{:S(2)}) async-start(bf16[32,8,256]{2,1,0:T(8,128)(2,1)} %bitcast.9), calls=%async_computation | async-start | bytes 262144 | tf_op jit(solution)/shard_map/all_to_all | solution.py:440
  11.9 8.6 %copy-start = (f32[12,12,216]{2,1,0:T(8,128)S(1)}, f32[12,12,216]{2,1,0:T(8,128)}, u32[]{:S(2)}) copy-start(f32[12,12,216]{2,1,0:T(8,128)} %adjoint_ref.1) | copy-start | bytes 373252
  11.9 8.6 %copy-start.1 = (f32[64,216]{1,0:T(8,128)S(1)}, f32[64,216]{1,0:T(8,128)}, u32[]{:S(2)}) copy-start(f32[64,216]{1,0:T(8,128)} %table_ref.1) | copy-start | bytes 165892
  21.0 21.0 %collective-permute-start = (bf16[17,16,128]{2,1,0:T(8,128)(2,1)S(1)}, bf16[17,16,128]{2,1,0:T(8,128)(2,1)S(1)}, u32[]{:S(2)}, u32[]{:S(2)}) collective-permute-start(bf16[17,16,128]{2,1,0:T(8,128)(2,1)S(1)} %get-tuple-element.10), channel_id=1, source_target_pairs={{0,1},{1,0},{2,3},{3,2},{4,5},{5,4},{6,7},{7,6},{8,9},{9,8},{10,11... | collective-permute-start | bytes 208904 | tf_op jit(solution)/shard_map/ppermute | solution.py:452
  26.2 19.7 %collective-permute-start.1 = (bf16[17,16,128]{2,1,0:T(8,128)(2,1)S(1)}, bf16[17,16,128]{2,1,0:T(8,128)(2,1)S(1)}, u32[]{:S(2)}, u32[]{:S(2)}) collective-permute-start(bf16[17,16,128]{2,1,0:T(8,128)(2,1)S(1)} %get-tuple-element.11), channel_id=1, source_target_pairs={{1,2},{2,1},{3,4},{4,3},{5,6},{6,5},{7,8},{8,7},{9,10},{10,9},{11,... | collective-permute-start | bytes 208904 | tf_op jit(solution)/shard_map/ppermute | solution.py:453
  46.2 3.9 %collective-permute-start.2 = (bf16[20,16,256]{2,1,0:T(8,128)(2,1)S(1)}, bf16[20,16,256]{2,1,0:T(8,128)(2,1)S(1)}, u32[]{:S(2)}, u32[]{:S(2)}) collective-permute-start(bf16[20,16,256]{2,1,0:T(8,128)(2,1)S(1)} %get-tuple-element.14), channel_id=1, source_target_pairs={{0,32},{32,0},{64,96},{96,64},{128,160},{160,128},{192,224},{224,1... | collective-permute-start | bytes 491528 | tf_op jit(solution)/shard_map/ppermute | solution.py:461
  48.1 8.7 %collective-permute-start.3 = (bf16[20,16,256]{2,1,0:T(8,128)(2,1)S(1)}, bf16[20,16,256]{2,1,0:T(8,128)(2,1)S(1)}, u32[]{:S(2)}, u32[]{:S(2)}) collective-permute-start(bf16[20,16,256]{2,1,0:T(8,128)(2,1)S(1)} %get-tuple-element.15), channel_id=1, source_target_pairs={{0,992},{32,64},{64,32},{96,128},{128,96},{160,192},{192,160},{224... | collective-permute-start | bytes 491528 | tf_op jit(solution)/shard_map/ppermute | solution.py:458
  58.3 3.8 %copy-start.2 = (bf16[384,12]{0,1:T(8,128)(2,1)S(1)}, bf16[384,12]{0,1:T(8,128)(2,1)}, u32[]{:S(2)}) copy-start(bf16[384,12]{0,1:T(8,128)(2,1)} %param.17) | copy-start | bytes 27652
  58.3 11.2 %all-to-all-start.1 = ((bf16[32,8,128]{2,1,0:T(8,128)(2,1)}), bf16[32,8,128]{2,1,0:T(8,128)(2,1)S(1)}, u32[]{:S(2)}, u32[]{:S(2)}) async-start(bf16[32,8,128]{2,1,0:T(8,128)(2,1)} %bitcast.3), calls=%async_computation.1 | async-start | bytes 131072 | tf_op jit(solution)/shard_map/all_to_all | solution.py:479

commit v3 on v2

--- a/solution.py
+++ b/solution.py
@@ -38,11 +38,6 @@
         compiler_params=pltpu.CompilerParams(vmem_limit_bytes=limit),
         **specs,
     )
-
-
-def split2(value):
-    high = value.astype(BF16).astype(F32)
-    return high, (value - high).astype(BF16).astype(F32)
 
 
 def route_body(
@@ -94,7 +89,8 @@
     out_ref[:, :, :ROWS, : 2 * LEVELS] = winds_ref[...]
 
 
-STRIP = 17
+STRIP = 11
+SPARE = (WIDTH - 128, WIDTH - 112)
 
 
 def pieces(row):
@@ -107,48 +103,40 @@
 
 
 def pack_strip(lam_rows, wind_rows):
-    parts = [split2(row) for row in lam_rows]
-    rows = [high for high, _ in parts] + [low for _, low in parts]
-    extra = pieces(rows[6]) + pieces(rows[7])
+    extra = pieces(lam_rows[3])
     lane = iota((SUB, 128), 1)
     halves = []
-    for index in range(6):
-        packed = with_piece(rows[index], extra[index])
-        spare = pltpu.roll(wind_rows[index][:, 128:], WIDTH - 128, 1)
-        halves += [packed[:, :128], jnp.where(lane < WIDTH - 128, packed[:, 128:], spare)]
+    for index in range(3):
+        packed = with_piece(lam_rows[index], extra[index])
+        one, two = (pltpu.roll(wind_rows[index + 3 * i][:, 128:], SPARE[i], 1) for i in range(2))
+        halves += [
+            packed[:, :128],
+            jnp.where(lane < SPARE[0], packed[:, 128:], jnp.where(lane < SPARE[1], one, two)),
+        ]
     main = [row[:, :128] for row in wind_rows]
     extra = pieces(main[4])
     halves += [with_piece(main[index], extra[index]) for index in range(3)] + [main[3], main[5]]
     return halves
 
 
+def rejoin(tiles):
+    first, second, third = (tile[8:16] for tile in tiles)
+    sub = iota(first.shape, 0)
+    return jnp.concatenate([jnp.where(sub < 4, pltpu.roll(first, 4, 0), second), pltpu.roll(third, 4, 0)], axis=0)
+
+
 def unpack_strip(halves):
-    lane = iota((SUB, 128), 1)
-    sub = iota((8, WIDE), 0)
-    tiles = [
-        jnp.concatenate([halves[2 * i], jnp.where(lane < WIDTH - 128, halves[2 * i + 1], 0.0)], axis=1)
-        for i in range(6)
-    ]
-    rows = list(tiles)
-    for index in (0, 3):
-        first, second, third = (tile[8:16] for tile in tiles[index : index + 3])
-        rows.append(
-            jnp.concatenate([jnp.where(sub < 4, pltpu.roll(first, 4, 0), second), pltpu.roll(third, 4, 0)], axis=0)
-        )
-    lam_rows = [rows[i] + rows[i + 4] for i in range(4)]
-    main = [halves[12], halves[13], halves[14], halves[15], None, halves[16]]
-    first, second, third = (half[8:16] for half in main[:3])
-    main[4] = jnp.concatenate(
-        [jnp.where(sub[:, :128] < 4, pltpu.roll(first, 4, 0), second), pltpu.roll(third, 4, 0)], axis=0
-    )
+    tiles = [jnp.concatenate(halves[2 * i : 2 * i + 2], axis=1) for i in range(3)]
+    lam_rows = tiles + [rejoin(tiles)]
+    main = halves[6:10] + [rejoin(halves[6:9]), halves[10]]
     wind_rows = []
     for index in range(6):
-        spare = pltpu.roll(halves[2 * index + 1], 256 - WIDTH, 1)
-        wind_rows.append(jnp.concatenate([main[index], jnp.where(lane < 2 * LEVELS - 128, spare, 0.0)], axis=1))
+        last = pltpu.roll(halves[2 * (index % 3) + 1], 128 - SPARE[index // 3], 1)
+        wind_rows.append(jnp.concatenate([main[index], last], axis=1))
     return lam_rows, wind_rows
 
 
-def force_body(recv_ref, table_ref, adjoint_ref, winds_ref, lam_ref, first_ref, second_ref, table_s):
+def force_body(recv_ref, table_ref, adjoint_ref, winds_ref, lam_ref, north_ref, south_ref, table_s):
     total = recv_ref.shape[0]
     nkernel = table_ref.shape[0]
     recv = recv_ref[...]
@@ -178,19 +166,15 @@
     )
     lam_ref[...] = force.reshape(ROWS, SUB, WIDE)
     lam_ref[:, :ROWS, :WIDTH] = lam_ref[:, :ROWS, :WIDTH] + adjoint_ref[...]
-    made = []
-    for lower in (False, True):
+    for lower, strip in ((False, north_ref), (True, south_ref)):
         start = 0 if lower else ROWS - HALO
         wind_rows = []
         for step in (1, 2, 3):
             depth = HALO - step
             begin = 0 if lower else ROWS - depth
             wind_rows += [winds_ref[4 - step, begin + i].astype(F32) for i in range(depth)]
-        made.append(pack_strip([lam_ref[start + i] for i in range(HALO)], wind_rows))
-    even = lax.rem(lax.axis_index("lat"), 2) == 0
-    for index, (north, south) in enumerate(zip(*made, strict=True)):
-        first_ref[index] = jnp.where(even, north, south).astype(BF16)
-        second_ref[index] = jnp.where(even, south, north).astype(BF16)
+        for index, half in enumerate(pack_strip([lam_ref[start + i] for i in range(HALO)], wind_rows)):
+            strip[index] = half.astype(BF16)
 
 
 WIND_FIRST = {1: 0, 2: 3, 3: 5}
@@ -207,16 +191,15 @@
     return base + (row if row >= 0 else row + ROWS + 2 * reach)
 
 
-def edge_body(lam_ref, from_first, from_second, winds_ref, sibling_ref, cross_ref, lam_out, winds_out):
-    even_lat = lax.rem(lax.axis_index("lat"), 2) == 0
-    first = [from_first[i].astype(F32) for i in range(STRIP)]
-    second = [from_second[i].astype(F32) for i in range(STRIP)]
-    north_lam, north_winds = unpack_strip([jnp.where(even_lat, a, b) for a, b in zip(first, second, strict=True)])
-    south_lam, south_winds = unpack_strip([jnp.where(even_lat, b, a) for a, b in zip(first, second, strict=True)])
+def edge_body(lam_ref, from_south, from_north, winds_ref, sibling_ref, cross_ref, lam_out, winds_out):
+    south_lam, south_winds = unpack_strip([from_south[i].astype(F32) for i in range(STRIP)])
+    north_lam, north_winds = unpack_strip([from_north[i].astype(F32) for i in range(STRIP)])
     even = lax.rem(lax.axis_index("lon"), 2) == 0
     sub = iota((8, WIDE), 0)
+    lane = iota((8, 128), 1)
     none = jnp.zeros((SUB, WIDE), F32)
-    for row in range(-HALO, ROWS + HALO):
+    held = {}
+    for row in sorted(range(-HALO, ROWS + HALO), key=ext_index):
         own = 0 <= row < ROWS
         lam = lam_ref[row] if own else (south_lam[row + HALO] if row < 0 else north_lam[row - ROWS])
         lam_out[ext_index(row)] = lam
@@ -236,17 +219,27 @@
         made = []
         for tile in (1, 0):
             cut = slice(8 * tile, 8 * tile + 8)
-            high, low = split2(lam[cut])
-            values = jnp.where(sub < 4, high, pltpu.roll(low, 4, 0))
             upper = pltpu.roll(wind[1][cut], 4, 0)
             if tile == 1:
                 rest = jnp.where(sub >= 2, wind[2][cut], pltpu.roll(wind[3][cut], 6, 0))
             else:
                 rest = jnp.where(sub < 2, wind[2][cut], pltpu.roll(wind[3][cut], 2, 0))
-            made.append(jnp.concatenate([values, jnp.where(sub >= 4, upper, rest)], axis=0))
-        to_east, to_west = made
-        sibling_ref[ext_index(row)] = jnp.where(even, to_east, to_west).astype(BF16)
-        cross_ref[ext_index(row)] = jnp.where(even, to_west, to_east).astype(BF16)
+            made.append((lam[cut], jnp.where(sub >= 4, upper, rest)))
+        if ext_index(row) % 2 == 0:
+            held = made
+            continue
+        strips = []
+        for (lam_a, wind_a), (lam_b, wind_b) in zip(held, made, strict=True):
+            both = jnp.where(sub < 4, lam_a, pltpu.roll(lam_b, 4, 0))
+            one = pltpu.roll(wind_a[:, 128:], SPARE[0], 1)
+            two = pltpu.roll(wind_b[:, 128:], SPARE[1], 1)
+            last = jnp.where(lane < SPARE[0], both[:, 128:], jnp.where(lane < SPARE[1], one, two))
+            upper = jnp.concatenate([both[:, :128], last], axis=1)
+            lower = jnp.concatenate([wind_a[:, :128], wind_b[:, :128]], axis=1)
+            strips.append(jnp.concatenate([upper, lower], axis=0))
+        to_east, to_west = strips
+        sibling_ref[ext_index(row) // 2] = jnp.where(even, to_east, to_west).astype(BF16)
+        cross_ref[ext_index(row) // 2] = jnp.where(even, to_west, to_east).astype(BF16)
 
 
 def pack_low(tile):
@@ -255,7 +248,7 @@
 
 
 def assemble(refs, lam_s, wide_s, narrow):
-    lam_ref, winds_ref, from_sibling, from_cross = refs
+    lam_ref, winds_ref, from_cross, from_sibling = refs
     even = lax.rem(lax.axis_index("lon"), 2) == 0
     sub = iota((8, 128 if narrow else WIDE), 0)
     lanes = 128 if narrow else WIDE
@@ -263,21 +256,30 @@
     for row in range(-HALO, ROWS + HALO):
         at = ext_index(row)
         lam = keep(lam_ref[at])
-        sibling = from_sibling[at].astype(F32)
-        cross = from_cross[at].astype(F32)
+        sibling = from_sibling[at // 2].astype(F32)
+        cross = from_cross[at // 2].astype(F32)
         east = jnp.where(even, sibling, cross)
         west = jnp.where(even, cross, sibling)
+        odd = at % 2
         east_lam, west_lam = keep(east[0:8]), keep(west[0:8])
+        if not odd:
+            east_lam, west_lam = pltpu.roll(east_lam, 4, 0), pltpu.roll(west_lam, 4, 0)
         lam_s[at, 0:8] = lam[0:8]
-        lam_s[at, 8:16] = jnp.where(sub < 4, lam[8:16], east_lam + pltpu.roll(east_lam, 4, 0))
-        lam_s[at, 16:24] = west_lam + pltpu.roll(west_lam, 4, 0)
+        lam_s[at, 8:16] = jnp.where(sub < 4, lam[8:16], east_lam)
+        lam_s[at, 16:24] = west_lam
+        east_wind, west_wind = (side[8:16, 128 * odd : 128 * odd + 128] for side in (east, west))
+        if not narrow:
+            east_wind, west_wind = (
+                jnp.concatenate([main, pltpu.roll(side[0:8, 128:], 128 - SPARE[odd], 1)], axis=1)
+                for main, side in ((east_wind, east), (west_wind, west))
+            )
         for step in range(1, 5):
             reach = HALO - step
             if not -reach <= row < ROWS + reach:
                 continue
             place = wind_index(step, row)
             wind = winds_ref[place, :, :lanes].astype(F32)
-            ew, ww = east[8:16, :lanes], west[8:16, :lanes]
+            ew, ww = east_wind, west_wind
             if step == 2:
                 ew, ww = pltpu.roll(ew, 4, 0), pltpu.roll(ww, 4, 0)
             if step == 3:
@@ -358,9 +360,9 @@
 
 
 def surface_body(
-    lam_ref, winds_ref, from_sibling, from_cross, out_ref, lam_a, lam_b, wide_s, coef_s, acc_s
+    lam_ref, winds_ref, from_cross, from_sibling, out_ref, lam_a, lam_b, wide_s, coef_s, acc_s
 ):
-    refs = (lam_ref, winds_ref, from_sibling, from_cross)
+    refs = (lam_ref, winds_ref, from_cross, from_sibling)
     assemble(refs, lam_a, wide_s, True)
 
     def emit(step, row, value):
@@ -381,8 +383,8 @@
         out_ref[SUB * pair : SUB * pair + SUB] = both
 
 
-def steps_body(lam_ref, winds_ref, from_sibling, from_cross, field_ref, lam_a, lam_b, wide_s, coef_s):
-    refs = (lam_ref, winds_ref, from_sibling, from_cross)
+def steps_body(lam_ref, winds_ref, from_cross, from_sibling, field_ref, lam_a, lam_b, wide_s, coef_s):
+    refs = (lam_ref, winds_ref, from_cross, from_sibling)
     assemble(refs, lam_a, wide_s, False)
 
     def emit(step, row, value):
@@ -441,20 +443,20 @@
     winds = vmem_call(pad_winds_body, shape((4, ROWS, SUB, WIDE), BF16), name="pad_winds")(stored_winds)
     turned = vmem_call(correlation_body, shape((2 * SUB, lon_count * 8), BF16), name="correlation")(correlation.T)
     strip = shape((STRIP, SUB, 128), BF16)
-    lam, first, second = vmem_call(
+    lam, north, south = vmem_call(
         force_body,
         (shape((ROWS, SUB, WIDE), F32), strip, strip),
         [pltpu.VMEM((3 * kernel_table.shape[0], WIDE), BF16)],
         name="force",
     )(recv, kernel_table, adjoint_in, winds)
-    partner = [(i, i ^ 1) for i in range(lat_count) if i ^ 1 < lat_count]
-    other = [(i, i + 1 if i % 2 else i - 1) for i in range(1, lat_count - 1 + lat_count % 2)]
-    from_first = lax.ppermute(first, "lat", partner)
-    from_second = lax.ppermute(second, "lat", other)
-    edge = shape((EXT, SUB, WIDE), BF16)
+    up = [(i, i + 1) for i in range(lat_count - 1)]
+    down = [(i + 1, i) for i in range(lat_count - 1)]
+    from_south = lax.ppermute(north, "lat", up)
+    from_north = lax.ppermute(south, "lat", down)
+    edge = shape((EXT // 2, SUB, WIDE), BF16)
     to_sibling, to_cross, lam_ext, winds_ext = vmem_call(
         edge_body, (edge, edge, shape((EXT, SUB, WIDE), F32), shape((60, SUB, WIDE), BF16)), name="edge"
-    )(lam, from_first, from_second, winds)
+    )(lam, from_south, from_north, winds)
     from_cross = lax.ppermute(
         to_cross, "lon", [(i, (i + (1 if i % 2 else -1)) % lon_count) for i in range(lon_count)]
     )
@@ -469,7 +471,7 @@
             pltpu.VMEM((EXT, cols, 2 * lanes), F32),
         ]
 
-    state = (lam_ext, winds_ext, from_sibling, from_cross)
+    state = (lam_ext, winds_ext, from_cross, from_sibling)
     surface = vmem_call(
         surface_body,
         shape((lon_count * 8, 128), BF16),

time: 71.1 us -> 66.8 us (0.940)
  waiting for transfers between devices: 24.4 us -> 18.2 us
  starting transfers between devices: 37.8 us -> 39.8 us
    ppermute x1, waiting for transfers between devices: 6.81 us -> 2.86 us  [per_device(): lax.ppermute(to_cross, 'lon', [(i, (i + (1 if i % 2 else -1)) % lon_count...]
    ppermute x2, waiting for transfers between devices: 3.93 us -> 1.69 us  [the longest x1 0.96 us: per_device(): from_south = lax.ppermute(north, 'lat', up)]
    ppermute x1, starting transfers between devices: 1.92 us -> 3.07 us  [per_device(): lax.ppermute(to_sibling, 'lon', [(i, i ^ 1) for i in range(lon_count)])]
    all_to_all x1, starting transfers between devices: 3.75 us -> 4.68 us  [per_device(): lax.all_to_all(surface, 'lon', split_axis=0, concat_axis=0, tiled=True)]
  transfers between devices with their start and end apart: 6 -> 6, of which waited for: 4 -> 5; matrix products, arithmetic and copies ran while one was open for 0% -> 0% of each run, Pallas kernels for 3% -> 4%
where the time goes in v3:
time: 66.8 us; the launch traced here: 66.2 us
  starting transfers between devices  39.8 us (60%)
  waiting for transfers between devices  18.2 us (27%)
  Pallas kernels  7.32 us (11%)
  between operations  0.76 us (1%)
    ppermute x1, starting transfers between devices, per_device(): from_north = lax.ppermute(south, 'lat', down)  15.8 us
    all_to_all x1, starting transfers between devices, per_device(): recv = lax.all_to_all(sent, 'lon', split_axis=0, concat_axis=0, tiled=True)  9.19 us
    all_to_all x1, waiting for transfers between devices, per_device(): recv = lax.all_to_all(sent, 'lon', split_axis=0, concat_axis=0, tiled=True)  8.54 us
    ppermute x1, starting transfers between devices, per_device(): from_south = lax.ppermute(north, 'lat', up)  5.19 us
    all_to_all x1, waiting for transfers between devices, per_device(): lax.all_to_all(surface, 'lon', split_axis=0, concat_axis=0, tiled=True)  5.09 us
    all_to_all x1, starting transfers between devices, per_device(): lax.all_to_all(surface, 'lon', split_axis=0, concat_axis=0, tiled=True)  4.68 us
    ppermute x1, starting transfers between devices, per_device(): lax.ppermute(to_sibling, 'lon', [(i, i ^ 1) for i in range(lon_count)])  3.07 us
    ppermute x1, waiting for transfers between devices, per_device(): lax.ppermute(to_cross, 'lon', [(i, (i + (1 if i % 2 else -1)) % lon_count...  2.86 us
  transfers between devices with their start and end apart: 6, of which 5 were waited for; matrix products, arithmetic and copies ran while one was open for 0% of the time, Pallas kernels for 4%

profile of v3, /device:TPU:14, one launch (start us, length us, event | category | flops | bytes accessed | tf_op | source)
XLA Modules:
  0.0 66.2 jit_solution(16770854957761410063)
XLA Ops:
  0.6 0.0 copy-start.3
  0.6 2.0 %route.1 = bf16[256,256]{1,0:T(8,128)(2,1)} custom-call(s32[1,1,32]{2,1,0:T(1,128)} %counts_hbm.1, s32[1,1,32]{2,1,0:T(1,128)} %offsets_hbm.1, s32[1,1,256]{2,1,0:T(1,128)} %columns_hbm.1, s32[1,1,256]{2,1,0:T(1,128)} %kernels_hbm.1, bf16[1,1,216,256]{3,2,1,0:T(8,128)(2,1)} %bitcast.10), custom_call_target="tpu_custom_call" | custom-call | tf_op jit(solution)/shard_map/route/pallas_call | solution.py:427
  2.6 9.2 %all-to-all-start = ((bf16[32,8,256]{2,1,0:T(8,128)(2,1)}), bf16[32,8,256]{2,1,0:T(8,128)(2,1)S(1)}, u32[]{:S(2)}, u32[]{:S(2)}) async-start(bf16[32,8,256]{2,1,0:T(8,128)(2,1)} %bitcast.9), calls=%async_computation | async-start | bytes 262144 | tf_op jit(solution)/shard_map/all_to_all | solution.py:442
  11.8 0.0 copy-done.3
  11.9 0.0 copy-start
  11.9 0.0 copy-start.1
  11.9 0.1 pad_winds.1.winds_ref
  12.0 8.5 %all-to-all-done = bf16[32,8,256]{2,1,0:T(8,128)(2,1)S(1)} async-done(((bf16[32,8,256]{2,1,0:T(8,128)(2,1)}), bf16[32,8,256]{2,1,0:T(8,128)(2,1)S(1)}, u32[]{:S(2)}, u32[]{:S(2)}) %all-to-all-start) | async-done | bytes 131104 | tf_op jit(solution)/shard_map/all_to_all | solution.py:442
  20.5 0.0 copy-done
  20.5 0.0 copy-done.1
  20.5 0.5 force.1
  21.0 5.2 %collective-permute-start = (bf16[11,16,128]{2,1,0:T(8,128)(2,1)S(1)}, bf16[11,16,128]{2,1,0:T(8,128)(2,1)S(1)}, u32[]{:S(2)}, u32[]{:S(2)}) collective-permute-start(bf16[11,16,128]{2,1,0:T(8,128)(2,1)S(1)} %get-tuple-element.10), channel_id=1, source_target_pairs={{0,1},{1,2},{2,3},{3,4},{4,5},{5,6},{6,7},{7,8},{8,9},{9,10},{10,1... | collective-permute-start | bytes 135176 | tf_op jit(solution)/shard_map/ppermute | solution.py:454
  26.2 15.8 %collective-permute-start.1 = (bf16[11,16,128]{2,1,0:T(8,128)(2,1)S(1)}, bf16[11,16,128]{2,1,0:T(8,128)(2,1)S(1)}, u32[]{:S(2)}, u32[]{:S(2)}) collective-permute-start(bf16[11,16,128]{2,1,0:T(8,128)(2,1)S(1)} %get-tuple-element.11), channel_id=1, source_target_pairs={{1,0},{2,1},{3,2},{4,3},{5,4},{6,5},{7,6},{8,7},{9,8},{10,9},{11,1... | collective-permute-start | bytes 135176 | tf_op jit(solution)/shard_map/ppermute | solution.py:455
  42.0 1.0 %collective-permute-done.from_south = bf16[11,16,128]{2,1,0:T(8,128)(2,1)S(1)} collective-permute-done((bf16[11,16,128]{2,1,0:T(8,128)(2,1)S(1)}, bf16[11,16,128]{2,1,0:T(8,128)(2,1)S(1)}, u32[]{:S(2)}, u32[]{:S(2)}) %collective-permute-start) | collective-permute-done | bytes 45088 | tf_op jit(solution)/shard_map/ppermute | solution.py:454
  43.0 0.7 %collective-permute-done.1.from_north = bf16[11,16,128]{2,1,0:T(8,128)(2,1)S(1)} collective-permute-done((bf16[11,16,128]{2,1,0:T(8,128)(2,1)S(1)}, bf16[11,16,128]{2,1,0:T(8,128)(2,1)S(1)}, u32[]{:S(2)}, u32[]{:S(2)}) %collective-permute-start.1) | collective-permute-done | bytes 45088 | tf_op jit(solution)/shard_map/ppermute | solution.py:455
  43.7 0.2 edge.1
  43.9 1.9 %collective-permute-start.2 = (bf16[10,16,256]{2,1,0:T(8,128)(2,1)S(1)}, bf16[10,16,256]{2,1,0:T(8,128)(2,1)S(1)}, u32[]{:S(2)}, u32[]{:S(2)}) collective-permute-start(bf16[10,16,256]{2,1,0:T(8,128)(2,1)S(1)} %get-tuple-element.14), channel_id=1, source_target_pairs={{0,992},{32,64},{64,32},{96,128},{128,96},{160,192},{192,160},{224... | collective-permute-start | bytes 245768 | tf_op jit(solution)/shard_map/ppermute | solution.py:460
  45.8 3.1 %collective-permute-start.3 = (bf16[10,16,256]{2,1,0:T(8,128)(2,1)S(1)}, bf16[10,16,256]{2,1,0:T(8,128)(2,1)S(1)}, u32[]{:S(2)}, u32[]{:S(2)}) collective-permute-start(bf16[10,16,256]{2,1,0:T(8,128)(2,1)S(1)} %get-tuple-element.15), channel_id=1, source_target_pairs={{0,32},{32,0},{64,96},{96,64},{128,160},{160,128},{192,224},{224,1... | collective-permute-start | bytes 245768 | tf_op jit(solution)/shard_map/ppermute | solution.py:463
  48.9 2.9 %collective-permute-done.2.from_cross = bf16[10,16,256]{2,1,0:T(8,128)(2,1)S(1)} collective-permute-done((bf16[10,16,256]{2,1,0:T(8,128)(2,1)S(1)}, bf16[10,16,256]{2,1,0:T(8,128)(2,1)S(1)}, u32[]{:S(2)}, u32[]{:S(2)}) %collective-permute-start.2) | collective-permute-done | bytes 81952 | tf_op jit(solution)/shard_map/ppermute | solution.py:460
  51.7 0.0 collective-permute-done.3.from_sibling
  51.7 1.5 %surface.1 = bf16[256,128]{1,0:T(8,128)(2,1)} custom-call(f32[20,16,256]{2,1,0:T(8,128)S(1)} %get-tuple-element.12.lam_ref, bf16[60,16,256]{2,1,0:T(8,128)(2,1)S(1)} %get-tuple-element.13.winds_ref, bf16[10,16,256]{2,1,0:T(8,128)(2,1)S(1)} %collective-permute-done.2.from_cross, bf16[10,16,256]{2,1,0:T(8,128)(2,1)S(1)} %collective-permute-done.3.from_sibling), custom_call_target="tpu_custom_call" | custom-call | tf_op jit(solution)/shard_map/surface/pallas_call | solution.py:475
  53.2 0.0 copy-start.2
  53.2 4.7 %all-to-all-start.1 = ((bf16[32,8,128]{2,1,0:T(8,128)(2,1)}), bf16[32,8,128]{2,1,0:T(8,128)(2,1)S(1)}, u32[]{:S(2)}, u32[]{:S(2)}) async-start(bf16[32,8,128]{2,1,0:T(8,128)(2,1)} %bitcast.3), calls=%async_computation.1 | async-start | bytes 131072 | tf_op jit(solution)/shard_map/all_to_all | solution.py:481
  57.9 0.0 copy-done.2
  57.9 0.2 correlation.1.correlation_ref
  58.1 2.1 %steps.1 = f32[12,12,216]{2,1,0:T(8,128)} custom-call(f32[20,16,256]{2,1,0:T(8,128)S(1)} %get-tuple-element.12.lam_ref, bf16[60,16,256]{2,1,0:T(8,128)(2,1)S(1)} %get-tuple-element.13.winds_ref, bf16[10,16,256]{2,1,0:T(8,128)(2,1)S(1)} %collective-permute-done.2.from_cross, bf16[10,16,256]{2,1,0:T(8,128)(2,1)S(1)} %collective-permute-done.3.from_sibling), custom_call_target="tpu_custom_call" | custom-call | tf_op jit(solution)/shard_map/steps/pallas_call | solution.py:482
  60.2 5.1 %all-to-all-done.1 = bf16[32,8,128]{2,1,0:T(8,128)(2,1)S(1)} async-done(((bf16[32,8,128]{2,1,0:T(8,128)(2,1)}), bf16[32,8,128]{2,1,0:T(8,128)(2,1)S(1)}, u32[]{:S(2)}, u32[]{:S(2)}) %all-to-all-start.1) | async-done | bytes 65568 | tf_op jit(solution)/shard_map/all_to_all | solution.py:481
  65.3 0.9 %gradient.1 = f32[12,3,12]{2,1,0:T(4,128)} custom-call(bf16[256,128]{1,0:T(8,128)(2,1)S(1)} %bitcast.7, bf16[32,256]{1,0:T(8,128)(2,1)S(1)} %correlation.1.correlation_ref), custom_call_target="tpu_custom_call" | custom-call | tf_op jit(solution)/shard_map/gradient/pallas_call | solution.py:483
  (1 shorter events, 0.0 us)
Async XLA Ops:
  0.6 11.2 %copy-start.3 = (bf16[4,12,12,144]{3,0,2,1:T(4,128)(2,1)S(1)}, bf16[4,12,12,144]{3,0,2,1:T(4,128)(2,1)}, u32[]{:S(2)}) copy-start(bf16[4,12,12,144]{3,0,2,1:T(4,128)(2,1)} %param.10) | copy-start | bytes 497668
  2.6 17.9 %all-to-all-start = ((bf16[32,8,256]{2,1,0:T(8,128)(2,1)}), bf16[32,8,256]{2,1,0:T(8,128)(2,1)S(1)}, u32[]{:S(2)}, u32[]{:S(2)}) async-start(bf16[32,8,256]{2,1,0:T(8,128)(2,1)} %bitcast.9), calls=%async_computation | async-start | bytes 262144 | tf_op jit(solution)/shard_map/all_to_all | solution.py:442
  11.9 8.6 %copy-start = (f32[12,12,216]{2,1,0:T(8,128)S(1)}, f32[12,12,216]{2,1,0:T(8,128)}, u32[]{:S(2)}) copy-start(f32[12,12,216]{2,1,0:T(8,128)} %adjoint_ref.1) | copy-start | bytes 373252
  11.9 8.6 %copy-start.1 = (f32[64,216]{1,0:T(8,128)S(1)}, f32[64,216]{1,0:T(8,128)}, u32[]{:S(2)}) copy-start(f32[64,216]{1,0:T(8,128)} %table_ref.1) | copy-start | bytes 165892
  21.0 21.9 %collective-permute-start = (bf16[11,16,128]{2,1,0:T(8,128)(2,1)S(1)}, bf16[11,16,128]{2,1,0:T(8,128)(2,1)S(1)}, u32[]{:S(2)}, u32[]{:S(2)}) collective-permute-start(bf16[11,16,128]{2,1,0:T(8,128)(2,1)S(1)} %get-tuple-element.10), channel_id=1, source_target_pairs={{0,1},{1,2},{2,3},{3,4},{4,5},{5,6},{6,7},{7,8},{8,9},{9,10},{10,1... | collective-permute-start | bytes 135176 | tf_op jit(solution)/shard_map/ppermute | solution.py:454
  26.2 17.5 %collective-permute-start.1 = (bf16[11,16,128]{2,1,0:T(8,128)(2,1)S(1)}, bf16[11,16,128]{2,1,0:T(8,128)(2,1)S(1)}, u32[]{:S(2)}, u32[]{:S(2)}) collective-permute-start(bf16[11,16,128]{2,1,0:T(8,128)(2,1)S(1)} %get-tuple-element.11), channel_id=1, source_target_pairs={{1,0},{2,1},{3,2},{4,3},{5,4},{6,5},{7,6},{8,7},{9,8},{10,9},{11,1... | collective-permute-start | bytes 135176 | tf_op jit(solution)/shard_map/ppermute | solution.py:455
  43.9 7.9 %collective-permute-start.2 = (bf16[10,16,256]{2,1,0:T(8,128)(2,1)S(1)}, bf16[10,16,256]{2,1,0:T(8,128)(2,1)S(1)}, u32[]{:S(2)}, u32[]{:S(2)}) collective-permute-start(bf16[10,16,256]{2,1,0:T(8,128)(2,1)S(1)} %get-tuple-element.14), channel_id=1, source_target_pairs={{0,992},{32,64},{64,32},{96,128},{128,96},{160,192},{192,160},{224... | collective-permute-start | bytes 245768 | tf_op jit(solution)/shard_map/ppermute | solution.py:460
  45.8 5.9 %collective-permute-start.3 = (bf16[10,16,256]{2,1,0:T(8,128)(2,1)S(1)}, bf16[10,16,256]{2,1,0:T(8,128)(2,1)S(1)}, u32[]{:S(2)}, u32[]{:S(2)}) collective-permute-start(bf16[10,16,256]{2,1,0:T(8,128)(2,1)S(1)} %get-tuple-element.15), channel_id=1, source_target_pairs={{0,32},{32,0},{64,96},{96,64},{128,160},{160,128},{192,224},{224,1... | collective-permute-start | bytes 245768 | tf_op jit(solution)/shard_map/ppermute | solution.py:463
  53.2 4.7 %copy-start.2 = (bf16[384,12]{0,1:T(8,128)(2,1)S(1)}, bf16[384,12]{0,1:T(8,128)(2,1)}, u32[]{:S(2)}) copy-start(bf16[384,12]{0,1:T(8,128)(2,1)} %param.17) | copy-start | bytes 27652
  53.2 12.1 %all-to-all-start.1 = ((bf16[32,8,128]{2,1,0:T(8,128)(2,1)}), bf16[32,8,128]{2,1,0:T(8,128)(2,1)S(1)}, u32[]{:S(2)}, u32[]{:S(2)}) async-start(bf16[32,8,128]{2,1,0:T(8,128)(2,1)} %bitcast.3), calls=%async_computation.1 | async-start | bytes 131072 | tf_op jit(solution)/shard_map/all_to_all | solution.py:481

commit v4 on v3

--- a/solution.py
+++ b/solution.py
@@ -84,9 +84,44 @@
     out_ref[:, half:WIDTH] = sent[:, half:]
 
 
-def pad_winds_body(winds_ref, out_ref):
+def pack_levels(tiles):
+    lane = iota(tiles[0].shape, 1)
+    lane = jnp.where(lane >= LEVELS, lane - LEVELS, lane)
+    packed = tiles[0]
+    for index in range(1, len(tiles)):
+        packed = jnp.where(lane >= 4 * index, pltpu.roll(tiles[index], 4 * index, 1), packed)
+    return packed
+
+
+def winds_body(winds_ref, out_ref, sibling_ref, cross_ref):
     out_ref[...] = jnp.zeros_like(out_ref)
     out_ref[:, :, :ROWS, : 2 * LEVELS] = winds_ref[...]
+    even = lax.rem(lax.axis_index("lon"), 2) == 0
+    sub = iota((8, 128), 0)
+    made = []
+    for tile in (1, 0):
+        rows = []
+        for row in range(ROWS):
+            cuts = [out_ref[4 - step, row, :, :128].astype(F32)[8 * tile : 8 * tile + 8] for step in (1, 2, 3, 4)]
+            parts = [jnp.where(sub < 4, cuts[i], pltpu.roll(cuts[i + 1], 4, 0)) for i in (0, 2)]
+            rows.append(jnp.concatenate(parts, axis=0))
+        made.append(pack_levels(rows))
+    to_east, to_west = made
+    sibling_ref[...] = jnp.where(even, to_east, to_west).astype(BF16)
+    cross_ref[...] = jnp.where(even, to_west, to_east).astype(BF16)
+
+
+def edge_winds(from_cross, from_sibling, row):
+    even = lax.rem(lax.axis_index("lon"), 2) == 0
+    sibling = from_sibling[...].astype(F32)
+    cross = from_cross[...].astype(F32)
+    sides = []
+    for side in (jnp.where(even, sibling, cross), jnp.where(even, cross, sibling)):
+        if row:
+            side = pltpu.roll(side, 128 - 4 * row, 1)
+        first, second = side[0:8], side[8:16]
+        sides.append({1: pltpu.roll(first, 4, 0), 2: first, 3: pltpu.roll(second, 4, 0), 4: second})
+    return sides
 
 
 STRIP = 11
@@ -102,7 +137,7 @@
     return jnp.concatenate([row[0:8], jnp.where(sub < 4, row[8:16], piece)], axis=0)
 
 
-def pack_strip(lam_rows, wind_rows):
+def pack_strip(lam_rows, wind_rows, east, west):
     extra = pieces(lam_rows[3])
     lane = iota((SUB, 128), 1)
     halves = []
@@ -115,7 +150,8 @@
         ]
     main = [row[:, :128] for row in wind_rows]
     extra = pieces(main[4])
-    halves += [with_piece(main[index], extra[index]) for index in range(3)] + [main[3], main[5]]
+    halves += [with_piece(main[index], extra[index]) for index in range(3)]
+    halves += [with_piece(main[3], pack_levels(east)), with_piece(main[5], pack_levels(west))]
     return halves
 
 
@@ -136,7 +172,9 @@
     return lam_rows, wind_rows
 
 
-def force_body(recv_ref, table_ref, adjoint_ref, winds_ref, lam_ref, north_ref, south_ref, table_s):
+def force_body(
+    recv_ref, table_ref, adjoint_ref, winds_ref, from_cross, from_sibling, lam_ref, north_ref, south_ref, table_s
+):
     total = recv_ref.shape[0]
     nkernel = table_ref.shape[0]
     recv = recv_ref[...]
@@ -168,12 +206,16 @@
     lam_ref[:, :ROWS, :WIDTH] = lam_ref[:, :ROWS, :WIDTH] + adjoint_ref[...]
     for lower, strip in ((False, north_ref), (True, south_ref)):
         start = 0 if lower else ROWS - HALO
-        wind_rows = []
+        wind_rows, east, west = [], [], []
         for step in (1, 2, 3):
             depth = HALO - step
             begin = 0 if lower else ROWS - depth
-            wind_rows += [winds_ref[4 - step, begin + i].astype(F32) for i in range(depth)]
-        for index, half in enumerate(pack_strip([lam_ref[start + i] for i in range(HALO)], wind_rows)):
+            for row in range(begin, begin + depth):
+                wind_rows.append(winds_ref[4 - step, row].astype(F32))
+                sides = edge_winds(from_cross, from_sibling, row)
+                east.append(sides[0][step])
+                west.append(sides[1][step])
+        for index, half in enumerate(pack_strip([lam_ref[start + i] for i in range(HALO)], wind_rows, east, west)):
             strip[index] = half.astype(BF16)
 
 
@@ -191,7 +233,7 @@
     return base + (row if row >= 0 else row + ROWS + 2 * reach)
 
 
-def edge_body(lam_ref, from_south, from_north, winds_ref, sibling_ref, cross_ref, lam_out, winds_out):
+def edge_body(lam_ref, from_south, from_north, winds_ref, _, sibling_ref, cross_ref, lam_out, winds_out):
     south_lam, south_winds = unpack_strip([from_south[i].astype(F32) for i in range(STRIP)])
     north_lam, north_winds = unpack_strip([from_north[i].astype(F32) for i in range(STRIP)])
     even = lax.rem(lax.axis_index("lon"), 2) == 0
@@ -247,38 +289,35 @@
     return jnp.where((lane >= 16) & (lane < 24), tile[..., 128:], tile[..., :128])
 
 
-def assemble(refs, lam_s, wide_s, narrow):
+def assemble(refs, lam_s, wide_s):
     lam_ref, winds_ref, from_cross, from_sibling = refs
     even = lax.rem(lax.axis_index("lon"), 2) == 0
-    sub = iota((8, 128 if narrow else WIDE), 0)
-    lanes = 128 if narrow else WIDE
-    keep = pack_low if narrow else (lambda tile: tile)
+    sub = iota((8, WIDE), 0)
     for row in range(-HALO, ROWS + HALO):
         at = ext_index(row)
-        lam = keep(lam_ref[at])
+        lam = lam_ref[at]
         sibling = from_sibling[at // 2].astype(F32)
         cross = from_cross[at // 2].astype(F32)
         east = jnp.where(even, sibling, cross)
         west = jnp.where(even, cross, sibling)
         odd = at % 2
-        east_lam, west_lam = keep(east[0:8]), keep(west[0:8])
+        east_lam, west_lam = east[0:8], west[0:8]
         if not odd:
             east_lam, west_lam = pltpu.roll(east_lam, 4, 0), pltpu.roll(west_lam, 4, 0)
         lam_s[at, 0:8] = lam[0:8]
         lam_s[at, 8:16] = jnp.where(sub < 4, lam[8:16], east_lam)
         lam_s[at, 16:24] = west_lam
         east_wind, west_wind = (side[8:16, 128 * odd : 128 * odd + 128] for side in (east, west))
-        if not narrow:
-            east_wind, west_wind = (
-                jnp.concatenate([main, pltpu.roll(side[0:8, 128:], 128 - SPARE[odd], 1)], axis=1)
-                for main, side in ((east_wind, east), (west_wind, west))
-            )
+        east_wind, west_wind = (
+            jnp.concatenate([main, pltpu.roll(side[0:8, 128:], 128 - SPARE[odd], 1)], axis=1)
+            for main, side in ((east_wind, east), (west_wind, west))
+        )
         for step in range(1, 5):
             reach = HALO - step
             if not -reach <= row < ROWS + reach:
                 continue
             place = wind_index(step, row)
-            wind = winds_ref[place, :, :lanes].astype(F32)
+            wind = winds_ref[place].astype(F32)
             ew, ww = east_wind, west_wind
             if step == 2:
                 ew, ww = pltpu.roll(ew, 4, 0), pltpu.roll(ww, 4, 0)
@@ -359,33 +398,79 @@
         now, later = later, now
 
 
+def assemble_low(refs, lam_s, wide_s):
+    lam_ref, from_south, from_north, winds_ref, from_cross, from_sibling = refs
+    sub = iota((8, 128), 0)
+    halos = []
+    for strip in (from_south, from_north):
+        halves = [strip[i].astype(F32) for i in range(STRIP)]
+        halos.append((*unpack_strip(halves), halves[9][8:16], halves[10][8:16]))
+    for row in range(-HALO, ROWS + HALO):
+        own = 0 <= row < ROWS
+        at = ext_index(row)
+        if own:
+            lam = pack_low(lam_ref[row])
+            sides = edge_winds(from_cross, from_sibling, row)
+        else:
+            lam_rows, wind_rows, east, west = halos[0 if row < 0 else 1]
+            lam = pack_low(lam_rows[row + HALO if row < 0 else row - ROWS])
+        lam_s[at, 0:8] = lam[0:8]
+        lam_s[at, 8:16] = jnp.where(sub < 4, lam[8:16], 0.0)
+        lam_s[at, 16:24] = jnp.zeros((8, 128), F32)
+        for step in range(1, 5):
+            reach = HALO - step
+            if not -reach <= row < ROWS + reach:
+                continue
+            if own:
+                wind = winds_ref[4 - step, row, :, :128].astype(F32)
+                east_wind, west_wind = sides[0][step], sides[1][step]
+            else:
+                index = WIND_FIRST[step] + (row + reach if row < 0 else row - ROWS)
+                wind = wind_rows[index][:, :128]
+                east_wind, west_wind = (pltpu.roll(side, 128 - 4 * index, 1) if index else side for side in (east, west))
+            place = wind_index(step, row)
+            wide_s[place, 0:16] = jnp.concatenate(
+                [wind[0:8], jnp.where(sub < 4, wind[8:16], east_wind)], axis=0
+            ).astype(BF16)
+            wide_s[place, 16:24] = west_wind.astype(BF16)
+
+
+LOW = WIDTH // 6
+
+
 def surface_body(
-    lam_ref, winds_ref, from_cross, from_sibling, out_ref, lam_a, lam_b, wide_s, coef_s, acc_s
+    lam_ref, from_south, from_north, winds_ref, from_cross, from_sibling, out_ref, lam_a, lam_b, wide_s, coef_s, acc_s
 ):
-    refs = (lam_ref, winds_ref, from_cross, from_sibling)
-    assemble(refs, lam_a, wide_s, True)
+    assemble_low((lam_ref, from_south, from_north, winds_ref, from_cross, from_sibling), lam_a, wide_s)
 
     def emit(step, row, value):
-        acc_s[row] = value[:SUB] if step == 1 else acc_s[row] + value[:SUB]
+        acc_s[row] = value if step == 1 else acc_s[row] + value
 
     advance(lam_a, lam_b, wide_s, coef_s, True, emit)
-    lane = iota((SUB, 128), 1)
-    surface = jnp.zeros((SUB, 128), F32)
+    lane = iota((SUB + 8, 128), 1)
+    surface = jnp.zeros((SUB + 8, 128), F32)
     for row in range(ROWS):
         held = acc_s[row]
         for species, source in enumerate((0, LEVELS, 16)):
             at = row * SPECIES + species
             surface = jnp.where(lane == at, pltpu.roll(held, (at - source) % 128, 1), surface)
-    surface = jnp.where(iota((SUB, 128), 0) < ROWS, surface, 0.0)
-    block = jnp.where(lane[:8] < 64, surface[0:8], pltpu.roll(surface[8:16], 64, 1))
-    both = jnp.concatenate([block, block], axis=0).astype(BF16)
-    for pair in range(out_ref.shape[0] // SUB):
-        out_ref[SUB * pair : SUB * pair + SUB] = both
+    high = surface.astype(BF16).astype(F32)
+    low = (surface - high).astype(BF16).astype(F32)
+    lane = iota((8, 128), 1)
+    parts = []
+    for tile, last in ((0, high), (1, low)):
+        cut = slice(8 * tile, 8 * tile + 8)
+        second = pltpu.roll(low[cut], LOW, 1)
+        third = pltpu.roll(last[16:24], 2 * LOW, 1)
+        parts.append(jnp.where(lane < LOW, high[cut], jnp.where(lane < 2 * LOW, second, third)))
+    block = jnp.concatenate(parts, axis=0).astype(BF16)
+    for target in range(out_ref.shape[0] // SUB):
+        out_ref[SUB * target : SUB * target + SUB] = block
 
 
 def steps_body(lam_ref, winds_ref, from_cross, from_sibling, field_ref, lam_a, lam_b, wide_s, coef_s):
     refs = (lam_ref, winds_ref, from_cross, from_sibling)
-    assemble(refs, lam_a, wide_s, False)
+    assemble(refs, lam_a, wide_s)
 
     def emit(step, row, value):
         if step == 4:
@@ -409,8 +494,25 @@
         out_ref[SUB * index : SUB * index + SUB] = part.astype(BF16)
 
 
-def gradient_body(surface_ref, correlation_ref, out_ref):
-    both = jnp.dot(correlation_ref[...], surface_ref[...], preferred_element_type=F32)
+def gradient_body(surface_ref, correlation_ref, out_ref, blocks_s):
+    blocks = surface_ref.shape[0] // SUB
+    lane = iota((8, 128), 1)
+    sub = iota((8, 128), 0)
+    mains, easts, wests = [], [], []
+    for block in range(blocks):
+        both = surface_ref[SUB * block : SUB * block + SUB].astype(F32)
+        whole = both + pltpu.roll(both, 128 - LOW, 1)
+        mains.append(whole)
+        easts.append(pltpu.roll(whole[8:16], 4, 0))
+        wests.append(pltpu.roll(pltpu.roll(both[0:8] + both[8:16], 128 - 2 * LOW, 1), 4, 0))
+    for pair in range(blocks // 2):
+        parts = []
+        for block in (2 * pair, 2 * pair + 1):
+            left = mains[block][0:8] + jnp.where(sub < 4, easts[block - 1], 0.0)
+            right = jnp.where(sub < 4, mains[block][8:16] + wests[(block + 1) % blocks], 0.0)
+            parts.append(jnp.where(lane < 64, left, pltpu.roll(right, 64, 1)))
+        blocks_s[SUB * pair : SUB * pair + SUB] = jnp.concatenate(parts, axis=0).astype(BF16)
+    both = jnp.dot(correlation_ref[...], blocks_s[...], preferred_element_type=F32)
     sums = both[:SUB] + pltpu.roll(both[SUB:], 64, 1)
     result = jnp.transpose(sums)
     for row in range(ROWS):
@@ -440,7 +542,14 @@
         in_specs=[pl.BlockSpec(memory_space=pltpu.HBM)] * 5,
     )(counts, offsets, columns, kernel_ids, jnp.swapaxes(innovations, 2, 3))
     recv = lax.all_to_all(sent, "lon", split_axis=0, concat_axis=0, tiled=True)
-    winds = vmem_call(pad_winds_body, shape((4, ROWS, SUB, WIDE), BF16), name="pad_winds")(stored_winds)
+    rim = shape((SUB, 128), BF16)
+    winds, rim_sibling, rim_cross = vmem_call(
+        winds_body, (shape((4, ROWS, SUB, WIDE), BF16), rim, rim), name="winds"
+    )(stored_winds)
+    across = [(i, (i + (1 if i % 2 else -1)) % lon_count) for i in range(lon_count)]
+    within = [(i, i ^ 1) for i in range(lon_count)]
+    winds_cross = lax.ppermute(rim_cross, "lon", across)
+    winds_sibling = lax.ppermute(rim_sibling, "lon", within)
     turned = vmem_call(correlation_body, shape((2 * SUB, lon_count * 8), BF16), name="correlation")(correlation.T)
     strip = shape((STRIP, SUB, 128), BF16)
     lam, north, south = vmem_call(
@@ -448,19 +557,11 @@
         (shape((ROWS, SUB, WIDE), F32), strip, strip),
         [pltpu.VMEM((3 * kernel_table.shape[0], WIDE), BF16)],
         name="force",
-    )(recv, kernel_table, adjoint_in, winds)
+    )(recv, kernel_table, adjoint_in, winds, winds_cross, winds_sibling)
     up = [(i, i + 1) for i in range(lat_count - 1)]
     down = [(i + 1, i) for i in range(lat_count - 1)]
     from_south = lax.ppermute(north, "lat", up)
     from_north = lax.ppermute(south, "lat", down)
-    edge = shape((EXT // 2, SUB, WIDE), BF16)
-    to_sibling, to_cross, lam_ext, winds_ext = vmem_call(
-        edge_body, (edge, edge, shape((EXT, SUB, WIDE), F32), shape((60, SUB, WIDE), BF16)), name="edge"
-    )(lam, from_south, from_north, winds)
-    from_cross = lax.ppermute(
-        to_cross, "lon", [(i, (i + (1 if i % 2 else -1)) % lon_count) for i in range(lon_count)]
-    )
-    from_sibling = lax.ppermute(to_sibling, "lon", [(i, i ^ 1) for i in range(lon_count)])
     cols = SUB + 8
 
     def scratch(lanes):
@@ -471,16 +572,35 @@
             pltpu.VMEM((EXT, cols, 2 * lanes), F32),
         ]
 
-    state = (lam_ext, winds_ext, from_cross, from_sibling)
     surface = vmem_call(
         surface_body,
-        shape((lon_count * 8, 128), BF16),
-        scratch(128) + [pltpu.VMEM((ROWS, SUB, 128), F32)],
+        shape((lon_count * SUB, 128), BF16),
+        scratch(128) + [pltpu.VMEM((ROWS, cols, 128), F32)],
         name="surface",
+    )(lam, from_south, from_north, winds, winds_cross, winds_sibling)
+    gathered = lax.all_to_all(surface, "lon", split_axis=0, concat_axis=0, tiled=True)
+    edge = shape((EXT // 2, SUB, WIDE), BF16)
+    to_sibling, to_cross, lam_ext, winds_ext = vmem_call(
+        edge_body,
+        (edge, edge, shape((EXT, SUB, WIDE), F32), shape((60, SUB, WIDE), BF16)),
+        name="edge",
+        in_specs=[pl.BlockSpec(memory_space=pltpu.VMEM)] * 4 + [pl.BlockSpec(memory_space=pl.ANY)],
+    )(lam, from_south, from_north, winds, surface)
+    from_cross = lax.ppermute(to_cross, "lon", across)
+    from_sibling = lax.ppermute(to_sibling, "lon", within)
+    state = (lam_ext, winds_ext, from_cross, from_sibling)
+    gradient = vmem_call(
+        gradient_body,
+        shape((ROWS, SPECIES, ROWS), F32),
+        [pltpu.VMEM((lon_count * 8, 128), BF16)],
+        name="gradient",
+    )(gathered, turned)
+    field = vmem_call(
+        steps_body,
+        shape((ROWS, ROWS, WIDTH), F32),
+        scratch(WIDE),
+        name="steps",
     )(*state)
-    gathered = lax.all_to_all(surface, "lon", split_axis=0, concat_axis=0, tiled=True)
-    field = vmem_call(steps_body, shape((ROWS, ROWS, WIDTH), F32), scratch(WIDE), name="steps")(*state)
-    gradient = vmem_call(gradient_body, shape((ROWS, SPECIES, ROWS), F32), name="gradient")(gathered, turned)
     return field, gradient
 
 

time: 66.8 us -> 63.1 us (0.945)
  waiting for transfers between devices: 18.2 us -> 5.39 us
  starting transfers between devices: 39.8 us -> 48.7 us
    ppermute x2 -> x4, starting transfers between devices: 4.99 us -> 12.5 us  [the longest x1 4.33 us: per_device(): winds_cross = lax.ppermute(rim_cross, 'lon', across)]
    all_to_all x1, waiting for transfers between devices: 8.54 us -> 1.04 us  [per_device(): recv = lax.all_to_all(sent, 'lon', split_axis=0, concat_axis=0, tiled=True)]
    all_to_all x1, waiting for transfers between devices: 5.09 us -> 0.01 us  [per_device(): lax.all_to_all(surface, 'lon', split_axis=0, concat_axis=0, tiled=True)]
    all_to_all x1, starting transfers between devices: 4.68 us -> 6.02 us  [per_device(): lax.all_to_all(surface, 'lon', split_axis=0, concat_axis=0, tiled=True)]
    ppermute x2 -> x4, waiting for transfers between devices: 2.86 us -> 2.65 us  [the longest x1 1.52 us: per_device(): from_cross = lax.ppermute(to_cross, 'lon', across)]
  transfers between devices with their start and end apart: 6 -> 8, of which waited for: 5 -> 6; matrix products, arithmetic and copies ran while one was open for 0% -> 0% of each run, Pallas kernels for 4% -> 4%
where the time goes in v4:
time: 63.1 us; the launch traced here: 62.6 us
  starting transfers between devices  48.7 us (77%)
  Pallas kernels  7.71 us (12%)
  waiting for transfers between devices  5.39 us (9%)
  between operations  0.77 us (1%)
    ppermute x1, starting transfers between devices, per_device(): from_north = lax.ppermute(south, 'lat', down)  15.8 us
    all_to_all x1, starting transfers between devices, per_device(): recv = lax.all_to_all(sent, 'lon', split_axis=0, concat_axis=0, tiled=True)  9.19 us
    all_to_all x1, starting transfers between devices, per_device(): lax.all_to_all(surface, 'lon', split_axis=0, concat_axis=0, tiled=True)  6.02 us
    ppermute x1, starting transfers between devices, per_device(): from_south = lax.ppermute(north, 'lat', up)  5.19 us
    ppermute x1, starting transfers between devices, per_device(): winds_cross = lax.ppermute(rim_cross, 'lon', across)  4.33 us
    ppermute x1, starting transfers between devices, per_device(): from_cross = lax.ppermute(to_cross, 'lon', across)  4.33 us
    pallas_call x1, Pallas kernels, per_device(): vmem_call(steps_body, shape((ROWS, ROWS, WIDTH), F32), scratch(WIDE), nam...  2.1 us
    pallas_call x1, Pallas kernels, per_device(): vmem_call(route_body, shape((lon_count * CAP, WIDE), BF16), [pltpu.VMEM((...  1.98 us
  transfers between devices with their start and end apart: 8, of which 6 were waited for; matrix products, arithmetic and copies ran while one was open for 0% of the time, Pallas kernels for 4%

profile of v4, /device:TPU:14, one launch (start us, length us, event | category | flops | bytes accessed | tf_op | source)
XLA Modules:
  0.0 62.6 jit_solution(11698597166507236690)
XLA Ops:
  0.6 0.0 copy-start.3
  0.6 2.0 %route.1 = bf16[256,256]{1,0:T(8,128)(2,1)} custom-call(s32[1,1,32]{2,1,0:T(1,128)} %counts_hbm.1, s32[1,1,32]{2,1,0:T(1,128)} %offsets_hbm.1, s32[1,1,256]{2,1,0:T(1,128)} %columns_hbm.1, s32[1,1,256]{2,1,0:T(1,128)} %kernels_hbm.1, bf16[1,1,216,256]{3,2,1,0:T(8,128)(2,1)} %bitcast.10), custom_call_target="tpu_custom_call" | custom-call | tf_op jit(solution)/shard_map/route/pallas_call | solution.py:529
  2.6 9.2 %all-to-all-start = ((bf16[32,8,256]{2,1,0:T(8,128)(2,1)}), bf16[32,8,256]{2,1,0:T(8,128)(2,1)S(1)}, u32[]{:S(2)}, u32[]{:S(2)}) async-start(bf16[32,8,256]{2,1,0:T(8,128)(2,1)} %bitcast.9), calls=%async_computation | async-start | bytes 262144 | tf_op jit(solution)/shard_map/all_to_all | solution.py:544
  11.8 0.0 copy-done.3
  11.9 0.0 copy-start
  11.9 0.0 copy-start.1
  11.9 0.2 winds.1
  12.1 4.3 %collective-permute-start = (bf16[16,128]{1,0:T(8,128)(2,1)S(1)}, bf16[16,128]{1,0:T(8,128)(2,1)S(1)}, u32[]{:S(2)}, u32[]{:S(2)}) collective-permute-start(bf16[16,128]{1,0:T(8,128)(2,1)S(1)} %get-tuple-element.13), channel_id=1, source_target_pairs={{0,992},{32,64},{64,32},{96,128},{128,96},{160,192},{192,160},{224... | collective-permute-start | bytes 12296 | tf_op jit(solution)/shard_map/ppermute | solution.py:551
  16.4 1.9 %collective-permute-start.1 = (bf16[16,128]{1,0:T(8,128)(2,1)S(1)}, bf16[16,128]{1,0:T(8,128)(2,1)S(1)}, u32[]{:S(2)}, u32[]{:S(2)}) collective-permute-start(bf16[16,128]{1,0:T(8,128)(2,1)S(1)} %get-tuple-element.14), channel_id=1, source_target_pairs={{0,32},{32,0},{64,96},{96,64},{128,160},{160,128},{192,224},{224,1... | collective-permute-start | bytes 12296 | tf_op jit(solution)/shard_map/ppermute | solution.py:552
  18.4 0.8 %collective-permute-done.from_cross = bf16[16,128]{1,0:T(8,128)(2,1)S(1)} collective-permute-done((bf16[16,128]{1,0:T(8,128)(2,1)S(1)}, bf16[16,128]{1,0:T(8,128)(2,1)S(1)}, u32[]{:S(2)}, u32[]{:S(2)}) %collective-permute-start) | collective-permute-done | bytes 4128 | tf_op jit(solution)/shard_map/ppermute | solution.py:551
  19.1 0.3 collective-permute-done.1.from_sibling
  19.5 1.0 %all-to-all-done = bf16[32,8,256]{2,1,0:T(8,128)(2,1)S(1)} async-done(((bf16[32,8,256]{2,1,0:T(8,128)(2,1)}), bf16[32,8,256]{2,1,0:T(8,128)(2,1)S(1)}, u32[]{:S(2)}, u32[]{:S(2)}) %all-to-all-start) | async-done | bytes 131104 | tf_op jit(solution)/shard_map/all_to_all | solution.py:544
  20.5 0.0 copy-done
  20.5 0.0 copy-done.1
  20.5 0.5 force.1
  21.0 5.2 %collective-permute-start.2 = (bf16[11,16,128]{2,1,0:T(8,128)(2,1)S(1)}, bf16[11,16,128]{2,1,0:T(8,128)(2,1)S(1)}, u32[]{:S(2)}, u32[]{:S(2)}) collective-permute-start(bf16[11,16,128]{2,1,0:T(8,128)(2,1)S(1)} %get-tuple-element.16), channel_id=1, source_target_pairs={{0,1},{1,2},{2,3},{3,4},{4,5},{5,6},{6,7},{7,8},{8,9},{9,10},{10,1... | collective-permute-start | bytes 135176 | tf_op jit(solution)/shard_map/ppermute | solution.py:563
  26.2 15.8 %collective-permute-start.3 = (bf16[11,16,128]{2,1,0:T(8,128)(2,1)S(1)}, bf16[11,16,128]{2,1,0:T(8,128)(2,1)S(1)}, u32[]{:S(2)}, u32[]{:S(2)}) collective-permute-start(bf16[11,16,128]{2,1,0:T(8,128)(2,1)S(1)} %get-tuple-element.17), channel_id=1, source_target_pairs={{1,0},{2,1},{3,2},{4,3},{5,4},{6,5},{7,6},{8,7},{9,8},{10,9},{11,1... | collective-permute-start | bytes 135176 | tf_op jit(solution)/shard_map/ppermute | solution.py:564
  42.0 1.0 %collective-permute-done.2.from_south = bf16[11,16,128]{2,1,0:T(8,128)(2,1)S(1)} collective-permute-done((bf16[11,16,128]{2,1,0:T(8,128)(2,1)S(1)}, bf16[11,16,128]{2,1,0:T(8,128)(2,1)S(1)}, u32[]{:S(2)}, u32[]{:S(2)}) %collective-permute-start.2) | collective-permute-done | bytes 45088 | tf_op jit(solution)/shard_map/ppermute | solution.py:563
  43.0 0.7 %collective-permute-done.3.from_north = bf16[11,16,128]{2,1,0:T(8,128)(2,1)S(1)} collective-permute-done((bf16[11,16,128]{2,1,0:T(8,128)(2,1)S(1)}, bf16[11,16,128]{2,1,0:T(8,128)(2,1)S(1)}, u32[]{:S(2)}, u32[]{:S(2)}) %collective-permute-start.3) | collective-permute-done | bytes 45088 | tf_op jit(solution)/shard_map/ppermute | solution.py:564
  43.7 1.5 %surface.1._ = bf16[512,128]{1,0:T(8,128)(2,1)} custom-call(f32[12,16,256]{2,1,0:T(8,128)S(1)} %get-tuple-element.15.lam_ref, bf16[11,16,128]{2,1,0:T(8,128)(2,1)S(1)} %collective-permute-done.2.from_south, bf16[11,16,128]{2,1,0:T(8,128)(2,1)S(1)} %collective-permute-done.3.from_north, bf16[4,12,16,256]{3,2,1,0:T(8,128)(2,1)S(1)} %get-tuple-element.12.winds_ref, ...), custom_call_target="tpu_custom_call" | custom-call | tf_op jit(solution)/shard_map/surface/pallas_call | solution.py:575
  45.2 6.0 %all-to-all-start.1 = ((bf16[32,16,128]{2,1,0:T(8,128)(2,1)}), bf16[32,16,128]{2,1,0:T(8,128)(2,1)S(1)}, u32[]{:S(2)}, u32[]{:S(2)}) async-start(bf16[32,16,128]{2,1,0:T(8,128)(2,1)} %bitcast.3), calls=%async_computation.1 | async-start | bytes 262144 | tf_op jit(solution)/shard_map/all_to_all | solution.py:581
  51.3 0.0 copy-start.2
  51.3 0.2 edge.1
  51.4 4.3 %collective-permute-start.4 = (bf16[10,16,256]{2,1,0:T(8,128)(2,1)S(1)}, bf16[10,16,256]{2,1,0:T(8,128)(2,1)S(1)}, u32[]{:S(2)}, u32[]{:S(2)}) collective-permute-start(bf16[10,16,256]{2,1,0:T(8,128)(2,1)S(1)} %get-tuple-element.20), channel_id=1, source_target_pairs={{0,992},{32,64},{64,32},{96,128},{128,96},{160,192},{192,160},{224... | collective-permute-start | bytes 245768 | tf_op jit(solution)/shard_map/ppermute | solution.py:589
  55.8 1.9 %collective-permute-start.5 = (bf16[10,16,256]{2,1,0:T(8,128)(2,1)S(1)}, bf16[10,16,256]{2,1,0:T(8,128)(2,1)S(1)}, u32[]{:S(2)}, u32[]{:S(2)}) collective-permute-start(bf16[10,16,256]{2,1,0:T(8,128)(2,1)S(1)} %get-tuple-element.21), channel_id=1, source_target_pairs={{0,32},{32,0},{64,96},{96,64},{128,160},{160,128},{192,224},{224,1... | collective-permute-start | bytes 245768 | tf_op jit(solution)/shard_map/ppermute | solution.py:590
  57.7 0.0 copy-done.2
  57.7 0.2 correlation.1.correlation_ref
  57.9 1.5 %collective-permute-done.4.from_cross = bf16[10,16,256]{2,1,0:T(8,128)(2,1)S(1)} collective-permute-done((bf16[10,16,256]{2,1,0:T(8,128)(2,1)S(1)}, bf16[10,16,256]{2,1,0:T(8,128)(2,1)S(1)}, u32[]{:S(2)}, u32[]{:S(2)}) %collective-permute-start.4) | collective-permute-done | bytes 81952 | tf_op jit(solution)/shard_map/ppermute | solution.py:589
  59.4 0.0 collective-permute-done.5.from_sibling
  59.4 2.1 %steps.1 = f32[12,12,216]{2,1,0:T(8,128)} custom-call(f32[20,16,256]{2,1,0:T(8,128)S(1)} %get-tuple-element.18.lam_ref, bf16[60,16,256]{2,1,0:T(8,128)(2,1)S(1)} %get-tuple-element.19.winds_ref, bf16[10,16,256]{2,1,0:T(8,128)(2,1)S(1)} %collective-permute-done.4.from_cross, bf16[10,16,256]{2,1,0:T(8,128)(2,1)S(1)} %collective-permute-done.5.from_sibling), custom_call_target="tpu_custom_call" | custom-call | tf_op jit(solution)/shard_map/steps/pallas_call | solution.py:598
  61.5 0.0 all-to-all-done.1
  61.5 1.1 %gradient.1 = f32[12,3,12]{2,1,0:T(4,128)} custom-call(bf16[512,128]{1,0:T(8,128)(2,1)S(1)} %bitcast.7, bf16[32,256]{1,0:T(8,128)(2,1)S(1)} %correlation.1.correlation_ref), custom_call_target="tpu_custom_call" | custom-call | tf_op jit(solution)/shard_map/gradient/pallas_call | solution.py:592
  (1 shorter events, 0.0 us)
Async XLA Ops:
  0.6 11.2 %copy-start.3 = (bf16[4,12,12,144]{3,0,2,1:T(4,128)(2,1)S(1)}, bf16[4,12,12,144]{3,0,2,1:T(4,128)(2,1)}, u32[]{:S(2)}) copy-start(bf16[4,12,12,144]{3,0,2,1:T(4,128)(2,1)} %param.10) | copy-start | bytes 497668
  2.6 17.9 %all-to-all-start = ((bf16[32,8,256]{2,1,0:T(8,128)(2,1)}), bf16[32,8,256]{2,1,0:T(8,128)(2,1)S(1)}, u32[]{:S(2)}, u32[]{:S(2)}) async-start(bf16[32,8,256]{2,1,0:T(8,128)(2,1)} %bitcast.9), calls=%async_computation | async-start | bytes 262144 | tf_op jit(solution)/shard_map/all_to_all | solution.py:544
  11.9 8.6 %copy-start = (f32[12,12,216]{2,1,0:T(8,128)S(1)}, f32[12,12,216]{2,1,0:T(8,128)}, u32[]{:S(2)}) copy-start(f32[12,12,216]{2,1,0:T(8,128)} %adjoint_ref.1) | copy-start | bytes 373252
  11.9 8.6 %copy-start.1 = (f32[64,216]{1,0:T(8,128)S(1)}, f32[64,216]{1,0:T(8,128)}, u32[]{:S(2)}) copy-start(f32[64,216]{1,0:T(8,128)} %table_ref.1) | copy-start | bytes 165892
  12.1 7.1 %collective-permute-start = (bf16[16,128]{1,0:T(8,128)(2,1)S(1)}, bf16[16,128]{1,0:T(8,128)(2,1)S(1)}, u32[]{:S(2)}, u32[]{:S(2)}) collective-permute-start(bf16[16,128]{1,0:T(8,128)(2,1)S(1)} %get-tuple-element.13), channel_id=1, source_target_pairs={{0,992},{32,64},{64,32},{96,128},{128,96},{160,192},{192,160},{224... | collective-permute-start | bytes 12296 | tf_op jit(solution)/shard_map/ppermute | solution.py:551
  16.4 3.1 %collective-permute-start.1 = (bf16[16,128]{1,0:T(8,128)(2,1)S(1)}, bf16[16,128]{1,0:T(8,128)(2,1)S(1)}, u32[]{:S(2)}, u32[]{:S(2)}) collective-permute-start(bf16[16,128]{1,0:T(8,128)(2,1)S(1)} %get-tuple-element.14), channel_id=1, source_target_pairs={{0,32},{32,0},{64,96},{96,64},{128,160},{160,128},{192,224},{224,1... | collective-permute-start | bytes 12296 | tf_op jit(solution)/shard_map/ppermute | solution.py:552
  21.0 21.9 %collective-permute-start.2 = (bf16[11,16,128]{2,1,0:T(8,128)(2,1)S(1)}, bf16[11,16,128]{2,1,0:T(8,128)(2,1)S(1)}, u32[]{:S(2)}, u32[]{:S(2)}) collective-permute-start(bf16[11,16,128]{2,1,0:T(8,128)(2,1)S(1)} %get-tuple-element.16), channel_id=1, source_target_pairs={{0,1},{1,2},{2,3},{3,4},{4,5},{5,6},{6,7},{7,8},{8,9},{9,10},{10,1... | collective-permute-start | bytes 135176 | tf_op jit(solution)/shard_map/ppermute | solution.py:563
  26.2 17.5 %collective-permute-start.3 = (bf16[11,16,128]{2,1,0:T(8,128)(2,1)S(1)}, bf16[11,16,128]{2,1,0:T(8,128)(2,1)S(1)}, u32[]{:S(2)}, u32[]{:S(2)}) collective-permute-start(bf16[11,16,128]{2,1,0:T(8,128)(2,1)S(1)} %get-tuple-element.17), channel_id=1, source_target_pairs={{1,0},{2,1},{3,2},{4,3},{5,4},{6,5},{7,6},{8,7},{9,8},{10,9},{11,1... | collective-permute-start | bytes 135176 | tf_op jit(solution)/shard_map/ppermute | solution.py:564
  45.2 16.3 %all-to-all-start.1 = ((bf16[32,16,128]{2,1,0:T(8,128)(2,1)}), bf16[32,16,128]{2,1,0:T(8,128)(2,1)S(1)}, u32[]{:S(2)}, u32[]{:S(2)}) async-start(bf16[32,16,128]{2,1,0:T(8,128)(2,1)} %bitcast.3), calls=%async_computation.1 | async-start | bytes 262144 | tf_op jit(solution)/shard_map/all_to_all | solution.py:581
  51.3 6.4 %copy-start.2 = (bf16[384,12]{0,1:T(8,128)(2,1)S(1)}, bf16[384,12]{0,1:T(8,128)(2,1)}, u32[]{:S(2)}) copy-start(bf16[384,12]{0,1:T(8,128)(2,1)} %param.17) | copy-start | bytes 27652
  51.4 8.0 %collective-permute-start.4 = (bf16[10,16,256]{2,1,0:T(8,128)(2,1)S(1)}, bf16[10,16,256]{2,1,0:T(8,128)(2,1)S(1)}, u32[]{:S(2)}, u32[]{:S(2)}) collective-permute-start(bf16[10,16,256]{2,1,0:T(8,128)(2,1)S(1)} %get-tuple-element.20), channel_id=1, source_target_pairs={{0,992},{32,64},{64,32},{96,128},{128,96},{160,192},{192,160},{224... | collective-permute-start | bytes 245768 | tf_op jit(solution)/shard_map/ppermute | solution.py:589
  55.8 3.7 %collective-permute-start.5 = (bf16[10,16,256]{2,1,0:T(8,128)(2,1)S(1)}, bf16[10,16,256]{2,1,0:T(8,128)(2,1)S(1)}, u32[]{:S(2)}, u32[]{:S(2)}) collective-permute-start(bf16[10,16,256]{2,1,0:T(8,128)(2,1)S(1)} %get-tuple-element.21), channel_id=1, source_target_pairs={{0,32},{32,0},{64,96},{96,64},{128,160},{160,128},{192,224},{224,1... | collective-permute-start | bytes 245768 | tf_op jit(solution)/shard_map/ppermute | solution.py:590

commit v5 on v4

--- a/solution.py
+++ b/solution.py
@@ -284,11 +284,6 @@
         cross_ref[ext_index(row) // 2] = jnp.where(even, to_west, to_east).astype(BF16)
 
 
-def pack_low(tile):
-    lane = iota(tile.shape[:-1] + (128,), len(tile.shape) - 1)
-    return jnp.where((lane >= 16) & (lane < 24), tile[..., 128:], tile[..., :128])
-
-
 def assemble(refs, lam_s, wide_s):
     lam_ref, winds_ref, from_cross, from_sibling = refs
     even = lax.rem(lax.axis_index("lon"), 2) == 0
@@ -329,73 +324,83 @@
             wide_s[place, 16:24] = ww.astype(BF16)
 
 
-def wind_spread(narrow):
-    lanes = 128 if narrow else WIDE
-    source = iota((lanes, 2 * lanes), 0)
-    lane = iota((lanes, 2 * lanes), 1)
-    second = lane >= lanes
-    lane = jnp.where(second, lane - lanes, lane)
-    if narrow:
-        level = jnp.where(lane >= LEVELS, lane - LEVELS, jnp.where(lane >= 16, lane - 16, lane))
-        used = level < 8
-    else:
-        level = lane - jnp.where(lane >= LEVELS, LEVELS, 0) - jnp.where(lane >= 2 * LEVELS, LEVELS, 0)
-        used = lane < WIDTH
-    match = (source == level + jnp.where(second, LEVELS, 0)) & used
+def wind_spread():
+    source = iota((WIDE, 2 * WIDE), 0)
+    lane = iota((WIDE, 2 * WIDE), 1)
+    second = lane >= WIDE
+    lane = jnp.where(second, lane - WIDE, lane)
+    level = lane - jnp.where(lane >= LEVELS, LEVELS, 0) - jnp.where(lane >= 2 * LEVELS, LEVELS, 0)
+    match = (source == level + jnp.where(second, LEVELS, 0)) & (lane < WIDTH)
     return jnp.where(match, 0.5, 0.0).astype(BF16)
 
 
-def advance(lam_a, lam_b, wide_s, coef_s, narrow, emit):
+def poles():
     lat = lax.axis_index("lat")
     has_south = jnp.where(lat > 0, 1.0, 0.0).astype(F32)
-    has_north = jnp.where(lat < lax.axis_size("lat") - 1, 1.0, 0.0).astype(F32)
+    return has_south, jnp.where(lat < lax.axis_size("lat") - 1, 1.0, 0.0).astype(F32)
+
+
+def updated(mid, north, south, u, v, top, bottom):
+    cols, lanes = mid.shape
+    east = pltpu.roll(mid, cols - 1, 0)
+    west = pltpu.roll(mid, 1, 0)
+    upper = pltpu.roll(mid, lanes - 1, 1)
+    if top is not None:
+        upper = jnp.where(top, mid, upper)
+    lower = jnp.where(bottom, mid, pltpu.roll(mid, 1, 1))
+    return (
+        CENTER * mid
+        + u * (east - west)
+        + v * (north - south)
+        + HORIZ_MIX * ((east + west) + (north + south))
+        + VERT_MIX * (upper + lower)
+    )
+
+
+def advance(lam_a, lam_b, wide_s, coef_s, field_ref):
+    has_south, has_north = poles()
     cols = SUB + 8
-    lanes = 128 if narrow else WIDE
-    spread = wind_spread(narrow)
-    lane = iota((cols, lanes), 1)
-    if narrow:
-        top = None
-        bottom = (lane == 0) | (lane == 16) | (lane == LEVELS)
-    else:
-        top = (lane == LEVELS - 1) | (lane == 2 * LEVELS - 1) | (lane == 3 * LEVELS - 1)
-        bottom = (lane == 0) | (lane == LEVELS) | (lane == 2 * LEVELS)
+    spread = wind_spread()
+    lane = iota((cols, WIDE), 1)
+    top = (lane == LEVELS - 1) | (lane == 2 * LEVELS - 1) | (lane == 3 * LEVELS - 1)
+    bottom = (lane == 0) | (lane == LEVELS) | (lane == 2 * LEVELS)
     now, later = lam_a, lam_b
     for step in range(1, 5):
         reach = HALO - step
         count = ROWS + 2 * reach
         base = wind_index(step, 0)
-        lhs = wide_s[base : base + count].reshape(count * cols, lanes)
-        coef_s[:count] = jnp.dot(lhs, spread, preferred_element_type=F32).reshape(count, cols, 2 * lanes)
+        lhs = wide_s[base : base + count].reshape(count * cols, WIDE)
+        coef_s[base : base + count] = jnp.dot(lhs, spread, preferred_element_type=F32).reshape(count, cols, 2 * WIDE)
         for row in range(-reach, ROWS + reach):
-            at = ext_index(row)
-            mid = now[at]
-            north = now[ext_index(row + 1)]
-            south = now[ext_index(row - 1)]
-            east = pltpu.roll(mid, cols - 1, 0)
-            west = pltpu.roll(mid, 1, 0)
-            upper = pltpu.roll(mid, lanes - 1, 1)
-            if top is not None:
-                upper = jnp.where(top, mid, upper)
-            lower = jnp.where(bottom, mid, pltpu.roll(mid, 1, 1))
-            place = wind_index(step, row) - base
-            u = coef_s[place, :, :lanes]
-            v = coef_s[place, :, lanes:]
-            new = (
-                CENTER * mid
-                + u * (east - west)
-                + v * (north - south)
-                + HORIZ_MIX * ((east + west) + (north + south))
-                + VERT_MIX * (upper + lower)
+            place = wind_index(step, row)
+            new = updated(
+                now[ext_index(row)], now[ext_index(row + 1)], now[ext_index(row - 1)],
+                coef_s[place, :, :WIDE], coef_s[place, :, WIDE:], top, bottom,
             )
             if row < 0:
                 new = new * has_south
             if row >= ROWS:
                 new = new * has_north
             if step < 4:
-                later[at] = new
-            if 0 <= row < ROWS:
-                emit(step, row, new)
+                later[ext_index(row)] = new
+            else:
+                field_ref[row] = new[:ROWS, :WIDTH]
         now, later = later, now
+
+
+GROUP = EXT // 4
+SPECIES_LANES = 8
+
+
+def low_levels(tile):
+    lane = iota((8, 128), 1)
+    first = tile[:, :128]
+    low = jnp.where(
+        lane < SPECIES_LANES,
+        first,
+        jnp.where(lane < 2 * SPECIES_LANES, pltpu.roll(first, 128 - LEVELS + SPECIES_LANES, 1), tile[:, 128:]),
+    )
+    return jnp.where(lane < SPECIES * SPECIES_LANES, low, 0.0)
 
 
 def assemble_low(refs, lam_s, wide_s):
@@ -405,21 +410,25 @@
     for strip in (from_south, from_north):
         halves = [strip[i].astype(F32) for i in range(STRIP)]
         halos.append((*unpack_strip(halves), halves[9][8:16], halves[10][8:16]))
+    held = [[jnp.zeros((8, 128), F32)] * 2 for _ in range(GROUP)]
     for row in range(-HALO, ROWS + HALO):
         own = 0 <= row < ROWS
-        at = ext_index(row)
+        group, at = divmod(row + HALO, GROUP)
         if own:
-            lam = pack_low(lam_ref[row])
+            lam = lam_ref[row]
             sides = edge_winds(from_cross, from_sibling, row)
         else:
             lam_rows, wind_rows, east, west = halos[0 if row < 0 else 1]
-            lam = pack_low(lam_rows[row + HALO if row < 0 else row - ROWS])
-        lam_s[at, 0:8] = lam[0:8]
-        lam_s[at, 8:16] = jnp.where(sub < 4, lam[8:16], 0.0)
-        lam_s[at, 16:24] = jnp.zeros((8, 128), F32)
+            lam = lam_rows[row + HALO if row < 0 else row - ROWS]
+        for tile in range(2):
+            low = low_levels(lam[8 * tile : 8 * tile + 8])
+            held[at][tile] = held[at][tile] + (pltpu.roll(low, 32 * group, 1) if group else low)
+        lanes = slice(128 * group, 128 * group + 128)
         for step in range(1, 5):
             reach = HALO - step
+            place = (step - 1) * GROUP + at
             if not -reach <= row < ROWS + reach:
+                wide_s[place, :, lanes] = jnp.zeros((SUB + 8, 128), BF16)
                 continue
             if own:
                 wind = winds_ref[4 - step, row, :, :128].astype(F32)
@@ -428,31 +437,65 @@
                 index = WIND_FIRST[step] + (row + reach if row < 0 else row - ROWS)
                 wind = wind_rows[index][:, :128]
                 east_wind, west_wind = (pltpu.roll(side, 128 - 4 * index, 1) if index else side for side in (east, west))
-            place = wind_index(step, row)
-            wide_s[place, 0:16] = jnp.concatenate(
+            wide_s[place, 0:16, lanes] = jnp.concatenate(
                 [wind[0:8], jnp.where(sub < 4, wind[8:16], east_wind)], axis=0
             ).astype(BF16)
-            wide_s[place, 16:24] = west_wind.astype(BF16)
+            wide_s[place, 16:24, lanes] = west_wind.astype(BF16)
+    for at in range(GROUP):
+        lam_s[at, 0:8] = held[at][0]
+        lam_s[at, 8:16] = jnp.where(sub < 4, held[at][1], 0.0)
+        lam_s[at, 16:24] = jnp.zeros((8, 128), F32)
+
+
+def low_spread():
+    source = iota((4 * 128, 2 * 128), 0)
+    lane = iota((4 * 128, 2 * 128), 1)
+    level = lane & (SPECIES_LANES - 1)
+    wanted = ((lane & 127) >> 5) * 128 + level + jnp.where(lane >= 128, LEVELS, 0)
+    match = (source == wanted) & (level < 4) & ((lane & 31) < SPECIES * SPECIES_LANES)
+    return jnp.where(match, 0.5, 0.0).astype(BF16)
+
+
+def advance_low(lam_a, lam_b, wide_s, coef_s, acc_s):
+    has_south, has_north = poles()
+    cols = SUB + 8
+    spread = low_spread()
+    lane = iota((cols, 128), 1)
+    bottom = (lane & (SPECIES_LANES - 1)) == 0
+    lhs = wide_s[...].reshape(4 * GROUP * cols, 4 * 128)
+    coef_s[...] = jnp.dot(lhs, spread, preferred_element_type=F32).reshape(4 * GROUP, cols, 2 * 128)
+    now, later = lam_a, lam_b
+    for step in range(1, 5):
+        for at in range(GROUP):
+            place = (step - 1) * GROUP + at
+            north = now[at + 1] if at < GROUP - 1 else pltpu.roll(now[0], 96, 1)
+            south = now[at - 1] if at else pltpu.roll(now[GROUP - 1], 32, 1)
+            new = updated(now[at], north, south, coef_s[place, :, :128], coef_s[place, :, 128:], None, bottom)
+            if at < HALO:
+                new = jnp.where(lane < 32, new * has_south, new)
+            if at > 0:
+                new = jnp.where(lane >= 96, new * has_north, new)
+            later[at] = new
+            acc_s[at] = new if step == 1 else acc_s[at] + new
+        now, later = later, now
 
 
 LOW = WIDTH // 6
 
 
 def surface_body(
-    lam_ref, from_south, from_north, winds_ref, from_cross, from_sibling, out_ref, lam_a, lam_b, wide_s, coef_s, acc_s
+    lam_ref, from_south, from_north, winds_ref, from_cross, from_sibling, _, out_ref, lam_a, lam_b, wide_s, coef_s, acc_s
 ):
     assemble_low((lam_ref, from_south, from_north, winds_ref, from_cross, from_sibling), lam_a, wide_s)
-
-    def emit(step, row, value):
-        acc_s[row] = value if step == 1 else acc_s[row] + value
-
-    advance(lam_a, lam_b, wide_s, coef_s, True, emit)
+    advance_low(lam_a, lam_b, wide_s, coef_s, acc_s)
     lane = iota((SUB + 8, 128), 1)
     surface = jnp.zeros((SUB + 8, 128), F32)
     for row in range(ROWS):
-        held = acc_s[row]
-        for species, source in enumerate((0, LEVELS, 16)):
+        group, place = divmod(row + HALO, GROUP)
+        held = acc_s[place]
+        for species in range(SPECIES):
             at = row * SPECIES + species
+            source = 32 * group + SPECIES_LANES * species
             surface = jnp.where(lane == at, pltpu.roll(held, (at - source) % 128, 1), surface)
     high = surface.astype(BF16).astype(F32)
     low = (surface - high).astype(BF16).astype(F32)
@@ -471,12 +514,7 @@
 def steps_body(lam_ref, winds_ref, from_cross, from_sibling, field_ref, lam_a, lam_b, wide_s, coef_s):
     refs = (lam_ref, winds_ref, from_cross, from_sibling)
     assemble(refs, lam_a, wide_s)
-
-    def emit(step, row, value):
-        if step == 4:
-            field_ref[row] = value[:ROWS, :WIDTH]
-
-    advance(lam_a, lam_b, wide_s, coef_s, False, emit)
+    advance(lam_a, lam_b, wide_s, coef_s, field_ref)
 
 
 def correlation_body(correlation_ref, out_ref):
@@ -563,28 +601,27 @@
     from_south = lax.ppermute(north, "lat", up)
     from_north = lax.ppermute(south, "lat", down)
     cols = SUB + 8
-
-    def scratch(lanes):
-        return [
-            pltpu.VMEM((EXT, cols, lanes), F32),
-            pltpu.VMEM((EXT, cols, lanes), F32),
-            pltpu.VMEM((60, cols, lanes), BF16),
-            pltpu.VMEM((EXT, cols, 2 * lanes), F32),
-        ]
-
+    vmem = pl.BlockSpec(memory_space=pltpu.VMEM)
     surface = vmem_call(
         surface_body,
         shape((lon_count * SUB, 128), BF16),
-        scratch(128) + [pltpu.VMEM((ROWS, cols, 128), F32)],
+        [
+            pltpu.VMEM((GROUP, cols, 128), F32),
+            pltpu.VMEM((GROUP, cols, 128), F32),
+            pltpu.VMEM((4 * GROUP, cols, 4 * 128), BF16),
+            pltpu.VMEM((4 * GROUP, cols, 2 * 128), F32),
+            pltpu.VMEM((GROUP, cols, 128), F32),
+        ],
         name="surface",
-    )(lam, from_south, from_north, winds, winds_cross, winds_sibling)
+        in_specs=[vmem] * 6 + [pl.BlockSpec(memory_space=pl.ANY)],
+    )(lam, from_south, from_north, winds, winds_cross, winds_sibling, turned)
     gathered = lax.all_to_all(surface, "lon", split_axis=0, concat_axis=0, tiled=True)
     edge = shape((EXT // 2, SUB, WIDE), BF16)
     to_sibling, to_cross, lam_ext, winds_ext = vmem_call(
         edge_body,
         (edge, edge, shape((EXT, SUB, WIDE), F32), shape((60, SUB, WIDE), BF16)),
         name="edge",
-        in_specs=[pl.BlockSpec(memory_space=pltpu.VMEM)] * 4 + [pl.BlockSpec(memory_space=pl.ANY)],
+        in_specs=[vmem] * 4 + [pl.BlockSpec(memory_space=pl.ANY)],
     )(lam, from_south, from_north, winds, surface)
     from_cross = lax.ppermute(to_cross, "lon", across)
     from_sibling = lax.ppermute(to_sibling, "lon", within)
@@ -598,7 +635,12 @@
     field = vmem_call(
         steps_body,
         shape((ROWS, ROWS, WIDTH), F32),
-        scratch(WIDE),
+        [
+            pltpu.VMEM((EXT, cols, WIDE), F32),
+            pltpu.VMEM((EXT, cols, WIDE), F32),
+            pltpu.VMEM((60, cols, WIDE), BF16),
+            pltpu.VMEM((60, cols, 2 * WIDE), F32),
+        ],
         name="steps",
     )(*state)
     return field, gradient

time: 63.1 us -> 63 us (level)
  no operation moved by 1% of the time
where the time goes in v5:
time: 63 us; the launch traced here: 62.6 us
  starting transfers between devices  48.7 us (77%)
  Pallas kernels  7.66 us (12%)
  waiting for transfers between devices  5.39 us (9%)
  between operations  0.76 us (1%)
    ppermute x1, starting transfers between devices, per_device(): from_north = lax.ppermute(south, 'lat', down)  15.8 us
    all_to_all x1, starting transfers between devices, per_device(): recv = lax.all_to_all(sent, 'lon', split_axis=0, concat_axis=0, tiled=True)  9.19 us
    all_to_all x1, starting transfers between devices, per_device(): lax.all_to_all(surface, 'lon', split_axis=0, concat_axis=0, tiled=True)  6.03 us
    ppermute x1, starting transfers between devices, per_device(): from_south = lax.ppermute(north, 'lat', up)  5.19 us
    ppermute x1, starting transfers between devices, per_device(): winds_cross = lax.ppermute(rim_cross, 'lon', across)  4.33 us
    ppermute x1, starting transfers between devices, per_device(): from_cross = lax.ppermute(to_cross, 'lon', across)  4.33 us
    pallas_call x1, Pallas kernels, per_device(): vmem_call(steps_body, shape((ROWS, ROWS, WIDTH), F32), [pltpu.VMEM((EXT,...  2.1 us
    pallas_call x1, Pallas kernels, per_device(): vmem_call(route_body, shape((lon_count * CAP, WIDE), BF16), [pltpu.VMEM((...  1.98 us
  transfers between devices with their start and end apart: 8, of which 6 were waited for; matrix products, arithmetic and copies ran while one was open for 0% of the time, Pallas kernels for 4%

profile of v5, /device:TPU:14, one launch (start us, length us, event | category | flops | bytes accessed | tf_op | source)
XLA Modules:
  0.0 62.6 jit_solution(13468179490446014707)
XLA Ops:
  0.6 0.0 copy-start.3
  0.6 2.0 %route.1 = bf16[256,256]{1,0:T(8,128)(2,1)} custom-call(s32[1,1,32]{2,1,0:T(1,128)} %counts_hbm.1, s32[1,1,32]{2,1,0:T(1,128)} %offsets_hbm.1, s32[1,1,256]{2,1,0:T(1,128)} %columns_hbm.1, s32[1,1,256]{2,1,0:T(1,128)} %kernels_hbm.1, bf16[1,1,216,256]{3,2,1,0:T(8,128)(2,1)} %bitcast.10), custom_call_target="tpu_custom_call" | custom-call | tf_op jit(solution)/shard_map/route/pallas_call | solution.py:567
  2.6 9.2 %all-to-all-start = ((bf16[32,8,256]{2,1,0:T(8,128)(2,1)}), bf16[32,8,256]{2,1,0:T(8,128)(2,1)S(1)}, u32[]{:S(2)}, u32[]{:S(2)}) async-start(bf16[32,8,256]{2,1,0:T(8,128)(2,1)} %bitcast.9), calls=%async_computation | async-start | bytes 262144 | tf_op jit(solution)/shard_map/all_to_all | solution.py:582
  11.8 0.0 copy-done.3
  11.9 0.0 copy-start
  11.9 0.0 copy-start.1
  11.9 0.2 winds.1
  12.1 4.3 %collective-permute-start = (bf16[16,128]{1,0:T(8,128)(2,1)S(1)}, bf16[16,128]{1,0:T(8,128)(2,1)S(1)}, u32[]{:S(2)}, u32[]{:S(2)}) collective-permute-start(bf16[16,128]{1,0:T(8,128)(2,1)S(1)} %get-tuple-element.13), channel_id=1, source_target_pairs={{0,992},{32,64},{64,32},{96,128},{128,96},{160,192},{192,160},{224... | collective-permute-start | bytes 12296 | tf_op jit(solution)/shard_map/ppermute | solution.py:589
  16.4 1.9 %collective-permute-start.1 = (bf16[16,128]{1,0:T(8,128)(2,1)S(1)}, bf16[16,128]{1,0:T(8,128)(2,1)S(1)}, u32[]{:S(2)}, u32[]{:S(2)}) collective-permute-start(bf16[16,128]{1,0:T(8,128)(2,1)S(1)} %get-tuple-element.14), channel_id=1, source_target_pairs={{0,32},{32,0},{64,96},{96,64},{128,160},{160,128},{192,224},{224,1... | collective-permute-start | bytes 12296 | tf_op jit(solution)/shard_map/ppermute | solution.py:590
  18.4 0.8 %collective-permute-done.from_cross = bf16[16,128]{1,0:T(8,128)(2,1)S(1)} collective-permute-done((bf16[16,128]{1,0:T(8,128)(2,1)S(1)}, bf16[16,128]{1,0:T(8,128)(2,1)S(1)}, u32[]{:S(2)}, u32[]{:S(2)}) %collective-permute-start) | collective-permute-done | bytes 4128 | tf_op jit(solution)/shard_map/ppermute | solution.py:589
  19.1 0.3 collective-permute-done.1.from_sibling
  19.5 1.0 %all-to-all-done = bf16[32,8,256]{2,1,0:T(8,128)(2,1)S(1)} async-done(((bf16[32,8,256]{2,1,0:T(8,128)(2,1)}), bf16[32,8,256]{2,1,0:T(8,128)(2,1)S(1)}, u32[]{:S(2)}, u32[]{:S(2)}) %all-to-all-start) | async-done | bytes 131104 | tf_op jit(solution)/shard_map/all_to_all | solution.py:582
  20.5 0.0 copy-done
  20.5 0.0 copy-done.1
  20.5 0.0 copy-start.2
  20.5 0.5 force.1
  21.0 5.2 %collective-permute-start.2 = (bf16[11,16,128]{2,1,0:T(8,128)(2,1)S(1)}, bf16[11,16,128]{2,1,0:T(8,128)(2,1)S(1)}, u32[]{:S(2)}, u32[]{:S(2)}) collective-permute-start(bf16[11,16,128]{2,1,0:T(8,128)(2,1)S(1)} %get-tuple-element.16), channel_id=1, source_target_pairs={{0,1},{1,2},{2,3},{3,4},{4,5},{5,6},{6,7},{7,8},{8,9},{9,10},{10,1... | collective-permute-start | bytes 135176 | tf_op jit(solution)/shard_map/ppermute | solution.py:601
  26.2 15.8 %collective-permute-start.3 = (bf16[11,16,128]{2,1,0:T(8,128)(2,1)S(1)}, bf16[11,16,128]{2,1,0:T(8,128)(2,1)S(1)}, u32[]{:S(2)}, u32[]{:S(2)}) collective-permute-start(bf16[11,16,128]{2,1,0:T(8,128)(2,1)S(1)} %get-tuple-element.17), channel_id=1, source_target_pairs={{1,0},{2,1},{3,2},{4,3},{5,4},{6,5},{7,6},{8,7},{9,8},{10,9},{11,1... | collective-permute-start | bytes 135176 | tf_op jit(solution)/shard_map/ppermute | solution.py:602
  42.0 0.0 copy-done.2
  42.0 0.2 correlation.1._.correlation_ref
  42.2 0.7 %collective-permute-done.2.from_south = bf16[11,16,128]{2,1,0:T(8,128)(2,1)S(1)} collective-permute-done((bf16[11,16,128]{2,1,0:T(8,128)(2,1)S(1)}, bf16[11,16,128]{2,1,0:T(8,128)(2,1)S(1)}, u32[]{:S(2)}, u32[]{:S(2)}) %collective-permute-start.2) | collective-permute-done | bytes 45088 | tf_op jit(solution)/shard_map/ppermute | solution.py:601
  43.0 0.7 %collective-permute-done.3.from_north = bf16[11,16,128]{2,1,0:T(8,128)(2,1)S(1)} collective-permute-done((bf16[11,16,128]{2,1,0:T(8,128)(2,1)S(1)}, bf16[11,16,128]{2,1,0:T(8,128)(2,1)S(1)}, u32[]{:S(2)}, u32[]{:S(2)}) %collective-permute-start.3) | collective-permute-done | bytes 45088 | tf_op jit(solution)/shard_map/ppermute | solution.py:602
  43.7 1.5 %surface.1._ = bf16[512,128]{1,0:T(8,128)(2,1)} custom-call(f32[12,16,256]{2,1,0:T(8,128)S(1)} %get-tuple-element.15.lam_ref, bf16[11,16,128]{2,1,0:T(8,128)(2,1)S(1)} %collective-permute-done.2.from_south, bf16[11,16,128]{2,1,0:T(8,128)(2,1)S(1)} %collective-permute-done.3.from_north, bf16[4,12,16,256]{3,2,1,0:T(8,128)(2,1)S(1)} %get-tuple-element.12.winds_ref, ...), custom_call_target="tpu_custom_call" | custom-call | tf_op jit(solution)/shard_map/surface/pallas_call | solution.py:605
  45.2 6.0 %all-to-all-start.1 = ((bf16[32,16,128]{2,1,0:T(8,128)(2,1)}), bf16[32,16,128]{2,1,0:T(8,128)(2,1)S(1)}, u32[]{:S(2)}, u32[]{:S(2)}) async-start(bf16[32,16,128]{2,1,0:T(8,128)(2,1)} %bitcast.4), calls=%async_computation.1 | async-start | bytes 262144 | tf_op jit(solution)/shard_map/all_to_all | solution.py:618
  51.2 0.2 edge.1
  51.4 4.3 %collective-permute-start.4 = (bf16[10,16,256]{2,1,0:T(8,128)(2,1)S(1)}, bf16[10,16,256]{2,1,0:T(8,128)(2,1)S(1)}, u32[]{:S(2)}, u32[]{:S(2)}) collective-permute-start(bf16[10,16,256]{2,1,0:T(8,128)(2,1)S(1)} %get-tuple-element.20), channel_id=1, source_target_pairs={{0,992},{32,64},{64,32},{96,128},{128,96},{160,192},{192,160},{224... | collective-permute-start | bytes 245768 | tf_op jit(solution)/shard_map/ppermute | solution.py:626
  55.7 1.9 %collective-permute-start.5 = (bf16[10,16,256]{2,1,0:T(8,128)(2,1)S(1)}, bf16[10,16,256]{2,1,0:T(8,128)(2,1)S(1)}, u32[]{:S(2)}, u32[]{:S(2)}) collective-permute-start(bf16[10,16,256]{2,1,0:T(8,128)(2,1)S(1)} %get-tuple-element.21), channel_id=1, source_target_pairs={{0,32},{32,0},{64,96},{96,64},{128,160},{160,128},{192,224},{224,1... | collective-permute-start | bytes 245768 | tf_op jit(solution)/shard_map/ppermute | solution.py:627
  57.7 1.7 %collective-permute-done.4.from_cross = bf16[10,16,256]{2,1,0:T(8,128)(2,1)S(1)} collective-permute-done((bf16[10,16,256]{2,1,0:T(8,128)(2,1)S(1)}, bf16[10,16,256]{2,1,0:T(8,128)(2,1)S(1)}, u32[]{:S(2)}, u32[]{:S(2)}) %collective-permute-start.4) | collective-permute-done | bytes 81952 | tf_op jit(solution)/shard_map/ppermute | solution.py:626
  59.4 0.0 collective-permute-done.5.from_sibling
  59.4 2.1 %steps.1 = f32[12,12,216]{2,1,0:T(8,128)} custom-call(f32[20,16,256]{2,1,0:T(8,128)S(1)} %get-tuple-element.18.lam_ref, bf16[60,16,256]{2,1,0:T(8,128)(2,1)S(1)} %get-tuple-element.19.winds_ref, bf16[10,16,256]{2,1,0:T(8,128)(2,1)S(1)} %collective-permute-done.4.from_cross, bf16[10,16,256]{2,1,0:T(8,128)(2,1)S(1)} %collective-permute-done.5.from_sibling), custom_call_target="tpu_custom_call" | custom-call | tf_op jit(solution)/shard_map/steps/pallas_call | solution.py:635
  61.5 0.0 all-to-all-done.1
  61.5 1.1 %gradient.1 = f32[12,3,12]{2,1,0:T(4,128)} custom-call(bf16[512,128]{1,0:T(8,128)(2,1)S(1)} %bitcast.7, bf16[32,256]{1,0:T(8,128)(2,1)S(1)} %correlation.1._.correlation_ref), custom_call_target="tpu_custom_call" | custom-call | tf_op jit(solution)/shard_map/gradient/pallas_call | solution.py:629
  (1 shorter events, 0.0 us)
Async XLA Ops:
  0.6 11.2 %copy-start.3 = (bf16[4,12,12,144]{3,0,2,1:T(4,128)(2,1)S(1)}, bf16[4,12,12,144]{3,0,2,1:T(4,128)(2,1)}, u32[]{:S(2)}) copy-start(bf16[4,12,12,144]{3,0,2,1:T(4,128)(2,1)} %param.10) | copy-start | bytes 497668
  2.6 17.9 %all-to-all-start = ((bf16[32,8,256]{2,1,0:T(8,128)(2,1)}), bf16[32,8,256]{2,1,0:T(8,128)(2,1)S(1)}, u32[]{:S(2)}, u32[]{:S(2)}) async-start(bf16[32,8,256]{2,1,0:T(8,128)(2,1)} %bitcast.9), calls=%async_computation | async-start | bytes 262144 | tf_op jit(solution)/shard_map/all_to_all | solution.py:582
  11.9 8.6 %copy-start = (f32[12,12,216]{2,1,0:T(8,128)S(1)}, f32[12,12,216]{2,1,0:T(8,128)}, u32[]{:S(2)}) copy-start(f32[12,12,216]{2,1,0:T(8,128)} %adjoint_ref.1) | copy-start | bytes 373252
  11.9 8.6 %copy-start.1 = (f32[64,216]{1,0:T(8,128)S(1)}, f32[64,216]{1,0:T(8,128)}, u32[]{:S(2)}) copy-start(f32[64,216]{1,0:T(8,128)} %table_ref.1) | copy-start | bytes 165892
  12.1 7.1 %collective-permute-start = (bf16[16,128]{1,0:T(8,128)(2,1)S(1)}, bf16[16,128]{1,0:T(8,128)(2,1)S(1)}, u32[]{:S(2)}, u32[]{:S(2)}) collective-permute-start(bf16[16,128]{1,0:T(8,128)(2,1)S(1)} %get-tuple-element.13), channel_id=1, source_target_pairs={{0,992},{32,64},{64,32},{96,128},{128,96},{160,192},{192,160},{224... | collective-permute-start | bytes 12296 | tf_op jit(solution)/shard_map/ppermute | solution.py:589
  16.4 3.1 %collective-permute-start.1 = (bf16[16,128]{1,0:T(8,128)(2,1)S(1)}, bf16[16,128]{1,0:T(8,128)(2,1)S(1)}, u32[]{:S(2)}, u32[]{:S(2)}) collective-permute-start(bf16[16,128]{1,0:T(8,128)(2,1)S(1)} %get-tuple-element.14), channel_id=1, source_target_pairs={{0,32},{32,0},{64,96},{96,64},{128,160},{160,128},{192,224},{224,1... | collective-permute-start | bytes 12296 | tf_op jit(solution)/shard_map/ppermute | solution.py:590
  20.5 21.5 %copy-start.2 = (bf16[384,12]{0,1:T(8,128)(2,1)S(1)}, bf16[384,12]{0,1:T(8,128)(2,1)}, u32[]{:S(2)}) copy-start(bf16[384,12]{0,1:T(8,128)(2,1)} %param.17) | copy-start | bytes 27652
  21.0 21.9 %collective-permute-start.2 = (bf16[11,16,128]{2,1,0:T(8,128)(2,1)S(1)}, bf16[11,16,128]{2,1,0:T(8,128)(2,1)S(1)}, u32[]{:S(2)}, u32[]{:S(2)}) collective-permute-start(bf16[11,16,128]{2,1,0:T(8,128)(2,1)S(1)} %get-tuple-element.16), channel_id=1, source_target_pairs={{0,1},{1,2},{2,3},{3,4},{4,5},{5,6},{6,7},{7,8},{8,9},{9,10},{10,1... | collective-permute-start | bytes 135176 | tf_op jit(solution)/shard_map/ppermute | solution.py:601
  26.2 17.5 %collective-permute-start.3 = (bf16[11,16,128]{2,1,0:T(8,128)(2,1)S(1)}, bf16[11,16,128]{2,1,0:T(8,128)(2,1)S(1)}, u32[]{:S(2)}, u32[]{:S(2)}) collective-permute-start(bf16[11,16,128]{2,1,0:T(8,128)(2,1)S(1)} %get-tuple-element.17), channel_id=1, source_target_pairs={{1,0},{2,1},{3,2},{4,3},{5,4},{6,5},{7,6},{8,7},{9,8},{10,9},{11,1... | collective-permute-start | bytes 135176 | tf_op jit(solution)/shard_map/ppermute | solution.py:602
  45.2 16.3 %all-to-all-start.1 = ((bf16[32,16,128]{2,1,0:T(8,128)(2,1)}), bf16[32,16,128]{2,1,0:T(8,128)(2,1)S(1)}, u32[]{:S(2)}, u32[]{:S(2)}) async-start(bf16[32,16,128]{2,1,0:T(8,128)(2,1)} %bitcast.4), calls=%async_computation.1 | async-start | bytes 262144 | tf_op jit(solution)/shard_map/all_to_all | solution.py:618
  51.4 8.0 %collective-permute-start.4 = (bf16[10,16,256]{2,1,0:T(8,128)(2,1)S(1)}, bf16[10,16,256]{2,1,0:T(8,128)(2,1)S(1)}, u32[]{:S(2)}, u32[]{:S(2)}) collective-permute-start(bf16[10,16,256]{2,1,0:T(8,128)(2,1)S(1)} %get-tuple-element.20), channel_id=1, source_target_pairs={{0,992},{32,64},{64,32},{96,128},{128,96},{160,192},{192,160},{224... | collective-permute-start | bytes 245768 | tf_op jit(solution)/shard_map/ppermute | solution.py:626
  55.7 3.7 %collective-permute-start.5 = (bf16[10,16,256]{2,1,0:T(8,128)(2,1)S(1)}, bf16[10,16,256]{2,1,0:T(8,128)(2,1)S(1)}, u32[]{:S(2)}, u32[]{:S(2)}) collective-permute-start(bf16[10,16,256]{2,1,0:T(8,128)(2,1)S(1)} %get-tuple-element.21), channel_id=1, source_target_pairs={{0,32},{32,0},{64,96},{96,64},{128,160},{160,128},{192,224},{224,1... | collective-permute-start | bytes 245768 | tf_op jit(solution)/shard_map/ppermute | solution.py:627

commit v6 on v5

--- a/solution.py
+++ b/solution.py
@@ -41,8 +41,8 @@
 
 
 def route_body(
-    counts_hbm, offsets_hbm, columns_hbm, kernels_hbm, innov_hbm, out_ref,
-    counts_s, offsets_s, columns_s, kernels_s, innov_s, sems,
+    counts_hbm, offsets_hbm, columns_hbm, kernels_hbm, innov_hbm, out_hbm,
+    counts_s, offsets_s, columns_s, kernels_s, innov_s, sent_s, sems, out_sems,
 ):
     moves = (
         (counts_hbm.at[0], counts_s),
@@ -75,13 +75,22 @@
         jnp.where(line == KERNEL_LANE - half, kernels_s[...].astype(F32), 0.0),
     ).astype(BF16)
     tail = lax.dot_general(pick, codes, (((1,), (1,)), ((), ())), preferred_element_type=F32)
-    out_ref[:, half:] = tail.astype(BF16)
+    sent_s[:, half:] = tail.astype(BF16)
     copies[4].wait()
-    sent = lax.dot_general(
-        pick, innov_s[...], (((1,), (1,)), ((), ())), preferred_element_type=F32
-    ).astype(BF16)
-    out_ref[:, :half] = sent[:, :half]
-    out_ref[:, half:WIDTH] = sent[:, half:]
+    size = pick.shape[0] // 2
+    outs = []
+    for part in range(2):
+        rows = slice(part * size, part * size + size)
+        sent = lax.dot_general(
+            pick[rows], innov_s[...], (((1,), (1,)), ((), ())), preferred_element_type=F32
+        ).astype(BF16)
+        sent_s[rows, :half] = sent[:, :half]
+        sent_s[rows, half:WIDTH] = sent[:, half:]
+        span = pl.ds(part * size, size)
+        outs.append(pltpu.make_async_copy(sent_s.at[span], out_hbm.at[span], out_sems.at[part]))
+        outs[part].start()
+    for copy in outs:
+        copy.wait()
 
 
 def pack_levels(tiles):
@@ -573,9 +582,12 @@
             pltpu.VMEM((1, held), jnp.int32),
             pltpu.VMEM((1, held), jnp.int32),
             pltpu.VMEM((WIDTH, held), BF16),
+            pltpu.VMEM((lon_count * CAP, WIDE), BF16),
             pltpu.SemaphoreType.DMA((5,)),
+            pltpu.SemaphoreType.DMA((2,)),
         ],
         name="route",
+        out_specs=pl.BlockSpec(memory_space=pltpu.HBM),
         limit=63 * 1000 * 1000,
         in_specs=[pl.BlockSpec(memory_space=pltpu.HBM)] * 5,
     )(counts, offsets, columns, kernel_ids, jnp.swapaxes(innovations, 2, 3))

time: 63 us -> 63 us (level)
  no operation moved by 1% of the time
where the time goes in v6:
time: 63 us; the launch traced here: 62.6 us
  starting transfers between devices  48.7 us (77%)
  Pallas kernels  7.64 us (12%)
  waiting for transfers between devices  5.39 us (9%)
  between operations  0.76 us (1%)
    ppermute x1, starting transfers between devices, per_device(): from_north = lax.ppermute(south, 'lat', down)  15.8 us
    all_to_all x1, starting transfers between devices, per_device(): recv = lax.all_to_all(sent, 'lon', split_axis=0, concat_axis=0, tiled=True)  9.19 us
    all_to_all x1, starting transfers between devices, per_device(): lax.all_to_all(surface, 'lon', split_axis=0, concat_axis=0, tiled=True)  6.03 us
    ppermute x1, starting transfers between devices, per_device(): from_south = lax.ppermute(north, 'lat', up)  5.19 us
    ppermute x1, starting transfers between devices, per_device(): winds_cross = lax.ppermute(rim_cross, 'lon', across)  4.33 us
    ppermute x1, starting transfers between devices, per_device(): from_cross = lax.ppermute(to_cross, 'lon', across)  4.33 us
    pallas_call x1, Pallas kernels, per_device(): vmem_call(steps_body, shape((ROWS, ROWS, WIDTH), F32), [pltpu.VMEM((EXT,...  2.1 us
    pallas_call x1, Pallas kernels, per_device(): vmem_call(route_body, shape((lon_count * CAP, WIDE), BF16), [pltpu.VMEM((...  1.97 us
  transfers between devices with their start and end apart: 8, of which 6 were waited for; matrix products, arithmetic and copies ran while one was open for 0% of the time, Pallas kernels for 4%

profile of v6, /device:TPU:14, one launch (start us, length us, event | category | flops | bytes accessed | tf_op | source)
XLA Modules:
  0.0 62.6 jit_solution(13781472705276012503)
XLA Ops:
  0.6 0.0 copy-start.3
  0.6 2.0 %route.1 = bf16[256,256]{1,0:T(8,128)(2,1)} custom-call(s32[1,1,32]{2,1,0:T(1,128)} %counts_hbm.1, s32[1,1,32]{2,1,0:T(1,128)} %offsets_hbm.1, s32[1,1,256]{2,1,0:T(1,128)} %columns_hbm.1, s32[1,1,256]{2,1,0:T(1,128)} %kernels_hbm.1, bf16[1,1,216,256]{3,2,1,0:T(8,128)(2,1)} %bitcast.10), custom_call_target="tpu_custom_call" | custom-call | tf_op jit(solution)/shard_map/route/pallas_call | solution.py:576
  2.6 9.2 %all-to-all-start = ((bf16[32,8,256]{2,1,0:T(8,128)(2,1)}), bf16[32,8,256]{2,1,0:T(8,128)(2,1)S(1)}, u32[]{:S(2)}, u32[]{:S(2)}) async-start(bf16[32,8,256]{2,1,0:T(8,128)(2,1)} %bitcast.9), calls=%async_computation | async-start | bytes 262144 | tf_op jit(solution)/shard_map/all_to_all | solution.py:594
  11.8 0.0 copy-done.3
  11.9 0.0 copy-start
  11.9 0.0 copy-start.1
  11.9 0.2 winds.1
  12.1 4.3 %collective-permute-start = (bf16[16,128]{1,0:T(8,128)(2,1)S(1)}, bf16[16,128]{1,0:T(8,128)(2,1)S(1)}, u32[]{:S(2)}, u32[]{:S(2)}) collective-permute-start(bf16[16,128]{1,0:T(8,128)(2,1)S(1)} %get-tuple-element.13), channel_id=1, source_target_pairs={{0,992},{32,64},{64,32},{96,128},{128,96},{160,192},{192,160},{224... | collective-permute-start | bytes 12296 | tf_op jit(solution)/shard_map/ppermute | solution.py:601
  16.4 1.9 %collective-permute-start.1 = (bf16[16,128]{1,0:T(8,128)(2,1)S(1)}, bf16[16,128]{1,0:T(8,128)(2,1)S(1)}, u32[]{:S(2)}, u32[]{:S(2)}) collective-permute-start(bf16[16,128]{1,0:T(8,128)(2,1)S(1)} %get-tuple-element.14), channel_id=1, source_target_pairs={{0,32},{32,0},{64,96},{96,64},{128,160},{160,128},{192,224},{224,1... | collective-permute-start | bytes 12296 | tf_op jit(solution)/shard_map/ppermute | solution.py:602
  18.3 0.8 %collective-permute-done.from_cross = bf16[16,128]{1,0:T(8,128)(2,1)S(1)} collective-permute-done((bf16[16,128]{1,0:T(8,128)(2,1)S(1)}, bf16[16,128]{1,0:T(8,128)(2,1)S(1)}, u32[]{:S(2)}, u32[]{:S(2)}) %collective-permute-start) | collective-permute-done | bytes 4128 | tf_op jit(solution)/shard_map/ppermute | solution.py:601
  19.1 0.3 collective-permute-done.1.from_sibling
  19.5 1.0 %all-to-all-done = bf16[32,8,256]{2,1,0:T(8,128)(2,1)S(1)} async-done(((bf16[32,8,256]{2,1,0:T(8,128)(2,1)}), bf16[32,8,256]{2,1,0:T(8,128)(2,1)S(1)}, u32[]{:S(2)}, u32[]{:S(2)}) %all-to-all-start) | async-done | bytes 131104 | tf_op jit(solution)/shard_map/all_to_all | solution.py:594
  20.5 0.0 copy-done
  20.5 0.0 copy-done.1
  20.5 0.0 copy-start.2
  20.5 0.5 force.1
  21.0 5.2 %collective-permute-start.2 = (bf16[11,16,128]{2,1,0:T(8,128)(2,1)S(1)}, bf16[11,16,128]{2,1,0:T(8,128)(2,1)S(1)}, u32[]{:S(2)}, u32[]{:S(2)}) collective-permute-start(bf16[11,16,128]{2,1,0:T(8,128)(2,1)S(1)} %get-tuple-element.16), channel_id=1, source_target_pairs={{0,1},{1,2},{2,3},{3,4},{4,5},{5,6},{6,7},{7,8},{8,9},{9,10},{10,1... | collective-permute-start | bytes 135176 | tf_op jit(solution)/shard_map/ppermute | solution.py:613
  26.2 15.8 %collective-permute-start.3 = (bf16[11,16,128]{2,1,0:T(8,128)(2,1)S(1)}, bf16[11,16,128]{2,1,0:T(8,128)(2,1)S(1)}, u32[]{:S(2)}, u32[]{:S(2)}) collective-permute-start(bf16[11,16,128]{2,1,0:T(8,128)(2,1)S(1)} %get-tuple-element.17), channel_id=1, source_target_pairs={{1,0},{2,1},{3,2},{4,3},{5,4},{6,5},{7,6},{8,7},{9,8},{10,9},{11,1... | collective-permute-start | bytes 135176 | tf_op jit(solution)/shard_map/ppermute | solution.py:614
  42.0 0.0 copy-done.2
  42.0 0.2 correlation.1._.correlation_ref
  42.2 0.7 %collective-permute-done.2.from_south = bf16[11,16,128]{2,1,0:T(8,128)(2,1)S(1)} collective-permute-done((bf16[11,16,128]{2,1,0:T(8,128)(2,1)S(1)}, bf16[11,16,128]{2,1,0:T(8,128)(2,1)S(1)}, u32[]{:S(2)}, u32[]{:S(2)}) %collective-permute-start.2) | collective-permute-done | bytes 45088 | tf_op jit(solution)/shard_map/ppermute | solution.py:613
  43.0 0.7 %collective-permute-done.3.from_north = bf16[11,16,128]{2,1,0:T(8,128)(2,1)S(1)} collective-permute-done((bf16[11,16,128]{2,1,0:T(8,128)(2,1)S(1)}, bf16[11,16,128]{2,1,0:T(8,128)(2,1)S(1)}, u32[]{:S(2)}, u32[]{:S(2)}) %collective-permute-start.3) | collective-permute-done | bytes 45088 | tf_op jit(solution)/shard_map/ppermute | solution.py:614
  43.7 1.5 %surface.1._ = bf16[512,128]{1,0:T(8,128)(2,1)} custom-call(f32[12,16,256]{2,1,0:T(8,128)S(1)} %get-tuple-element.15.lam_ref, bf16[11,16,128]{2,1,0:T(8,128)(2,1)S(1)} %collective-permute-done.2.from_south, bf16[11,16,128]{2,1,0:T(8,128)(2,1)S(1)} %collective-permute-done.3.from_north, bf16[4,12,16,256]{3,2,1,0:T(8,128)(2,1)S(1)} %get-tuple-element.12.winds_ref, ...), custom_call_target="tpu_custom_call" | custom-call | tf_op jit(solution)/shard_map/surface/pallas_call | solution.py:617
  45.2 6.0 %all-to-all-start.1 = ((bf16[32,16,128]{2,1,0:T(8,128)(2,1)}), bf16[32,16,128]{2,1,0:T(8,128)(2,1)S(1)}, u32[]{:S(2)}, u32[]{:S(2)}) async-start(bf16[32,16,128]{2,1,0:T(8,128)(2,1)} %bitcast.4), calls=%async_computation.1 | async-start | bytes 262144 | tf_op jit(solution)/shard_map/all_to_all | solution.py:630
  51.2 0.2 edge.1
  51.4 4.3 %collective-permute-start.4 = (bf16[10,16,256]{2,1,0:T(8,128)(2,1)S(1)}, bf16[10,16,256]{2,1,0:T(8,128)(2,1)S(1)}, u32[]{:S(2)}, u32[]{:S(2)}) collective-permute-start(bf16[10,16,256]{2,1,0:T(8,128)(2,1)S(1)} %get-tuple-element.20), channel_id=1, source_target_pairs={{0,992},{32,64},{64,32},{96,128},{128,96},{160,192},{192,160},{224... | collective-permute-start | bytes 245768 | tf_op jit(solution)/shard_map/ppermute | solution.py:638
  55.7 1.9 %collective-permute-start.5 = (bf16[10,16,256]{2,1,0:T(8,128)(2,1)S(1)}, bf16[10,16,256]{2,1,0:T(8,128)(2,1)S(1)}, u32[]{:S(2)}, u32[]{:S(2)}) collective-permute-start(bf16[10,16,256]{2,1,0:T(8,128)(2,1)S(1)} %get-tuple-element.21), channel_id=1, source_target_pairs={{0,32},{32,0},{64,96},{96,64},{128,160},{160,128},{192,224},{224,1... | collective-permute-start | bytes 245768 | tf_op jit(solution)/shard_map/ppermute | solution.py:639
  57.6 1.7 %collective-permute-done.4.from_cross = bf16[10,16,256]{2,1,0:T(8,128)(2,1)S(1)} collective-permute-done((bf16[10,16,256]{2,1,0:T(8,128)(2,1)S(1)}, bf16[10,16,256]{2,1,0:T(8,128)(2,1)S(1)}, u32[]{:S(2)}, u32[]{:S(2)}) %collective-permute-start.4) | collective-permute-done | bytes 81952 | tf_op jit(solution)/shard_map/ppermute | solution.py:638
  59.4 0.0 collective-permute-done.5.from_sibling
  59.4 2.1 %steps.1 = f32[12,12,216]{2,1,0:T(8,128)} custom-call(f32[20,16,256]{2,1,0:T(8,128)S(1)} %get-tuple-element.18.lam_ref, bf16[60,16,256]{2,1,0:T(8,128)(2,1)S(1)} %get-tuple-element.19.winds_ref, bf16[10,16,256]{2,1,0:T(8,128)(2,1)S(1)} %collective-permute-done.4.from_cross, bf16[10,16,256]{2,1,0:T(8,128)(2,1)S(1)} %collective-permute-done.5.from_sibling), custom_call_target="tpu_custom_call" | custom-call | tf_op jit(solution)/shard_map/steps/pallas_call | solution.py:647
  61.5 0.0 all-to-all-done.1
  61.5 1.1 %gradient.1 = f32[12,3,12]{2,1,0:T(4,128)} custom-call(bf16[512,128]{1,0:T(8,128)(2,1)S(1)} %bitcast.7, bf16[32,256]{1,0:T(8,128)(2,1)S(1)} %correlation.1._.correlation_ref), custom_call_target="tpu_custom_call" | custom-call | tf_op jit(solution)/shard_map/gradient/pallas_call | solution.py:641
  (1 shorter events, 0.0 us)
Async XLA Ops:
  0.6 11.2 %copy-start.3 = (bf16[4,12,12,144]{3,0,2,1:T(4,128)(2,1)S(1)}, bf16[4,12,12,144]{3,0,2,1:T(4,128)(2,1)}, u32[]{:S(2)}) copy-start(bf16[4,12,12,144]{3,0,2,1:T(4,128)(2,1)} %param.10) | copy-start | bytes 497668
  2.6 17.9 %all-to-all-start = ((bf16[32,8,256]{2,1,0:T(8,128)(2,1)}), bf16[32,8,256]{2,1,0:T(8,128)(2,1)S(1)}, u32[]{:S(2)}, u32[]{:S(2)}) async-start(bf16[32,8,256]{2,1,0:T(8,128)(2,1)} %bitcast.9), calls=%async_computation | async-start | bytes 262144 | tf_op jit(solution)/shard_map/all_to_all | solution.py:594
  11.9 8.6 %copy-start = (f32[12,12,216]{2,1,0:T(8,128)S(1)}, f32[12,12,216]{2,1,0:T(8,128)}, u32[]{:S(2)}) copy-start(f32[12,12,216]{2,1,0:T(8,128)} %adjoint_ref.1) | copy-start | bytes 373252
  11.9 8.6 %copy-start.1 = (f32[64,216]{1,0:T(8,128)S(1)}, f32[64,216]{1,0:T(8,128)}, u32[]{:S(2)}) copy-start(f32[64,216]{1,0:T(8,128)} %table_ref.1) | copy-start | bytes 165892
  12.1 7.1 %collective-permute-start = (bf16[16,128]{1,0:T(8,128)(2,1)S(1)}, bf16[16,128]{1,0:T(8,128)(2,1)S(1)}, u32[]{:S(2)}, u32[]{:S(2)}) collective-permute-start(bf16[16,128]{1,0:T(8,128)(2,1)S(1)} %get-tuple-element.13), channel_id=1, source_target_pairs={{0,992},{32,64},{64,32},{96,128},{128,96},{160,192},{192,160},{224... | collective-permute-start | bytes 12296 | tf_op jit(solution)/shard_map/ppermute | solution.py:601
  16.4 3.1 %collective-permute-start.1 = (bf16[16,128]{1,0:T(8,128)(2,1)S(1)}, bf16[16,128]{1,0:T(8,128)(2,1)S(1)}, u32[]{:S(2)}, u32[]{:S(2)}) collective-permute-start(bf16[16,128]{1,0:T(8,128)(2,1)S(1)} %get-tuple-element.14), channel_id=1, source_target_pairs={{0,32},{32,0},{64,96},{96,64},{128,160},{160,128},{192,224},{224,1... | collective-permute-start | bytes 12296 | tf_op jit(solution)/shard_map/ppermute | solution.py:602
  20.5 21.5 %copy-start.2 = (bf16[384,12]{0,1:T(8,128)(2,1)S(1)}, bf16[384,12]{0,1:T(8,128)(2,1)}, u32[]{:S(2)}) copy-start(bf16[384,12]{0,1:T(8,128)(2,1)} %param.17) | copy-start | bytes 27652
  21.0 21.9 %collective-permute-start.2 = (bf16[11,16,128]{2,1,0:T(8,128)(2,1)S(1)}, bf16[11,16,128]{2,1,0:T(8,128)(2,1)S(1)}, u32[]{:S(2)}, u32[]{:S(2)}) collective-permute-start(bf16[11,16,128]{2,1,0:T(8,128)(2,1)S(1)} %get-tuple-element.16), channel_id=1, source_target_pairs={{0,1},{1,2},{2,3},{3,4},{4,5},{5,6},{6,7},{7,8},{8,9},{9,10},{10,1... | collective-permute-start | bytes 135176 | tf_op jit(solution)/shard_map/ppermute | solution.py:613
  26.2 17.5 %collective-permute-start.3 = (bf16[11,16,128]{2,1,0:T(8,128)(2,1)S(1)}, bf16[11,16,128]{2,1,0:T(8,128)(2,1)S(1)}, u32[]{:S(2)}, u32[]{:S(2)}) collective-permute-start(bf16[11,16,128]{2,1,0:T(8,128)(2,1)S(1)} %get-tuple-element.17), channel_id=1, source_target_pairs={{1,0},{2,1},{3,2},{4,3},{5,4},{6,5},{7,6},{8,7},{9,8},{10,9},{11,1... | collective-permute-start | bytes 135176 | tf_op jit(solution)/shard_map/ppermute | solution.py:614
  45.2 16.3 %all-to-all-start.1 = ((bf16[32,16,128]{2,1,0:T(8,128)(2,1)}), bf16[32,16,128]{2,1,0:T(8,128)(2,1)S(1)}, u32[]{:S(2)}, u32[]{:S(2)}) async-start(bf16[32,16,128]{2,1,0:T(8,128)(2,1)} %bitcast.4), calls=%async_computation.1 | async-start | bytes 262144 | tf_op jit(solution)/shard_map/all_to_all | solution.py:630
  51.4 8.0 %collective-permute-start.4 = (bf16[10,16,256]{2,1,0:T(8,128)(2,1)S(1)}, bf16[10,16,256]{2,1,0:T(8,128)(2,1)S(1)}, u32[]{:S(2)}, u32[]{:S(2)}) collective-permute-start(bf16[10,16,256]{2,1,0:T(8,128)(2,1)S(1)} %get-tuple-element.20), channel_id=1, source_target_pairs={{0,992},{32,64},{64,32},{96,128},{128,96},{160,192},{192,160},{224... | collective-permute-start | bytes 245768 | tf_op jit(solution)/shard_map/ppermute | solution.py:638
  55.7 3.7 %collective-permute-start.5 = (bf16[10,16,256]{2,1,0:T(8,128)(2,1)S(1)}, bf16[10,16,256]{2,1,0:T(8,128)(2,1)S(1)}, u32[]{:S(2)}, u32[]{:S(2)}) collective-permute-start(bf16[10,16,256]{2,1,0:T(8,128)(2,1)S(1)} %get-tuple-element.21), channel_id=1, source_target_pairs={{0,32},{32,0},{64,96},{96,64},{128,160},{160,128},{192,224},{224,1... | collective-permute-start | bytes 245768 | tf_op jit(solution)/shard_map/ppermute | solution.py:639
